TPU v7x, 256 devices: a whole 4x4x8 slice. The times are simulated.
256 devices in a mesh: blk: 64 (over z, x, core), grp: 4 (over y).
Axes of the slice: x: 4, y: 4, z: 8, core: 2. Of those that a mesh axis runs over, the one named last changes fastest.
Arguments:
- flow: float32 [3072, 5, 4096], P(('blk', 'grp')), may hold values from -3 to 6, as said below
- adjoint: float32 [3072, 5, 4096], P(('blk', 'grp')), may hold values from -6 to 6
- cut_flag: int32 [3072, 4096], P(('blk', 'grp')), may hold values 0 or 1
- lateral_owner: int32 [3072, 4, 1], P(('blk', 'grp')), may hold values from 0 to 63; in each aligned block of 48 rows (0 to 47, 48 to 95, ..., all dimensions but the last counted through in order) at most 2 rows name the same one
- lateral_link: int32 [3072, 4], P(('blk', 'grp')), may hold values from 0 to 59
- vertical_link: int32 [3072, 2], P(('blk', 'grp')), may hold values from 0 to 59
Outputs:
- indicator: float32 [3072, 4096], P(('blk', 'grp'))
Inputs may be any that keep to these rules, and one draw needn't show every extreme that they name: `flow`: density lies between 1 and 2, pressure between 1 and 2, every velocity component between -1.25 and 1.25. `lateral_owner`: among the faces 0 to 3 of the blocks of one device, at most 2 have their neighbour on any one blk index, and in every draw some device reaches 2.
All inputs are finite; a program needn't handle non-finite values. No bound on the sum of `cut_flag` on one device may be relied on, other than what follows from the above.
Results may differ from a plain program's by a relative error of at most 0.0003.
Values sent between devices are 32-bit elements; how exact they have to be, the bound alone decides.
No kernel may reach another device: no remote copies, remote signals or barrier semaphores. Data moves between devices by JAX's collectives and lax.ppermute only.
A program may use at most 128 MiB of HBM per device.

v0:
```python
import jax
import jax.numpy as jnp
from jax import lax
from jax.sharding import PartitionSpec as P

EDGE = 16


HEAT_RATIO = 1.4
ENTROPY_FIX = 0.2
FREESTREAM = (1.0, 0.0, 0.0, 0.3, 1.0)


def extended(cells, sides, width):
    for axis, dim in sides:
        count = lax.axis_size(axis)
        ends = count - 1
        head = lax.slice_in_dim(cells, 0, width, axis=dim)
        tail = lax.slice_in_dim(cells, cells.shape[dim] - width, cells.shape[dim], axis=dim)
        cells = jnp.concatenate(
            [
                lax.ppermute(tail, axis, [(i, (i + 1) % count) for i in range(ends)]),
                cells,
                lax.ppermute(head, axis, [((i + 1) % count, i) for i in range(ends)]),
            ],
            axis=dim,
        )
    return cells


def primitive(conserved):
    density = conserved[:, 0]
    velocity = conserved[:, 1:4] / density[:, None]
    pressure = (HEAT_RATIO - 1.0) * (
        conserved[:, 4] - 0.5 * density * jnp.sum(velocity * velocity, axis=1)
    )
    return jnp.concatenate([density[:, None], velocity, pressure[:, None]], axis=1)


def minmod(first_diff, second_diff):
    return jnp.where(
        first_diff * second_diff > 0.0,
        jnp.sign(first_diff) * jnp.minimum(jnp.abs(first_diff), jnp.abs(second_diff)),
        0.0,
    )


def harten(wave_rate, spread):
    return jnp.where(
        wave_rate < spread, (wave_rate * wave_rate + spread * spread) / (2.0 * spread), wave_rate
    )


def roe_flux(left_state, right_state, normal_axis):
    left_rho = left_state[0]
    right_rho = right_state[0]
    left_vel = left_state[1:4]
    right_vel = right_state[1:4]
    left_press = left_state[4]
    right_press = right_state[4]
    factor = HEAT_RATIO / (HEAT_RATIO - 1.0)
    left_enth = factor * left_press / left_rho + 0.5 * jnp.sum(left_vel * left_vel, axis=0)
    right_enth = factor * right_press / right_rho + 0.5 * jnp.sum(right_vel * right_vel, axis=0)
    left_root = jnp.sqrt(left_rho)
    right_root = jnp.sqrt(right_rho)
    weight_sum = left_root + right_root
    mean_vel = (left_root * left_vel + right_root * right_vel) / weight_sum
    mean_enth = (left_root * left_enth + right_root * right_enth) / weight_sum
    speed_sq = jnp.sum(mean_vel * mean_vel, axis=0)
    sound_sq = (HEAT_RATIO - 1.0) * (mean_enth - 0.5 * speed_sq)
    sound_speed = jnp.sqrt(sound_sq)
    mean_rho = left_root * right_root
    normal = mean_vel[normal_axis]
    jump_vel = right_vel - left_vel
    jump_rho = right_rho - left_rho
    jump_press = right_press - left_press
    jump_normal = jump_vel[normal_axis]
    wave_slow = (jump_press - mean_rho * sound_speed * jump_normal) / (2.0 * sound_sq)
    wave_fast = (jump_press + mean_rho * sound_speed * jump_normal) / (2.0 * sound_sq)
    wave_entropy = jump_rho - jump_press / sound_sq
    spread = ENTROPY_FIX * sound_speed
    slow_part = harten(jnp.abs(normal - sound_speed), spread) * wave_slow
    fast_part = harten(jnp.abs(normal + sound_speed), spread) * wave_fast
    mid_part = jnp.abs(normal) * wave_entropy
    shear_part = jnp.abs(normal) * mean_rho
    unit_vector = [1.0 if axis_no == normal_axis else 0.0 for axis_no in range(3)]
    shear_jump = [jump_vel[axis_no] - jump_normal * unit_vector[axis_no] for axis_no in range(3)]
    diss_mass = slow_part + fast_part + mid_part
    diss_mom = [
        slow_part * (mean_vel[axis_no] - sound_speed * unit_vector[axis_no])
        + fast_part * (mean_vel[axis_no] + sound_speed * unit_vector[axis_no])
        + mid_part * mean_vel[axis_no]
        + shear_part * shear_jump[axis_no]
        for axis_no in range(3)
    ]
    diss_energy = (
        slow_part * (mean_enth - normal * sound_speed)
        + fast_part * (mean_enth + normal * sound_speed)
        + mid_part * 0.5 * speed_sq
        + shear_part
        * (mean_vel[0] * shear_jump[0] + mean_vel[1] * shear_jump[1] + mean_vel[2] * shear_jump[2])
    )
    left_normal = left_vel[normal_axis]
    right_normal = right_vel[normal_axis]
    mass_flux = 0.5 * (left_rho * left_normal + right_rho * right_normal) - 0.5 * diss_mass
    momentum = [
        0.5
        * (
            left_rho * left_normal * left_vel[axis_no]
            + right_rho * right_normal * right_vel[axis_no]
            + (left_press + right_press) * unit_vector[axis_no]
        )
        - 0.5 * diss_mom[axis_no]
        for axis_no in range(3)
    ]
    energy = (
        0.5 * (left_rho * left_normal * left_enth + right_rho * right_normal * right_enth)
        - 0.5 * diss_energy
    )
    return jnp.stack([mass_flux] + momentum + [energy], axis=0)


def wall_flux(pressure, normal_axis):
    nothing = jnp.zeros_like(pressure)
    parts = [pressure if axis_no == normal_axis else nothing for axis_no in range(3)]
    return jnp.stack([nothing] + parts + [nothing], axis=0)


def face_flux(left_state, right_state, left_solid, right_solid, normal_axis):
    roe_value = roe_flux(left_state, right_state, normal_axis)
    from_left = (right_solid > 0.5) & (left_solid < 0.5)
    from_right = (left_solid > 0.5) & (right_solid < 0.5)
    return jnp.where(
        from_left,
        wall_flux(left_state[4], normal_axis),
        jnp.where(from_right, wall_flux(right_state[4], normal_axis), roe_value),
    )


def faces_of(values, edge_cells):
    plane_size = edge_cells * edge_cells
    face_shape = values.shape[:2] + (plane_size,)
    return jnp.stack(
        [
            values[:, :, 0],
            values[:, :, edge_cells - 1],
            values[:, :, :, :edge_cells].reshape(face_shape),
            values[:, :, :, plane_size - edge_cells :].reshape(face_shape),
            values[:, :, :, 0::edge_cells].reshape(face_shape),
            values[:, :, :, edge_cells - 1 :: edge_cells].reshape(face_shape),
        ],
        axis=1,
    )


def select_face(face_slab, level_code):
    channels = face_slab.shape[0]
    half_edge = EDGE // 2
    square = face_slab.reshape(channels, EDGE, EDGE)
    quarter_code = jnp.minimum(level_code, 3)
    anchor = jnp.zeros((), jnp.int32)
    first_start = quarter_code // 2 * half_edge
    second_start = quarter_code % 2 * half_edge
    quarter = lax.dynamic_slice(
        square, (anchor, first_start, second_start), (channels, half_edge, half_edge)
    )
    widened = jnp.broadcast_to(quarter[:, :, None, :, None], (channels, half_edge, 2, half_edge, 2))
    return jnp.where(level_code == 4, face_slab, widened.reshape(channels, EDGE * EDGE))


def shifted(values, ghosts, edge_cells):
    channels = values.shape[0]
    plane_size = edge_cells * edge_cells
    depth_index = lax.broadcasted_iota(jnp.int32, (1, 1, plane_size), 2) % edge_cells
    lower_x = jnp.concatenate([ghosts[0][:, None], values[:, :-1]], axis=1)
    upper_x = jnp.concatenate([values[:, 1:], ghosts[1][:, None]], axis=1)
    lower_y = jnp.concatenate(
        [
            ghosts[2].reshape(channels, edge_cells, edge_cells),
            values[:, :, : plane_size - edge_cells],
        ],
        axis=2,
    )
    upper_y = jnp.concatenate(
        [values[:, :, edge_cells:], ghosts[3].reshape(channels, edge_cells, edge_cells)], axis=2
    )
    low_rim = jnp.repeat(ghosts[4].reshape(channels, edge_cells, edge_cells), edge_cells, axis=2)
    high_rim = jnp.repeat(ghosts[5].reshape(channels, edge_cells, edge_cells), edge_cells, axis=2)
    lower_z = jnp.where(
        depth_index == 0, low_rim, jnp.concatenate([values[:, :, :1], values[:, :, :-1]], axis=2)
    )
    upper_z = jnp.where(
        depth_index == edge_cells - 1,
        high_rim,
        jnp.concatenate([values[:, :, 1:], values[:, :, -1:]], axis=2),
    )
    return ((lower_x, upper_x), (lower_y, upper_y), (lower_z, upper_z))


def plane_tables(edge_cells):
    plane_size = edge_cells * edge_cells
    fine_edge = 2 * edge_cells
    coarse_index = lax.broadcasted_iota(jnp.int32, (plane_size, 4 * plane_size), 0)
    fine_index = lax.broadcasted_iota(jnp.int32, (plane_size, 4 * plane_size), 1)
    fine_row = fine_index // fine_edge
    fine_col = fine_index % fine_edge
    parent = fine_row // 2 * edge_cells + fine_col // 2 == coarse_index
    ones_table = jnp.where(parent, 1.0, 0.0).astype(jnp.float32)
    row_table = jnp.where(parent, jnp.where(fine_row % 2 == 0, -0.25, 0.25), 0.0).astype(
        jnp.float32
    )
    col_table = jnp.where(parent, jnp.where(fine_col % 2 == 0, -0.25, 0.25), 0.0).astype(
        jnp.float32
    )
    return (ones_table, jnp.concatenate([ones_table, row_table, col_table], axis=0))


def prolong(values, ghosts, edge_cells, expand_table):
    channels = values.shape[0]
    plane_size = edge_cells * edge_cells
    slopes = [
        minmod(upper_side - values, values - lower_side)
        for lower_side, upper_side in shifted(values, ghosts, edge_cells)
    ]
    layer_sign = jnp.where(
        lax.broadcasted_iota(jnp.int32, (1, 2 * edge_cells, 1), 1) % 2 == 0, -0.25, 0.25
    )
    first_term = jnp.repeat(values, 2, axis=1) + jnp.repeat(slopes[0], 2, axis=1) * layer_sign
    stacked = jnp.concatenate(
        [first_term, jnp.repeat(slopes[1], 2, axis=1), jnp.repeat(slopes[2], 2, axis=1)], axis=2
    )
    fine_field = jnp.dot(
        stacked.reshape(channels * 2 * edge_cells, 3 * plane_size),
        expand_table,
        precision=lax.Precision.HIGHEST,
        preferred_element_type=jnp.float32,
    )
    return fine_field.reshape(channels, 2 * edge_cells, 4 * plane_size)


def residual(fine_field, fine_ghosts, solid_mask, size_fine):
    channels = fine_field.shape[0]
    plane_size = size_fine * size_fine
    depth_index = lax.broadcasted_iota(jnp.int32, (1, plane_size), 1) % size_fine
    rim_x = jnp.zeros((1, plane_size), jnp.float32)
    left_state = jnp.concatenate([fine_ghosts[0][:, None], fine_field], axis=1)
    right_state = jnp.concatenate([fine_field, fine_ghosts[1][:, None]], axis=1)
    flux_x = face_flux(
        left_state,
        right_state,
        jnp.concatenate([rim_x, solid_mask], axis=0),
        jnp.concatenate([solid_mask, rim_x], axis=0),
        0,
    )
    summed = flux_x[:, 1:] - flux_x[:, :-1]
    rim_y = jnp.zeros((size_fine, size_fine), jnp.float32)
    left_state = jnp.concatenate(
        [fine_ghosts[2].reshape(channels, size_fine, size_fine), fine_field], axis=2
    )
    right_state = jnp.concatenate(
        [fine_field, fine_ghosts[3].reshape(channels, size_fine, size_fine)], axis=2
    )
    flux_y = face_flux(
        left_state,
        right_state,
        jnp.concatenate([rim_y, solid_mask], axis=1),
        jnp.concatenate([solid_mask, rim_y], axis=1),
        1,
    )
    summed = summed + flux_y[:, :, size_fine:] - flux_y[:, :, :plane_size]
    low_rim = jnp.repeat(fine_ghosts[4].reshape(channels, size_fine, size_fine), size_fine, axis=2)
    lower_state = jnp.where(
        depth_index == 0,
        low_rim,
        jnp.concatenate([fine_field[:, :, :1], fine_field[:, :, :-1]], axis=2),
    )
    lower_solid = jnp.where(
        depth_index == 0, 0.0, jnp.concatenate([solid_mask[:, :1], solid_mask[:, :-1]], axis=1)
    )
    flux_low = face_flux(lower_state, fine_field, lower_solid, solid_mask, 2)
    top_state = fine_field[:, :, size_fine - 1 :: size_fine]
    flux_top = face_flux(
        top_state,
        fine_ghosts[5].reshape(channels, size_fine, size_fine),
        solid_mask[:, size_fine - 1 :: size_fine],
        rim_y,
        2,
    )
    flux_high = jnp.where(
        depth_index == size_fine - 1,
        jnp.repeat(flux_top, size_fine, axis=2),
        jnp.concatenate([flux_low[:, :, 1:], flux_low[:, :, -1:]], axis=2),
    )
    summed = summed + flux_high - flux_low
    return jnp.where(solid_mask > 0.5, 0.0, summed)


def make_indicator(ones_table, expand_table):

    def block_indicator(operands):
        flow_prim, adjoint_block, ghosts, flags = operands
        plane_size = EDGE * EDGE
        fine_flow = prolong(
            flow_prim.reshape(5, EDGE, plane_size), ghosts[:, :5], EDGE, expand_table
        )
        fine_adjoint = prolong(
            adjoint_block.reshape(5, EDGE, plane_size), ghosts[:, 5:], EDGE, expand_table
        )
        wide_ghosts = jnp.dot(
            ghosts[:, :5].reshape(30, plane_size),
            ones_table,
            precision=lax.Precision.HIGHEST,
            preferred_element_type=jnp.float32,
        ).reshape(6, 5, 4 * plane_size)
        flag_rows = jnp.repeat(flags.astype(jnp.float32).reshape(EDGE, plane_size), 2, axis=0)
        solid_mask = jnp.dot(
            flag_rows,
            ones_table,
            precision=lax.Precision.HIGHEST,
            preferred_element_type=jnp.float32,
        )
        fine_residual = residual(fine_flow, wide_ghosts, solid_mask, 2 * EDGE)
        weighted = jnp.sum(fine_adjoint * fine_residual, axis=0)
        paired = weighted[0::2] + weighted[1::2]
        coarse = jnp.dot(
            paired,
            ones_table.T,
            precision=lax.Precision.HIGHEST,
            preferred_element_type=jnp.float32,
        )
        return jnp.abs(coarse).reshape(EDGE * EDGE * EDGE)

    return block_indicator


def local(flow, adjoint, cut_flag, lateral_owner, lateral_link, vertical_link):
    blocks = flow.shape[0]
    plane_size = EDGE * EDGE
    peer_count = lax.axis_size("blk")
    capacity = max(2, 6 * blocks // peer_count)
    primitives = primitive(flow)
    coarse_both = jnp.concatenate([primitives, adjoint], axis=1).reshape(
        blocks, 10, EDGE, plane_size
    )
    face_all = faces_of(coarse_both, EDGE)
    owners = lateral_owner[:, :, 0].reshape(-1)
    lateral_codes = lateral_link.reshape(-1)
    far_sides = jnp.tile(jnp.array([1, 0, 3, 2], jnp.int32), blocks)
    requested = (lateral_codes // 5 * 4 + far_sides) * 5 + lateral_codes % 5
    matches = (owners[:, None] == jnp.arange(peer_count, dtype=jnp.int32)[None, :]).astype(
        jnp.int32
    )
    before = jnp.cumsum(matches, axis=0) - matches
    slot_pos = jnp.sum(before * matches, axis=1)
    requests = jnp.full((peer_count, capacity), -1, jnp.int32).at[owners, slot_pos].set(requested)
    wanted = lax.all_to_all(requests, "blk", split_axis=0, concat_axis=0, tiled=True)
    wanted_flat = wanted.reshape(-1)
    is_valid = wanted_flat >= 0
    safe_code = jnp.maximum(wanted_flat, 0)
    face_slabs = face_all[safe_code // 20, safe_code // 5 % 4]
    chosen = jax.vmap(select_face)(face_slabs, safe_code % 5)
    chosen = jnp.where(is_valid[:, None, None], chosen, 0.0)
    replies = chosen.reshape(wanted.shape + (10, plane_size))
    flow_back = lax.all_to_all(replies[:, :, :5], "blk", split_axis=0, concat_axis=0, tiled=True)
    adjoint_back = lax.all_to_all(replies[:, :, 5:], "blk", split_axis=0, concat_axis=0, tiled=True)
    returned = jnp.concatenate([flow_back, adjoint_back], axis=2)
    lateral = returned[owners, slot_pos].reshape(blocks, 4, 10, plane_size)
    stacked = jnp.stack([face_all[:, 4], face_all[:, 5]], axis=0)
    around_flow = extended(stacked[:, :, :5], (("grp", 0),), 1)
    around_adjoint = extended(stacked[:, :, 5:], (("grp", 0),), 1)
    beside_all = jnp.concatenate([around_flow, around_adjoint], axis=2)
    region = lax.axis_index("grp")
    last_region = lax.axis_size("grp") - 1
    lower_ghost = jax.vmap(select_face)(
        beside_all[0][vertical_link[:, 0] // 5], vertical_link[:, 0] % 5
    )
    upper_ghost = jax.vmap(select_face)(
        beside_all[3][vertical_link[:, 1] // 5], vertical_link[:, 1] % 5
    )
    state = jnp.array(FREESTREAM, jnp.float32)
    farfield_layer = jnp.concatenate(
        [
            jnp.broadcast_to(state[:, None], (5, plane_size)),
            jnp.zeros((5, plane_size), jnp.float32),
        ],
        axis=0,
    )
    lower_ghost = jnp.where(region == 0, farfield_layer, lower_ghost)
    upper_ghost = jnp.where(region == last_region, farfield_layer, upper_ghost)
    ghosts = jnp.concatenate([lateral, lower_ghost[:, None], upper_ghost[:, None]], axis=1)
    ones_table, expand_table = plane_tables(EDGE)
    return lax.map(
        make_indicator(ones_table, expand_table), (primitives, adjoint, ghosts, cut_flag)
    )


def solution(mesh):
    in_specs = (
        P(("blk", "grp"), None, None),
        P(("blk", "grp"), None, None),
        P(("blk", "grp"), None),
        P(("blk", "grp"), None, None),
        P(("blk", "grp"), None),
        P(("blk", "grp"), None),
    )
    out_specs = P(("blk", "grp"), None)
    return jax.shard_map(local, mesh=mesh, in_specs=in_specs, out_specs=out_specs, check_vma=False)
```

profile of v0, /device:TPU:1, one launch (start us, length us, event | category | flops | bytes accessed | tf_op | source)
XLA Modules:
  0.0 935.7 jit_solution(12260241586542603378)
XLA Ops:
  10.4 8.0 slice.1048
  26.2 8.2 slice.1049
  39.8 5.9 collective-permute-start.2
  65.4 14.0 %all-to-all-start = ((s32[64,1,2]{2,1,0:T(1,128)}), s32[64,1,2]{2,1,0:T(1,128)}, u32[]{:S(2)}, u32[]{:S(2)}) async-start(s32[64,1,2]{2,1,0:T(1,128)} %copy.142), calls=%async_computation | async-start | bytes 65536 | tf_op jit(solution)/shard_map/all_to_all | solution.py:356
  100.3 14.0 %copy.201 = f32[128,10,256]{1,0,2:T(8,128)} copy(f32[128,10,256]{2,1,0:T(8,128)S(1)} %gather_fusion) | data formatting | bytes 2621440 | tf_op jit(solution)/shard_map/vmap()/reshape | solution.py:159
  114.2 9.3 copy.167
  123.6 9.9 %gather_fusion.4 = f32[128,10,8,8]{1,0,3,2:T(8,128)} fusion(f32[128,10,16,16]{1,0,3,2:T(8,128)} %bitcast.548, s32[128]{0:T(128)S(1)} %get-tuple-element.482), kind=kCustom, calls=%fused_computation.4 | custom fusion | bytes 657408 | tf_op jit(solution)/shard_map/vmap()/gather | solution.py:164
  133.5 6.6 copy.166
  140.6 7.7 broadcast_in_dim.387
  148.2 11.9 %select_select_fusion.2 = f32[64,2,10,256]{2,3,1,0:T(8,128)S(1)} fusion(f32[64,2,10,256]{2,3,1,0:T(8,128)} %copy.167, f32[64,2,10,256]{2,3,1,0:T(8,128)} %bitcast.559, pred[64,2]{1,0:T(8,128)(4,1)S(1)} %copy.146, pred[64,2]{1,0:T(8,128)(4,1)S(1)} %copy.144), kind=kLoop, calls=%fused_computation.454 | loop fusion | flops 655360 | bytes 3932416 | tf_op jit(solution)/shard_map/jit(_where)/select_n | solution.py:362
  160.2 12.4 %fusion.308 = (f32[64,2,5,256]{2,3,1,0:T(8,128)}, f32[64,2,5,256]{2,3,1,0:T(8,128)}) fusion(f32[64,2,10,256]{2,3,1,0:T(8,128)S(1)} %select_select_fusion.2), kind=kLoop, calls=%fused_computation.650 | loop fusion | bytes 2621440 | tf_op jit(solution)/shard_map/slice | solution.py:364
  172.6 10.4 %copy.169 = f32[64,2,5,256]{3,1,2,0:T(2,128)} copy(f32[64,2,5,256]{2,3,1,0:T(8,128)} %get-tuple-element.455) | data formatting | bytes 1310720 | tf_op jit(solution)/shard_map/slice | solution.py:365
  183.0 10.6 %all-to-all-start.2 = ((f32[64,2,5,256]{3,1,2,0:T(2,128)}), f32[64,2,5,256]{3,1,2,0:T(2,128)S(1)}, u32[]{:S(2)}, u32[]{:S(2)}) async-start(f32[64,2,5,256]{3,1,2,0:T(2,128)} %copy.169), calls=%async_computation.2 | async-start | bytes 1310720 | tf_op jit(solution)/shard_map/all_to_all | solution.py:365
  196.3 10.5 %copy.168 = f32[64,2,5,256]{3,1,2,0:T(2,128)} copy(f32[64,2,5,256]{2,3,1,0:T(8,128)} %get-tuple-element.454) | data formatting | bytes 1310720 | tf_op jit(solution)/shard_map/slice | solution.py:364
  206.8 7.1 all-to-all-done.2
  213.9 5.9 all-to-all-start.1
  244.4 690.9 %while.15 = (s32[]{:T(128)}, f32[12,4096]{1,0:T(8,128)}, f32[12,5,4096]{2,0,1:T(8,128)}, f32[12,6,10,256]{3,1,0,2:T(8,128)S(1)}, f32[768,1024]{1,0:T(8,128)}, /*...) while((s32[]{:T(128)}, f32[12,4096]{1,0:T(8,128)}, ...), condition=%wide.region_18.19_spmd.clone.clone, body=%wide.region_4.18_spmd.clone.clone.sunk | while | flops 3323658496 | bytes 116343488 | solution.py:392
  293.9 4.8 fusion.401
  351.4 4.8 fusion.401
  466.5 4.8 fusion.401
  524.1 4.8 fusion.401
  696.8 4.8 fusion.401
  754.3 4.8 fusion.401
  927.0 4.8 fusion.401
  (2541 shorter events, 736.9 us)
Async XLA Ops:
  23.6 197.9 %collective-permute-start.3 = (f32[1,12,5,256]{3,2,1,0:T(8,128)}, f32[1,12,5,256]{3,2,1,0:T(8,128)}, u32[]{:S(2)}, u32[]{:S(2)}) collective-permute-start(f32[1,12,5,256]{3,2,1,0:T(8,128)} %get-tuple-element.468), channel_id=1, source_target_pairs={{1,0},{2,1},{3,2},{5,4},{6,5},{7,6},{9,8},{10,9},{11,10},{13,12},{... | collective-permute-start | bytes 184328 | tf_op jit(solution)/shard_map/ppermute | solution.py:24
  24.9 196.6 %collective-permute-start.1 = (f32[1,12,5,256]{3,2,1,0:T(8,128)}, f32[1,12,5,256]{3,2,1,0:T(8,128)}, u32[]{:S(2)}, u32[]{:S(2)}) collective-permute-start(f32[1,12,5,256]{3,2,1,0:T(8,128)} %get-tuple-element.467), channel_id=1, source_target_pairs={{1,0},{2,1},{3,2},{5,4},{6,5},{7,6},{9,8},{10,9},{11,10},{13,12},{... | collective-permute-start | bytes 184328 | tf_op jit(solution)/shard_map/ppermute | solution.py:24
  34.4 14.7 %copy-start.54 = (s32[12,4,1]{0,2,1:T(1,128)S(1)}, s32[12,4,1]{0,2,1:T(1,128)}, u32[]{:S(2)}) copy-start(s32[12,4,1]{0,2,1:T(1,128)} %param.13) | copy-start | bytes 580
  34.4 16.0 %copy-start.45 = (s32[12,4]{0,1:T(4,128)S(1)}, s32[12,4]{0,1:T(4,128)}, u32[]{:S(2)}) copy-start(s32[12,4]{0,1:T(4,128)} %param.14) | copy-start | bytes 580
  39.0 43.5 %copy-start.13 = (f32[1,12,10,256]{3,2,1,0:T(8,128)}, f32[1,12,10,256]{3,2,1,0:T(8,128)S(1)}, u32[]{:S(2)}) copy-start(f32[1,12,10,256]{3,2,1,0:T(8,128)S(1)} %reshape.1184) | copy-start | bytes 368644
  39.8 181.8 %collective-permute-start.2 = (f32[1,12,5,256]{3,2,1,0:T(8,128)}, f32[1,12,5,256]{3,2,1,0:T(8,128)}, u32[]{:S(2)}, u32[]{:S(2)}) collective-permute-start(f32[1,12,5,256]{3,2,1,0:T(8,128)} %get-tuple-element.466), channel_id=1, source_target_pairs={{0,1},{1,2},{2,3},{4,5},{5,6},{6,7},{8,9},{9,10},{10,11},{12,13},{... | collective-permute-start | bytes 184328 | tf_op jit(solution)/shard_map/ppermute | solution.py:22
  45.7 175.8 %collective-permute-start = (f32[1,12,5,256]{3,2,1,0:T(8,128)}, f32[1,12,5,256]{3,2,1,0:T(8,128)}, u32[]{:S(2)}, u32[]{:S(2)}) collective-permute-start(f32[1,12,5,256]{3,2,1,0:T(8,128)} %get-tuple-element.465), channel_id=1, source_target_pairs={{0,1},{1,2},{2,3},{4,5},{5,6},{6,7},{8,9},{9,10},{10,11},{12,13},{... | collective-permute-start | bytes 184328 | tf_op jit(solution)/shard_map/ppermute | solution.py:22
  65.4 30.2 %all-to-all-start = ((s32[64,1,2]{2,1,0:T(1,128)}), s32[64,1,2]{2,1,0:T(1,128)}, u32[]{:S(2)}, u32[]{:S(2)}) async-start(s32[64,1,2]{2,1,0:T(1,128)} %copy.142), calls=%async_computation | async-start | bytes 65536 | tf_op jit(solution)/shard_map/all_to_all | solution.py:356
  87.0 106.6 %copy-start.37 = (s32[1024]{0:T(1024)}, s32[1024]{0:T(1024)S(1)}, u32[]{:S(2)}) copy-start(s32[1024]{0:T(1024)S(1)} %get-tuple-element.848) | copy-start | bytes 12292
  87.0 106.6 %copy-start.40 = (s32[1024]{0:T(1024)}, s32[1024]{0:T(1024)S(1)}, u32[]{:S(2)}) copy-start(s32[1024]{0:T(1024)S(1)} %get-tuple-element.845) | copy-start | bytes 12292
  95.7 98.0 %copy-start.46 = (pred[1024]{0:T(1024)(128)(4,1)}, pred[1024]{0:T(1024)(128)(4,1)S(1)}, u32[]{:S(2)}) copy-start(pred[1024]{0:T(1024)(128)(4,1)S(1)} %get-tuple-element.849) | copy-start | bytes 3076
  172.6 21.1 %copy-start.50 = (pred[1024]{0:T(1024)(128)(4,1)S(1)}, pred[1024]{0:T(1024)(128)(4,1)}, u32[]{:S(2)}) copy-start(pred[1024]{0:T(1024)(128)(4,1)} %get-tuple-element.846) | copy-start | bytes 3076
  183.0 30.8 %all-to-all-start.2 = ((f32[64,2,5,256]{3,1,2,0:T(2,128)}), f32[64,2,5,256]{3,1,2,0:T(2,128)S(1)}, u32[]{:S(2)}, u32[]{:S(2)}) async-start(f32[64,2,5,256]{3,1,2,0:T(2,128)} %copy.169), calls=%async_computation.2 | async-start | bytes 1310720 | tf_op jit(solution)/shard_map/all_to_all | solution.py:365
  196.3 23.5 %copy-start.14 = (f32[1,12,10,256]{3,2,1,0:T(8,128)S(1)}, f32[1,12,10,256]{3,2,1,0:T(8,128)}, u32[]{:S(2)}) copy-start(f32[1,12,10,256]{3,2,1,0:T(8,128)} %copy-done.13) | copy-start | bytes 368644
  206.8 13.0 %copy-start.3 = (f32[12,3,4096]{2,1,0:T(4,128)S(1)}, f32[12,3,4096]{2,1,0:T(4,128)}, u32[]{:S(2)}) copy-start(f32[12,3,4096]{2,1,0:T(4,128)} %copy-done.2) | copy-start | bytes 1769476
  206.8 13.0 %copy-start.24 = (f32[12,1,4096]{2,1,0:T(1,128)S(1)}, f32[12,1,4096]{2,1,0:T(1,128)}, u32[]{:S(2)}) copy-start(f32[12,1,4096]{2,1,0:T(1,128)} %get-tuple-element.378) | copy-start | bytes 589828
  206.8 13.1 %copy-start.25 = (f32[12,1,4096]{2,1,0:T(1,128)S(1)}, f32[12,1,4096]{2,1,0:T(1,128)}, u32[]{:S(2)}) copy-start(f32[12,1,4096]{2,1,0:T(1,128)} %get-tuple-element.379) | copy-start | bytes 589828
  213.9 28.3 %all-to-all-start.1 = ((f32[64,2,5,256]{3,1,2,0:T(2,128)}), f32[64,2,5,256]{3,1,2,0:T(2,128)S(1)}, u32[]{:S(2)}, u32[]{:S(2)}) async-start(f32[64,2,5,256]{3,1,2,0:T(2,128)} %copy.168), calls=%async_computation.1 | async-start | bytes 1310720 | tf_op jit(solution)/shard_map/all_to_all | solution.py:364
  264.7 12.4 %copy-start.1 = (f32[5,32,1024]{2,1,0:T(8,128)}, f32[5,32,1024]{2,1,0:T(8,128)S(1)}, u32[]{:S(2)}) copy-start(f32[5,32,1024]{2,1,0:T(8,128)S(1)} %fusion.383) | copy-start | bytes 1966084 | tf_op jit(solution)/shard_map/while
  437.3 12.4 %copy-start.1 = (f32[5,32,1024]{2,1,0:T(8,128)}, f32[5,32,1024]{2,1,0:T(8,128)S(1)}, u32[]{:S(2)}) copy-start(f32[5,32,1024]{2,1,0:T(8,128)S(1)} %fusion.383) | copy-start | bytes 1966084 | tf_op jit(solution)/shard_map/while
  494.9 12.4 %copy-start.1 = (f32[5,32,1024]{2,1,0:T(8,128)}, f32[5,32,1024]{2,1,0:T(8,128)S(1)}, u32[]{:S(2)}) copy-start(f32[5,32,1024]{2,1,0:T(8,128)S(1)} %fusion.383) | copy-start | bytes 1966084 | tf_op jit(solution)/shard_map/while
  667.6 12.4 %copy-start.1 = (f32[5,32,1024]{2,1,0:T(8,128)}, f32[5,32,1024]{2,1,0:T(8,128)S(1)}, u32[]{:S(2)}) copy-start(f32[5,32,1024]{2,1,0:T(8,128)S(1)} %fusion.383) | copy-start | bytes 1966084 | tf_op jit(solution)/shard_map/while
  725.1 12.4 %copy-start.1 = (f32[5,32,1024]{2,1,0:T(8,128)}, f32[5,32,1024]{2,1,0:T(8,128)S(1)}, u32[]{:S(2)}) copy-start(f32[5,32,1024]{2,1,0:T(8,128)S(1)} %fusion.383) | copy-start | bytes 1966084 | tf_op jit(solution)/shard_map/while
  897.8 12.4 %copy-start.1 = (f32[5,32,1024]{2,1,0:T(8,128)}, f32[5,32,1024]{2,1,0:T(8,128)S(1)}, u32[]{:S(2)}) copy-start(f32[5,32,1024]{2,1,0:T(8,128)S(1)} %fusion.383) | copy-start | bytes 1966084 | tf_op jit(solution)/shard_map/while
  (326 other events, 1021.4 us)
where the time goes:
time: 949 us; the launch traced here: 936 us
  local copies, waits for them, and re-layouts  527 us (56%)
  other arithmetic  193 us (20%)
  matrix products  153 us (16%)
  starting transfers between devices  42.3 us (4%)
  loops' own time  11.8 us (1%)
    dot_general x24, matrix products, prolong(): jnp.dot(stacked.reshape(channels * 2 * edge_cells, 3 * plane_size), expan...  105 us
    while x180, other arithmetic  37.7 us
    select_n x24, other arithmetic, minmod(): jnp.where(first_diff * second_diff > 0.0, jnp.sign(first_diff) * jnp.mini...  27.2 us
    select_n x36, other arithmetic, face_flux(): jnp.where(from_left, wall_flux(left_state[4], normal_axis), jnp.where(fro...  26.7 us
    dynamic_slice x24, local copies, waits for them, and re-layouts, local(): lax.map(make_indicator(ones_table, expand_table), (primitives, adjoint, g...  26.7 us
    reshape x12, local copies, waits for them, and re-layouts, residual(): jnp.repeat(flux_top, size_fine, axis=2)  24.9 us
    gather x6, local copies, waits for them, and re-layouts, select_face(): lax.dynamic_slice(square, (anchor, first_start, second_start), (channels,...  24.1 us
    slice x2, local copies, waits for them, and re-layouts, local(): replies[:, :, :5]  22.9 us
  transfers between devices with their start and end apart: 7, of which 1 were waited for; matrix products, arithmetic and copies ran while one was open for 18% of the time, Pallas kernels for 0%

commit v1 on v0

v1 whole, which is shorter than its diff:
```python
import math

import jax
import jax.numpy as jnp
from jax import lax
from jax.experimental import pallas as pl
from jax.experimental.pallas import tpu as pltpu
from jax.sharding import PartitionSpec as P

EDGE = 16
NB = 12
PL = 2 * NB
ROWS = EDGE * PL
LANES = 128
PEERS = 64
FACES = 4 * PL
PXR = (EDGE + 2) * PL
MR = (EDGE + 1) * PL

VEL = math.sqrt(0.2)
PRESS = 0.2
WEIGHTS = (1.0 / VEL, 5.0, 5.0, 5.0, 2.5 / VEL)
FARFIELD = (1.0, 0.0, 0.0, 0.3 * VEL, PRESS)
KNEE = 0.4 / math.sqrt(5.0)
START = 1.2 / math.sqrt(5.0)
CURVE = 1.25 * math.sqrt(5.0)

VMEM_LIMIT = 56 * 2**20


def lane():
    return lax.broadcasted_iota(jnp.int32, (8, LANES), 1)


def even_row():
    return lax.broadcasted_iota(jnp.int32, (8, LANES), 0) % 2 == 0


def rolled(x, amount, axis=1):
    size = x.shape[axis]
    amount = amount % size
    return x if amount == 0 else pltpu.roll(x, amount, axis)


def rows8(start):
    if isinstance(start, int):
        return pl.ds(start, 8)
    return pl.ds(pl.multiple_of(start, 8), 8)


def compact_j(load, side):
    low = lane() // EDGE
    halves = []
    for ih in range(2):
        total = None
        for il in range(8):
            x = rolled(load(ih * 8 + il), 16 * il if side == 0 else 16 * il + 16)
            total = x if total is None else jnp.where(low == il, x, total)
        halves.append(total)
    if side == 0:
        return jnp.where(even_row(), halves[0], rolled(halves[1], 1, 0))
    return jnp.where(even_row(), rolled(halves[0], -1, 0), halves[1])


def compact_k(load, side):
    depth = lane() % EDGE
    total = None
    for i in range(EDGE):
        x = rolled(load(i), i if side == 0 else i - 15)
        total = x if total is None else jnp.where(depth == i, x, total)
    return total


def spread_j(low, high, i):
    ih, il = i // 8, i % 8
    a = low if ih == 0 else rolled(low, -1, 0)
    c = rolled(high, 1, 0) if ih == 0 else high
    return jnp.where(even_row(), rolled(a, -16 * il), rolled(c, 16 * (7 - il)))


def spread_k(low, high, i):
    return jnp.where(lane() % EDGE == 0, rolled(low, -i), rolled(high, 15 - i))


def column_of(packed, rows, width):
    at = lax.broadcasted_iota(jnp.int32, (rows, width), 0) // 2
    spot = lax.broadcasted_iota(jnp.int32, (rows, width), 1)
    return jnp.sum(jnp.where(at == spot, packed, 0.0), axis=1, keepdims=True)


def index_tables(own, vertical, index_ref):
    spots = lax.broadcasted_iota(jnp.int32, (PL, LANES), 1)
    half = lax.broadcasted_iota(jnp.int32, (PL, LANES), 0) % 2
    low, depth = spots // EDGE, spots % EDGE
    wide = (4 * half + low // 2) * EDGE + depth // 2

    def store(f, code, row_part, col_part, base, step):
        full = code == 4
        index_ref[pl.ds(f * PL, PL), :] = jnp.where(full, spots, wide + 8 * col_part)
        index_ref[pl.ds(144 + f * PL, PL), :] = base + step * jnp.where(full, half, row_part)

    at = lax.broadcasted_iota(jnp.int32, (PL, NB), 0) // 2
    spot = lax.broadcasted_iota(jnp.int32, (PL, NB), 1)
    entries = [own[f : f + 1, :].astype(jnp.int32) for f in range(4)]
    holders = [e >> 9 for e in entries]
    for f in range(4):
        value = column_of(own[f : f + 1, :], PL, NB).astype(jnp.int32)
        owner, code = value >> 9, value & 7
        rank = jnp.zeros((PL, 1), jnp.float32)
        for other in range(f + 1):
            same = holders[other] == owner
            if other == f:
                same = same & (spot < at)
            rank = rank + jnp.sum(jnp.where(same, 1.0, 0.0), axis=1, keepdims=True)
        rank = rank.astype(jnp.int32)
        store(f, code, code >> 1, code & 1, rank * 2 * PEERS + owner, PEERS)
    for side in range(2):
        value = column_of(vertical[side : side + 1, :], PL, NB).astype(jnp.int32)
        slot, code = value >> 3, value & 7
        store(4 + side, code, code & 1, code >> 1, slot * 2, 1)


def prep_kernel(
    flow_ref, adj_ref, flag_ref, own_ref, vertical_ref,
    prim_ref, adjl_ref, solid_ref, lat_ref, low_ref, high_ref, index_ref,
):
    def relaid(ref, c, out_ref):
        for t in range(2 * EDGE):
            i, jh = divmod(t, 2)
            part = ref[c, :, pl.ds(t * LANES, LANES)]
            out_ref[pl.ds(i * PL + jh + c * ROWS, NB, stride=2), :] = part.astype(jnp.float32)

    for c in range(5):
        relaid(flow_ref, c, prim_ref)
        relaid(adj_ref, c, adjl_ref)
    relaid(flag_ref, 0, solid_ref)
    index_tables(
        own_ref[...].astype(jnp.float32), vertical_ref[...].astype(jnp.float32), index_ref
    )

    def convert(n, _):
        at = [rows8(c * ROWS + n * 8) for c in range(5)]
        rho = prim_ref[at[0]]
        inv = 1.0 / rho
        vel = [prim_ref[at[c]] * inv for c in (1, 2, 3)]
        square = vel[0] * vel[0] + vel[1] * vel[1] + vel[2] * vel[2]
        prim_ref[at[4]] = (0.4 * PRESS) * (prim_ref[at[4]] - 0.5 * rho * square)
        for c in range(3):
            prim_ref[at[c + 1]] = vel[c] * VEL
        return 0

    lax.fori_loop(0, ROWS // 8, convert, 0)

    def layers(ref, first):
        def one(n, _):
            c, g = n // 3, n % 3

            def load(i):
                return ref[rows8(c * ROWS + i * PL + g * 8), :]

            out = (c + first) * FACES + g * 8
            lat_ref[rows8(out), :] = load(0)
            lat_ref[rows8(out + PL), :] = load(EDGE - 1)
            lat_ref[rows8(out + 2 * PL), :] = compact_j(load, 0)
            lat_ref[rows8(out + 3 * PL), :] = compact_j(load, 1)
            low_ref[rows8((c + first) * PL + g * 8), :] = compact_k(load, 0)
            high_ref[rows8((c + first) * PL + g * 8), :] = compact_k(load, 1)
            return 0

        lax.fori_loop(0, 15, one, 0)

    layers(prim_ref, 0)
    layers(adjl_ref, 5)


def reply_kernel(me_ref, asked_ref, lat_ref, first_ref, second_ref):
    before = lax.broadcasted_iota(jnp.int32, (NB, NB), 0) < lax.broadcasted_iota(
        jnp.int32, (NB, NB), 1
    )
    before = jnp.where(before, 1.0, 0.0)
    earlier = jnp.zeros((PEERS, 1), jnp.float32)
    entries = []
    for f in range(4):
        asked = asked_ref[:, f, :]
        match = (asked >> 9) == me_ref[0]
        hits = jnp.where(match, 1.0, 0.0)
        rank = jnp.dot(hits, before, preferred_element_type=jnp.float32) + earlier
        earlier = earlier + jnp.sum(hits, axis=1, keepdims=True)
        face = (asked >> 3) & 63
        target = (((face & 3) * PL) + ((face >> 2) * 2)).astype(jnp.float32) + 10.0
        entries.append((match, rank, target))
    column = lax.broadcasted_iota(jnp.int32, (PEERS, FACES), 1).astype(jnp.float32)
    picks = []
    for s in range(2):
        row = jnp.full((PEERS, 1), -10.0, jnp.float32)
        for match, rank, target in entries:
            mine = match & (rank > s - 0.5) & (rank < s + 0.5)
            row = row + jnp.sum(jnp.where(mine, target, 0.0), axis=1, keepdims=True)
        for h in range(2):
            picks.append(jnp.where(column == row + float(h), 1.0, 0.0))
    picks = jnp.concatenate(picks, axis=0)
    for c in range(10):
        out = jnp.dot(
            picks,
            lat_ref[pl.ds(c * FACES, FACES), :],
            precision=lax.Precision.HIGHEST,
            preferred_element_type=jnp.float32,
        )
        ref, at, stride = (first_ref, c * 4, 24) if c < 6 else (second_ref, (c - 6) * 4, 16)
        for q in range(4):
            ref[pl.ds(at + q, PEERS, stride=stride), :] = out[q * PEERS : (q + 1) * PEERS]


def one_hot(columns, width):
    parts = []
    for start in range(0, width, LANES):
        parts.append(
            jnp.where(
                columns == lax.broadcasted_iota(jnp.int32, columns.shape, 1) + start, 1.0, 0.0
            )
        )
    return parts[0] if len(parts) == 1 else jnp.concatenate(parts, axis=1)


def widened(x, index):
    parts = [
        jnp.take_along_axis(
            x[n : n + 8], index[n : n + 8], axis=1, mode="promise_in_bounds"
        )
        for n in range(0, x.shape[0], 8)
    ]
    return jnp.concatenate(parts, axis=0)


def ghost_planes(edge_ref, index_ref, received, around, far, g_ref):
    lateral = one_hot(index_ref[pl.ds(144, FACES), :], 4 * PEERS)
    vertical = [one_hot(index_ref[pl.ds(240 + s * PL, PL), :], LANES)[:, :PL] for s in range(2)]
    for c in range(5):
        x = jnp.concatenate([received(c, q) for q in range(4)], axis=0)
        y = jnp.dot(
            lateral, x, precision=lax.Precision.HIGHEST, preferred_element_type=jnp.float32
        )
        g_ref[pl.ds(c * 144, FACES), :] = widened(y, index_ref[pl.ds(0, FACES), :])
        for s in range(2):
            y = jnp.dot(
                vertical[s],
                around(s, c),
                precision=lax.Precision.HIGHEST,
                preferred_element_type=jnp.float32,
            )
            y = widened(y, index_ref[pl.ds(FACES + s * PL, PL), :])
            g_ref[pl.ds(c * 144 + FACES + s * PL, PL), :] = jnp.where(
                edge_ref[s] == 1, jnp.full_like(y, far[c]), y
            )


def spread_ghosts(g_ref, gj_ref, gk_ref):
    def one(n, _):
        c, g = n // 3, n % 3
        faces = [g_ref[rows8(c * 144 + f * PL + g * 8), :] for f in range(2, 6)]
        for i in range(EDGE):
            at = rows8(c * ROWS + i * PL + g * 8)
            gj_ref[at, :] = spread_j(faces[0], faces[1], i)
            gk_ref[at, :] = spread_k(faces[2], faces[3], i)
        return 0

    lax.fori_loop(0, 15, one, 0)


def minmod(a, c):
    return jnp.maximum(jnp.minimum(a, jnp.maximum(c, 0.0)), jnp.minimum(c, 0.0))


def masks():
    low, depth, even = lane() // EDGE, lane() % EDGE, even_row()
    return dict(
        k_last=depth == EDGE - 1,
        k_first=depth == 0,
        j_wrap=low == 7,
        j_back=low == 0,
        j_last=(low == 7) & ~even,
        j_first=(low == 0) & even,
    )


def next_k(x):
    return rolled(x, -1)


def last_k(x):
    return rolled(x, 1)


def next_j(x, m):
    r = rolled(x, -16)
    return jnp.where(m["j_wrap"], rolled(r, -1, 0), r)


def last_j(x, m):
    r = rolled(x, 16)
    return jnp.where(m["j_back"], rolled(r, 1, 0), r)


def slopes_of(below, x, above, gj, gk, m):
    x4 = 0.25 * x
    out = [minmod(0.25 * above - x4, x4 - 0.25 * below)]
    up = jnp.where(m["j_last"], gj, next_j(x, m))
    down = jnp.where(m["j_first"], gj, last_j(x, m))
    out.append(minmod(0.25 * up - x4, x4 - 0.25 * down))
    up = jnp.where(m["k_last"], gk, next_k(x))
    down = jnp.where(m["k_first"], gk, last_k(x))
    out.append(minmod(0.25 * up - x4, x4 - 0.25 * down))
    return out


def state(q):
    rho, u, v, w, p = q
    rs = lax.rsqrt(rho)
    enth = 7.0 * p * (rs * rs) + (u * u + v * v + w * w)
    return (rho, u, v, w, p, rho * rs, enth)


def four(base, first, second):
    out = []
    for a in (-1, 1):
        half = [x + s if a > 0 else x - s for x, s in zip(base, first)]
        for e in (-1, 1):
            out.append(state([x + s if e > 0 else x - s for x, s in zip(half, second)]))
    return out


def roe(left, right, axis):
    n = 1 + axis
    weight = right[5] * pl.reciprocal(left[5] + right[5], approx=True)
    jump = right[n] - left[n]
    mean = [None] * 4
    for c in (1, 2, 3):
        d = jump if c == n else right[c] - left[c]
        mean[c] = left[c] + weight * d
    enth = left[6] + weight * (right[6] - left[6])
    c2 = enth - (mean[1] * mean[1] + mean[2] * mean[2] + mean[3] * mean[3])
    rc = lax.rsqrt(c2)
    un = mean[n]
    ahead = un > 0.0
    sign = jnp.where(ahead, VEL, -VEL)
    b = jnp.maximum(START - jnp.abs(un) * rc, 0.0)
    s = jnp.minimum(b, KNEE)
    speed = 2.5 * b - s * (2.5 - (2.5 * CURVE) * s)
    wave = speed * ((right[4] - left[4]) * rc - sign * (left[5] * right[5] * jump))
    sc = sign * (c2 * rc)
    up = [jnp.where(ahead, left[c], right[c]) for c in (0, 1, 2, 3, 4, 6)]
    mass = up[0] * up[n]
    t = un * sc
    flux = [mass - wave]
    for c in (1, 2, 3):
        if c == n:
            flux.append((mass * up[c] + up[4]) - wave * (mean[c] - sc))
        else:
            flux.append(mass * up[c] - wave * mean[c])
    flux.append(mass * up[5] - wave * (enth - t - t))
    return flux


def face_sums(lefts, rights, axis):
    f = [roe(a, c, axis) for a, c in zip(lefts, rights)]
    plain, first, second = [], [], []
    for c in range(5):
        lo, hi = f[0][c] + f[1][c], f[2][c] + f[3][c]
        dlo, dhi = f[1][c] - f[0][c], f[3][c] - f[2][c]
        plain.append(lo + hi)
        first.append(hi - lo)
        second.append(dlo + dhi)
    return plain, first, second


def plain_sum(lefts, rights, axis):
    f = [roe(a, c, axis) for a, c in zip(lefts, rights)]
    return [(f[0][c] + f[1][c]) + (f[2][c] + f[3][c]) for c in range(5)]


def walled(sums, axis, solid_a, solid_b, wall_a, wall_b):
    from_a = (solid_b > 0.5) & (solid_a < 0.5)
    from_b = (solid_a > 0.5) & (solid_b < 0.5)
    any_wall = from_a | from_b
    out = []
    for part, pa, pb in zip(sums, wall_a, wall_b):
        new = []
        for c in range(5):
            if c == axis + 1:
                new.append(jnp.where(from_a, pa, jnp.where(from_b, pb, part[c])))
            else:
                new.append(jnp.where(any_wall, 0.0, part[c]))
        out.append(new)
    return out


def wall_sums(p, normal, first, second):
    return (4.0 * (p + normal), 4.0 * first, 4.0 * second)


TANGENTS = ((1, 2), (0, 2), (0, 1))


def flux_kernel(
    edge_ref, index_ref, prim_ref, solid_ref, got_ref, low_ref, high_ref, out_ref,
    g_ref, px_ref, s_ref, gj_ref, gk_ref, cb_ref, cf_ref, ej_ref, ek_ref, pv_ref,
):
    ghost_planes(
        edge_ref,
        index_ref,
        lambda c, q: got_ref[pl.ds(c * 4 + q, PEERS, stride=24), :],
        lambda s, c: (low_ref, high_ref)[s][pl.ds(c * PL, PL), :],
        FARFIELD,
        g_ref,
    )
    for c in range(5):
        px_ref[pl.ds(c * PXR, PL), :] = g_ref[pl.ds(c * 144, PL), :]
        px_ref[pl.ds(c * PXR + PL, ROWS), :] = prim_ref[pl.ds(c * ROWS, ROWS), :]
        px_ref[pl.ds(c * PXR + PL + ROWS, PL), :] = g_ref[pl.ds(c * 144 + PL, PL), :]
    spread_ghosts(g_ref, gj_ref, gk_ref)
    m = masks()

    def slopes(n, _):
        for c in range(5):
            at = c * PXR + PL + n * 8
            out = slopes_of(
                px_ref[rows8(at - PL), :],
                px_ref[rows8(at), :],
                px_ref[rows8(at + PL), :],
                gj_ref[rows8(c * ROWS + n * 8), :],
                gk_ref[rows8(c * ROWS + n * 8), :],
                m,
            )
            for d in range(3):
                s_ref[rows8((d * 5 + c) * ROWS + n * 8), :] = out[d]
        return 0

    lax.fori_loop(0, ROWS // 8, slopes, 0)

    def pack(n, _):
        c, g = n // 3, n % 3

        def value(i):
            return px_ref[rows8(c * PXR + PL + i * PL + g * 8), :]

        def slope(d, i):
            return s_ref[rows8((d * 5 + c) * ROWS + i * PL + g * 8), :]

        for way, compact in ((0, compact_j), (1, compact_k)):
            d = way + 1
            for side in range(2):
                parts = [
                    lambda i: value(i) - slope(d, i) if side == 0 else value(i) + slope(d, i)
                ] + [lambda i, t=t: slope(t, i) for t in TANGENTS[d]]
                for q in range(3):
                    cb_ref[rows8((((way * 2 + side) * 3 + q) * 5 + c) * PL + g * 8), :] = compact(
                        parts[q], side
                    )
        return 0

    lax.fori_loop(0, 15, pack, 0)

    def rim(g, _):
        for way in range(2):
            for side in range(2):
                at = (way * 2 + side) * 15
                quantities = [
                    [cb_ref[rows8((at + q * 5 + c) * PL + g * 8), :] for c in range(5)]
                    for q in range(3)
                ]
                own = four(*quantities)
                beyond = state(
                    [g_ref[rows8(c * 144 + (2 + way * 2 + side) * PL + g * 8), :] for c in range(5)]
                )
                outer = [beyond] * 4
                sums = face_sums(*((outer, own) if side == 0 else (own, outer)), way + 1)
                for q in range(3):
                    for c in range(5):
                        cf_ref[rows8((at + q * 5 + c) * PL + g * 8), :] = sums[q][c]
        return 0

    lax.fori_loop(0, 3, rim, 0)

    def unpack(n, _):
        q, g = n // 3, n % 3
        j0, j1, k0, k1 = (cf_ref[rows8((f * 15 + q) * PL + g * 8), :] for f in range(4))
        for i in range(EDGE):
            at = rows8(q * ROWS + i * PL + g * 8)
            ej_ref[at, :] = spread_j(j0, j1, i)
            ek_ref[at, :] = spread_k(k0, k1, i)
        return 0

    lax.fori_loop(0, 45, unpack, 0)

    def put_back(sums, row):
        for c in range(5):
            for moment, part in ((0, 0), (1, 0), (2, 1), (3, 2)):
                at = rows8((moment * 5 + c) * MR + row)
                out_ref[at, :] = out_ref[at, :] + sums[part][c]

    def column(g, _):
        g8 = g * 8
        below = state([g_ref[rows8(c * 144 + g8), :] for c in range(5)])
        for n in range(4):
            for q in range(7):
                pv_ref[pl.ds((n * 7 + q) * 8, 8), :] = below[q]
        for q in range(20):
            out_ref[rows8(q * MR + g8), :] = jnp.zeros((8, LANES), jnp.float32)

        def plane(i, _):
            row = i * PL + g8
            x = [px_ref[rows8(c * PXR + PL + row), :] for c in range(5)]
            s = [[s_ref[rows8((d * 5 + c) * ROWS + row), :] for c in range(5)] for d in range(3)]
            solid = solid_ref[rows8(row), :]
            child = [
                four([a + b if up else a - b for a, b in zip(x, s[0])], s[1], s[2])
                for up in (False, True)
            ]
            lower = [
                child[0],
                [child[0][0], child[0][1], child[1][0], child[1][1]],
                [child[0][0], child[0][2], child[1][0], child[1][2]],
            ]
            upper = [
                child[1],
                [child[0][2], child[0][3], child[1][2], child[1][3]],
                [child[0][1], child[0][3], child[1][1], child[1][3]],
            ]
            moments = [[None] * 5 for _ in range(4)]

            def add(k, c, value, sign):
                old = moments[k][c]
                if old is None:
                    moments[k][c] = value if sign > 0 else -value
                else:
                    moments[k][c] = old + value if sign > 0 else old - value

            for d in range(3):
                inner = plain_sum(lower[d], upper[d], d)
                for c in range(5):
                    add(d + 1, c, inner[c] + inner[c], -1)

            before = [
                tuple(pv_ref[pl.ds((n * 7 + q) * 8, 8), :] for q in range(7)) for n in range(4)
            ]
            prior = jnp.maximum(row - PL, g8)
            wall_a = wall_sums(
                px_ref[rows8(4 * PXR + PL + prior), :],
                *(s_ref[rows8((d * 5 + 4) * ROWS + prior), :] for d in range(3)),
            )
            wall_b = wall_sums(x[4], -s[0][4], s[1][4], s[2][4])
            sums = face_sums(before, child[0], 0)
            sums = walled(sums, 0, solid_ref[rows8(prior), :], solid, wall_a, wall_b)
            put_back(sums, row)
            for c in range(5):
                add(0, c, sums[0][c], -1)
                add(1, c, sums[0][c], 1)
                add(2, c, sums[1][c], -1)
                add(3, c, sums[2][c], -1)
            for n in range(4):
                for q in range(7):
                    pv_ref[pl.ds((n * 7 + q) * 8, 8), :] = child[1][n][q]

            for d in (1, 2):
                if d == 1:
                    ahead, back = (lambda y: next_j(y, m)), (lambda y: last_j(y, m))
                    first, last, rim_ref = m["j_first"], m["j_last"], ej_ref
                else:
                    ahead, back = next_k, last_k
                    first, last, rim_ref = m["k_first"], m["k_last"], ek_ref
                beyond = [tuple(ahead(y) for y in st) for st in lower[d]]
                sums = face_sums(upper[d], beyond, d)
                t0, t1 = TANGENTS[d]
                wall_a = wall_sums(x[4], s[d][4], s[t0][4], s[t1][4])
                wall_b = [
                    ahead(y) for y in wall_sums(x[4], -s[d][4], s[t0][4], s[t1][4])
                ]
                sums = walled(sums, d, solid, ahead(solid), wall_a, wall_b)
                for c in range(5):
                    edge = [rim_ref[rows8((q * 5 + c) * ROWS + row), :] for q in range(3)]
                    high = [jnp.where(last, edge[q], sums[q][c]) for q in range(3)]
                    low = [jnp.where(first, edge[q], back(sums[q][c])) for q in range(3)]
                    add(0, c, high[0], 1)
                    add(0, c, low[0], -1)
                    add(d + 1, c, high[0], 1)
                    add(d + 1, c, low[0], 1)
                    add(t0 + 1, c, high[1], 1)
                    add(t0 + 1, c, low[1], -1)
                    add(t1 + 1, c, high[2], 1)
                    add(t1 + 1, c, low[2], -1)
            for k in range(4):
                for c in range(5):
                    out_ref[rows8((k * 5 + c) * MR + PL + row), :] = moments[k][c]
            return 0

        lax.fori_loop(0, EDGE, plane, 0)
        before = [tuple(pv_ref[pl.ds((n * 7 + q) * 8, 8), :] for q in range(7)) for n in range(4)]
        above = state([g_ref[rows8(c * 144 + PL + g8), :] for c in range(5)])
        put_back(face_sums(before, [above] * 4, 0), EDGE * PL + g8)
        return 0

    lax.fori_loop(0, 3, column, 0)


def adjoint_kernel(
    edge_ref, index_ref, adj_ref, solid_ref, got0_ref, got_ref, low_ref, high_ref, mom_ref, out_ref,
    g_ref, px_ref, gj_ref, gk_ref, acc_ref,
):
    def received(c, q):
        if c == 0:
            return got0_ref[pl.ds(20 + q, PEERS, stride=24), :]
        return got_ref[pl.ds((c - 1) * 4 + q, PEERS, stride=16), :]

    ghost_planes(
        edge_ref,
        index_ref,
        received,
        lambda s, c: (low_ref, high_ref)[s][pl.ds((c + 5) * PL, PL), :],
        (0.0,) * 5,
        g_ref,
    )
    for c in range(5):
        px_ref[pl.ds(c * PXR, PL), :] = g_ref[pl.ds(c * 144, PL), :]
        px_ref[pl.ds(c * PXR + PL, ROWS), :] = adj_ref[pl.ds(c * ROWS, ROWS), :]
        px_ref[pl.ds(c * PXR + PL + ROWS, PL), :] = g_ref[pl.ds(c * 144 + PL, PL), :]
    spread_ghosts(g_ref, gj_ref, gk_ref)
    m = masks()

    def weigh(n, _):
        total = None
        for c in range(5):
            at = c * PXR + PL + n * 8
            x = px_ref[rows8(at), :]
            s = slopes_of(
                px_ref[rows8(at - PL), :],
                x,
                px_ref[rows8(at + PL), :],
                gj_ref[rows8(c * ROWS + n * 8), :],
                gk_ref[rows8(c * ROWS + n * 8), :],
                m,
            )
            y = [mom_ref[rows8((k * 5 + c) * MR + PL + n * 8), :] for k in range(4)]
            part = WEIGHTS[c] * (x * y[0] + s[0] * y[1] + s[1] * y[2] + s[2] * y[3])
            total = part if total is None else total + part
        acc_ref[rows8(n * 8), :] = jnp.where(
            solid_ref[rows8(n * 8), :] > 0.5, 0.0, jnp.abs(total)
        )
        return 0

    lax.fori_loop(0, ROWS // 8, weigh, 0)
    for t in range(2 * EDGE):
        i, jh = divmod(t, 2)
        out_ref[:, pl.ds(t * LANES, LANES)] = acc_ref[pl.ds(i * PL + jh, NB, stride=2), :]


def shape(*dims):
    return jax.ShapeDtypeStruct(dims, jnp.float32)


def scratch(*rows):
    return [pltpu.VMEM((r, LANES), jnp.float32) for r in rows]


SMEM = pl.BlockSpec(memory_space=pltpu.SMEM)
VMEM = pl.BlockSpec(memory_space=pltpu.VMEM)
PARAMS = pltpu.CompilerParams(vmem_limit_bytes=VMEM_LIMIT)


def prep(flow, adjoint, cut_flag, own, vertical):
    return pl.pallas_call(
        prep_kernel,
        out_shape=[
            shape(5 * ROWS, LANES),
            shape(5 * ROWS, LANES),
            shape(ROWS, LANES),
            shape(10 * FACES, LANES),
            shape(10 * PL, LANES),
            shape(10 * PL, LANES),
            jax.ShapeDtypeStruct((288, LANES), jnp.int32),
        ],
        in_specs=[VMEM] * 5,
        out_specs=[VMEM] * 7,
        compiler_params=PARAMS,
    )(flow.transpose(1, 0, 2), adjoint.transpose(1, 0, 2), cut_flag[None], own, vertical)


def reply(me, asked, layers):
    return pl.pallas_call(
        reply_kernel,
        out_shape=[shape(24 * PEERS, LANES), shape(16 * PEERS, LANES)],
        in_specs=[SMEM, VMEM, VMEM],
        out_specs=[VMEM] * 2,
        compiler_params=PARAMS,
    )(me, asked, layers)


def fluxes(edge, index, prim, solid, got, low, high):
    return pl.pallas_call(
        flux_kernel,
        out_shape=shape(20 * MR, LANES),
        in_specs=[SMEM] + [VMEM] * 6,
        out_specs=VMEM,
        scratch_shapes=scratch(
            5 * 144, 5 * PXR, 15 * ROWS, 5 * ROWS, 5 * ROWS, 60 * PL, 60 * PL, 15 * ROWS, 15 * ROWS, 224
        ),
        compiler_params=PARAMS,
    )(edge, index, prim, solid, got, low, high)


def weights(edge, index, adj, solid, got0, got, low, high, moments):
    return pl.pallas_call(
        adjoint_kernel,
        out_shape=shape(NB, EDGE * EDGE * EDGE),
        in_specs=[SMEM] + [VMEM] * 8,
        out_specs=VMEM,
        scratch_shapes=scratch(5 * 144, 5 * PXR, 5 * ROWS, 5 * ROWS, ROWS),
        compiler_params=PARAMS,
    )(edge, index, adj, solid, got0, got, low, high, moments)


def packed_requests(lateral_owner, lateral_link, vertical_link):
    link = lateral_link.T
    far = lax.broadcasted_iota(jnp.int32, link.shape, 0) ^ 1
    own = (lateral_owner[:, :, 0].T * 64 + link // 5 * 4 + far) * 8 + link % 5
    return own, vertical_link.T // 5 * 8 + vertical_link.T % 5


def exchange(block, axis):
    chunks = block.reshape(PEERS, -1, LANES)
    out = lax.all_to_all(chunks, axis, split_axis=0, concat_axis=0, tiled=True)
    return out.reshape(-1, LANES)


def local(flow, adjoint, cut_flag, lateral_owner, lateral_link, vertical_link):
    own, vertical = packed_requests(lateral_owner, lateral_link, vertical_link)
    asked = lax.all_gather(own, "blk")
    prim, adj, solid, layers, low_face, high_face, index = prep(
        flow, adjoint, cut_flag, own, vertical
    )
    regions = lax.axis_size("grp")
    region = lax.axis_index("grp")
    low = lax.ppermute(high_face, "grp", [(r, r + 1) for r in range(regions - 1)])
    high = lax.ppermute(low_face, "grp", [(r + 1, r) for r in range(regions - 1)])
    me = lax.axis_index("blk").astype(jnp.int32).reshape(1)
    first, second = reply(me, asked, layers)
    got0 = exchange(first, "blk")
    second, got0 = lax.optimization_barrier((second, got0))
    got = exchange(second, "blk")
    edge = jnp.stack([region == 0, region == regions - 1]).astype(jnp.int32)
    moments = fluxes(edge, index, prim, solid, got0, low, high)
    return weights(edge, index, adj, solid, got0, got, low, high, moments)


def solution(mesh):
    in_specs = (
        P(("blk", "grp"), None, None),
        P(("blk", "grp"), None, None),
        P(("blk", "grp"), None),
        P(("blk", "grp"), None, None),
        P(("blk", "grp"), None),
        P(("blk", "grp"), None),
    )
    out_specs = P(("blk", "grp"), None)
    return jax.shard_map(local, mesh=mesh, in_specs=in_specs, out_specs=out_specs, check_vma=False)
```

time: 949 us -> 175 us (0.18); the launches traced: 936 us -> 175 us
  local copies, waits for them, and re-layouts: 527 us -> 1.46 us
  other arithmetic: 193 us -> 3.29 us
  matrix products: 153 us -> 0 us
  blocking collectives: 0 us -> 87.4 us
  Pallas kernels: 0 us -> 67.6 us
  starting transfers between devices: 42.3 us -> 10.7 us
  loops' own time: 11.8 us -> 0 us
    dot_general x60 -> x0, matrix products: 153 us -> none  [the longest x24 105 us: prolong(): jnp.dot(stacked.reshape(channels * 2 * edge_cells, 3 * plane_size), expan...]
    slice x288 -> x0, local copies, waits for them, and re-layouts: 130 us -> none  [the longest x2 22.9 us: local(): replies[:, :, :5]]
    reshape x150 -> x0, local copies, waits for them, and re-layouts: 105 us -> none  [the longest x12 24.9 us: residual(): jnp.repeat(flux_top, size_fine, axis=2)]
    broadcast_in_dim x184 -> x0, local copies, waits for them, and re-layouts: 72.4 us -> none  [the longest x24 20.1 us: prolong(): jnp.repeat(slopes[0], 2, axis=1) * layer_sign]
    select_n x99 -> x0, other arithmetic: 72.1 us -> none  [the longest x24 27.2 us: minmod(): jnp.where(first_diff * second_diff > 0.0, jnp.sign(first_diff) * jnp.mini...]
    pallas_call x0 -> x4, Pallas kernels: none -> 67.6 us  [the longest x1 43.2 us: fluxes(): pl.pallas_call(flux_kernel, out_shape=shape(20 * MR, LANES), in_specs=[SM...]
    all_gather x0 -> x1, blocking collectives: none -> 57.9 us  [local(): asked = lax.all_gather(own, 'blk')]
    squeeze x228 -> x0, local copies, waits for them, and re-layouts: 43.9 us -> none  [the longest x12 14.9 us: shifted(): upper_x = jnp.concatenate([values[:, 1:], ghosts[1][:, None]], axis=1)]
  transfers between devices with their start and end apart: 7 -> 3, of which waited for: 1 -> 2; matrix products, arithmetic and copies ran while one was open for 18% -> 0% of each run, Pallas kernels for 0% -> 25%
where the time goes in v1:
time: 175 us
  blocking collectives  87.4 us (50%)
  Pallas kernels  67.6 us (39%)
  starting transfers between devices  10.7 us (6%)
  waiting for transfers between devices  4.13 us (2%)
  other arithmetic  3.29 us (2%)
    all_gather x1, blocking collectives, local(): asked = lax.all_gather(own, 'blk')  57.9 us
    pallas_call x1, Pallas kernels, fluxes(): pl.pallas_call(flux_kernel, out_shape=shape(20 * MR, LANES), in_specs=[SM...  43.2 us
    all_to_all x1, blocking collectives, exchange(): out = lax.all_to_all(chunks, axis, split_axis=0, concat_axis=0, tiled=True)  29.5 us
    pallas_call x1, Pallas kernels, weights(): pl.pallas_call(adjoint_kernel, out_shape=shape(NB, EDGE * EDGE * EDGE), i...  11.8 us
    pallas_call x1, Pallas kernels, prep(): pl.pallas_call(prep_kernel, out_shape=[shape(5 * ROWS, LANES), shape(5 *...  8.41 us
    all_to_all x1, starting transfers between devices, exchange(): out = lax.all_to_all(chunks, axis, split_axis=0, concat_axis=0, tiled=True)  6.24 us
    pallas_call x1, Pallas kernels, reply(): pl.pallas_call(reply_kernel, out_shape=[shape(24 * PEERS, LANES), shape(1...  4.12 us
    ppermute x1, waiting for transfers between devices, local(): lax.ppermute(low_face, 'grp', [(r + 1, r) for r in range(regions - 1)])  3.8 us
  transfers between devices with their start and end apart: 3, of which 2 were waited for; matrix products, arithmetic and copies ran while one was open for 0% of the time, Pallas kernels for 25%

profile of v1, /device:TPU:1, one launch (start us, length us, event | category | flops | bytes accessed | tf_op | source)
XLA Modules:
  0.0 174.6 jit_solution(16754587400526817743)
XLA Ops:
  0.0 1.3 fusion.9.vertical_ref
  1.3 0.7 broadcast_multiply_fusion
  2.0 0.8 fusion.4.own_ref
  2.7 0.0 copy-start.3
  2.7 57.9 %all-gather.1.asked_ref = s32[64,4,12]{2,1,0:T(4,128)} all-gather(s32[1,4,12]{2,1,0:T(4,128)S(1)} %bitcast.51), channel_id=2, replica_groups=mesh['blk'=64,'grp'=4] {'blk'}, dimensions={0}, use_global_device_ids=true | all-gather | bytes 12480 | tf_op jit(solution)/shard_map/all_gather | solution.py:736
  60.6 0.0 copy-done.3
  60.6 8.4 %shard_map.64 = (f32[1920,128]{1,0:T(8,128)}, f32[1920,128]{1,0:T(8,128)}, f32[384,128]{1,0:T(8,128)}, f32[960,128]{1,0:T(8,128)}, f32[240,128]{1,0:T(8,128)}, /*index=5*/f32[240,128]{1,0:T(8,128)}, s32[288,128]{1,0:T(8,128)}) custom-call(f32[5,12,4096]{2,1,0:T(8,128)} %bitcast.47, f32[5,12,4096]{2,1,0:T(8,128)} %bitcast.48, s32[1,12,4096]{2,1,0:T(8,128)} %bitcast.50, ...), custom_call_target="tpu_custom_call" | custom-call | tf_op jit(solution)/shard_map/pallas_call | solution.py:670
  69.0 4.1 %shard_map.65 = (f32[1536,128]{1,0:T(8,128)}, f32[1024,128]{1,0:T(8,128)}) custom-call(s32[1]{0:T(128)} %bitcast.13.me_ref, s32[64,4,12]{2,1,0:T(4,128)} %all-gather.1.asked_ref, f32[960,128]{1,0:T(8,128)} %get-tuple-element.19.lat_ref), custom_call_target="tpu_custom_call" | custom-call | tf_op jit(solution)/shard_map/pallas_call | solution.py:688
  73.1 0.0 copy-start.5
  73.1 29.5 %all_to_all.10 = f32[64,24,128]{2,1,0:T(8,128)} all-to-all(f32[64,24,128]{2,1,0:T(8,128)} %bitcast.49), channel_id=1, replica_groups=mesh['blk'=64,'grp'=4] {'blk'}, dimensions={0} | all-to-all | bytes 1572864 | tf_op jit(solution)/shard_map/all_to_all | solution.py:730
  102.6 6.2 %all-to-all-start.1 = ((f32[64,16,128]{2,1,0:T(8,128)}), f32[64,16,128]{2,1,0:T(8,128)S(1)}, u32[]{:S(2)}, u32[]{:S(2)}) async-start(f32[64,16,128]{2,1,0:T(8,128)} %bitcast.17), calls=%async_computation.1 | async-start | bytes 1048576 | tf_op jit(solution)/shard_map/all_to_all | solution.py:730
  108.9 0.0 copy-done.5
  108.9 3.2 %collective-permute-start = (f32[240,128]{1,0:T(8,128)S(1)}, f32[240,128]{1,0:T(8,128)S(1)}, u32[]{:S(2)}, u32[]{:S(2)}) collective-permute-start(f32[240,128]{1,0:T(8,128)S(1)} %copy-done.5), channel_id=1, source_target_pairs={{0,1},{1,2},{2,3},{4,5},{5,6},{6,7},{8,9},{9,10},{10,11},{12,13},{... | collective-permute-start | bytes 368648 | tf_op jit(solution)/shard_map/ppermute | solution.py:742
  112.1 0.0 copy-done.4
  112.1 1.3 collective-permute-start.1
  113.4 0.6 add_convert_fusion.edge_ref
  114.0 0.3 collective-permute-done.low_ref
  114.3 3.8 %collective-permute-done.1.high_ref = f32[240,128]{1,0:T(8,128)S(1)} collective-permute-done((f32[240,128]{1,0:T(8,128)S(1)}, f32[240,128]{1,0:T(8,128)S(1)}, u32[]{:S(2)}, u32[]{:S(2)}) %collective-permute-start.1) | collective-permute-done | bytes 122912 | tf_op jit(solution)/shard_map/ppermute | solution.py:743
  118.1 0.0 copy-done.1
  118.1 0.6 copy-done.2
  118.7 43.2 %shard_map.66.mom_ref = f32[8160,128]{1,0:T(8,128)} custom-call(s32[2]{0:T(128)} %add_convert_fusion.edge_ref, s32[288,128]{1,0:T(8,128)} %get-tuple-element.16.index_ref, f32[1920,128]{1,0:T(8,128)} %get-tuple-element.26.prim_ref, f32[384,128]{1,0:T(8,128)} %get-tuple-element.18.solid_ref, f32[1536,128]{1,0:T(8,128)} %bitcast.44, f32[240,128]{1,0:T(8,128)} %copy-done.1, ...), custom_call_target="tpu_custom_call" | custom-call | tf_op jit(solution)/shard_map/pallas_call | solution.py:698
  162.0 0.0 all-to-all-done.1
  162.0 0.8 copy-done
  162.8 11.8 %shard_map.67 = f32[12,4096]{1,0:T(8,128)} custom-call(s32[2]{0:T(128)} %add_convert_fusion.edge_ref, s32[288,128]{1,0:T(8,128)} %get-tuple-element.16.index_ref, f32[1920,128]{1,0:T(8,128)} %get-tuple-element.17.adj_ref, f32[384,128]{1,0:T(8,128)} %get-tuple-element.18.solid_ref, f32[1536,128]{1,0:T(8,128)} %bitcast.45, f32[1024,128]{1,0:T(8,128)} %bitcast.46, ...), custom_call_target="tpu_custom_call" | custom-call | tf_op jit(solution)/shard_map/pallas_call | solution.py:711
  (5 shorter events, 0.0 us)
Async XLA Ops:
  2.7 57.9 %copy-start.3 = (s32[4,12]{1,0:T(4,128)}, s32[4,12]{1,0:T(4,128)S(1)}, u32[]{:S(2)}) copy-start(s32[4,12]{1,0:T(4,128)S(1)} %fusion.4.own_ref) | copy-start | bytes 580
  73.1 35.7 %copy-start.5 = (f32[240,128]{1,0:T(8,128)S(1)}, f32[240,128]{1,0:T(8,128)}, u32[]{:S(2)}) copy-start(f32[240,128]{1,0:T(8,128)} %get-tuple-element.24) | copy-start | bytes 368644
  73.1 38.9 %copy-start.4 = (f32[240,128]{1,0:T(8,128)S(1)}, f32[240,128]{1,0:T(8,128)}, u32[]{:S(2)}) copy-start(f32[240,128]{1,0:T(8,128)} %get-tuple-element.25) | copy-start | bytes 368644
  102.6 59.4 %all-to-all-start.1 = ((f32[64,16,128]{2,1,0:T(8,128)}), f32[64,16,128]{2,1,0:T(8,128)S(1)}, u32[]{:S(2)}, u32[]{:S(2)}) async-start(f32[64,16,128]{2,1,0:T(8,128)} %bitcast.17), calls=%async_computation.1 | async-start | bytes 1048576 | tf_op jit(solution)/shard_map/all_to_all | solution.py:730
  108.9 5.4 %collective-permute-start = (f32[240,128]{1,0:T(8,128)S(1)}, f32[240,128]{1,0:T(8,128)S(1)}, u32[]{:S(2)}, u32[]{:S(2)}) collective-permute-start(f32[240,128]{1,0:T(8,128)S(1)} %copy-done.5), channel_id=1, source_target_pairs={{0,1},{1,2},{2,3},{4,5},{5,6},{6,7},{8,9},{9,10},{10,11},{12,13},{... | collective-permute-start | bytes 368648 | tf_op jit(solution)/shard_map/ppermute | solution.py:742
  112.1 6.0 %collective-permute-start.1 = (f32[240,128]{1,0:T(8,128)S(1)}, f32[240,128]{1,0:T(8,128)S(1)}, u32[]{:S(2)}, u32[]{:S(2)}) collective-permute-start(f32[240,128]{1,0:T(8,128)S(1)} %copy-done.4), channel_id=1, source_target_pairs={{1,0},{2,1},{3,2},{5,4},{6,5},{7,6},{9,8},{10,9},{11,10},{13,12},{... | collective-permute-start | bytes 368648 | tf_op jit(solution)/shard_map/ppermute | solution.py:743
  114.3 3.8 %copy-start.1 = (f32[240,128]{1,0:T(8,128)}, f32[240,128]{1,0:T(8,128)S(1)}, u32[]{:S(2)}) copy-start(f32[240,128]{1,0:T(8,128)S(1)} %collective-permute-done.low_ref) | copy-start | bytes 368644
  118.1 0.6 copy-start.2
  162.0 0.8 copy-start

commit v2 on v1

--- a/solution.py
+++ b/solution.py
@@ -733,7 +733,9 @@
 
 def local(flow, adjoint, cut_flag, lateral_owner, lateral_link, vertical_link):
     own, vertical = packed_requests(lateral_owner, lateral_link, vertical_link)
-    asked = lax.all_gather(own, "blk")
+    asked = lax.all_to_all(
+        jnp.broadcast_to(own, (PEERS,) + own.shape), "blk", split_axis=0, concat_axis=0, tiled=True
+    )
     prim, adj, solid, layers, low_face, high_face, index = prep(
         flow, adjoint, cut_flag, own, vertical
     )
@@ -743,6 +745,7 @@
     high = lax.ppermute(low_face, "grp", [(r + 1, r) for r in range(regions - 1)])
     me = lax.axis_index("blk").astype(jnp.int32).reshape(1)
     first, second = reply(me, asked, layers)
+    first, second, low, high = lax.optimization_barrier((first, second, low, high))
     got0 = exchange(first, "blk")
     second, got0 = lax.optimization_barrier((second, got0))
     got = exchange(second, "blk")

time: 175 us -> 138 us (0.79)
  blocking collectives: 87.4 us -> 28.2 us
  starting transfers between devices: 10.7 us -> 23.9 us
  waiting for transfers between devices: 4.13 us -> 11.1 us
    all_gather x1 -> x0, blocking collectives: 57.9 us -> none  [local(): asked = lax.all_gather(own, 'blk')]
    all_to_all x0 -> x1, starting transfers between devices: none -> 12.4 us  [local(): lax.all_to_all(jnp.broadcast_to(own, (PEERS,) + own.shape), 'blk', split_...]
    all_to_all x0 -> x1, waiting for transfers between devices: none -> 11.1 us  [local(): lax.all_to_all(jnp.broadcast_to(own, (PEERS,) + own.shape), 'blk', split_...]
    ppermute x1, waiting for transfers between devices: 3.8 us -> 0.01 us  [local(): lax.ppermute(low_face, 'grp', [(r + 1, r) for r in range(regions - 1)])]
  transfers between devices with their start and end apart: 3 -> 4, of which waited for: 2 -> 1; matrix products, arithmetic and copies ran while one was open for 0% -> 1% of each run, Pallas kernels for 25% -> 35%
where the time goes in v2:
time: 138 us; the launch traced here: 137 us
  Pallas kernels  67.6 us (49%)
  blocking collectives  28.2 us (20%)
  starting transfers between devices  23.9 us (17%)
  waiting for transfers between devices  11.1 us (8%)
  other arithmetic  3.96 us (3%)
  local copies, waits for them, and re-layouts  2.15 us (2%)
    pallas_call x1, Pallas kernels, fluxes(): pl.pallas_call(flux_kernel, out_shape=shape(20 * MR, LANES), in_specs=[SM...  43.2 us
    all_to_all x1, blocking collectives, exchange(): out = lax.all_to_all(chunks, axis, split_axis=0, concat_axis=0, tiled=True)  28.2 us
    all_to_all x1, starting transfers between devices, local(): lax.all_to_all(jnp.broadcast_to(own, (PEERS,) + own.shape), 'blk', split_...  12.4 us
    pallas_call x1, Pallas kernels, weights(): pl.pallas_call(adjoint_kernel, out_shape=shape(NB, EDGE * EDGE * EDGE), i...  11.8 us
    all_to_all x1, waiting for transfers between devices, local(): lax.all_to_all(jnp.broadcast_to(own, (PEERS,) + own.shape), 'blk', split_...  11.1 us
    pallas_call x1, Pallas kernels, prep(): pl.pallas_call(prep_kernel, out_shape=[shape(5 * ROWS, LANES), shape(5 *...  8.46 us
    all_to_all x1, starting transfers between devices, exchange(): out = lax.all_to_all(chunks, axis, split_axis=0, concat_axis=0, tiled=True)  6.11 us
    pallas_call x1, Pallas kernels, reply(): pl.pallas_call(reply_kernel, out_shape=[shape(24 * PEERS, LANES), shape(1...  4.12 us
  transfers between devices with their start and end apart: 4, of which 1 were waited for; matrix products, arithmetic and copies ran while one was open for 1% of the time, Pallas kernels for 35%

profile of v2, /device:TPU:1, one launch (start us, length us, event | category | flops | bytes accessed | tf_op | source)
XLA Modules:
  0.0 137.0 jit_solution(1065557016619568849)
XLA Ops:
  0.0 1.3 fusion.9.vertical_ref
  1.3 0.7 broadcast_multiply_fusion
  2.0 1.3 fusion.4.own_ref
  3.3 8.5 %shard_map.64 = (f32[1920,128]{1,0:T(8,128)}, f32[1920,128]{1,0:T(8,128)}, f32[384,128]{1,0:T(8,128)}, f32[960,128]{1,0:T(8,128)}, f32[240,128]{1,0:T(8,128)}, /*index=5*/f32[240,128]{1,0:T(8,128)}, s32[288,128]{1,0:T(8,128)}) custom-call(f32[5,12,4096]{2,1,0:T(8,128)} %bitcast.46, f32[5,12,4096]{2,1,0:T(8,128)} %bitcast.47, s32[1,12,4096]{2,1,0:T(8,128)} %bitcast.49, ...), custom_call_target="tpu_custom_call" | custom-call | tf_op jit(solution)/shard_map/pallas_call | solution.py:670
  11.8 4.0 %collective-permute-start = (f32[240,128]{1,0:T(8,128)}, f32[240,128]{1,0:T(8,128)S(1)}, u32[]{:S(2)}, u32[]{:S(2)}) collective-permute-start(f32[240,128]{1,0:T(8,128)} %get-tuple-element.26), channel_id=1, source_target_pairs={{0,1},{1,2},{2,3},{4,5},{5,6},{6,7},{8,9},{9,10},{10,11},{12,13},{... | collective-permute-start | bytes 368648 | tf_op jit(solution)/shard_map/ppermute | solution.py:744
  15.8 1.3 collective-permute-start.1
  17.1 0.0 copy-done.4
  17.1 0.7 broadcast_in_dim.7
  17.8 12.4 %all-to-all-start = ((s32[64,4,12]{2,1,0:T(4,128)}), s32[64,4,12]{2,1,0:T(4,128)S(1)}, u32[]{:S(2)}, u32[]{:S(2)}) async-start(s32[64,4,12]{2,1,0:T(4,128)} %broadcast_in_dim.7), calls=%async_computation | async-start | bytes 262144 | tf_op jit(solution)/shard_map/all_to_all | solution.py:736
  30.2 11.1 %all-to-all-done.asked_ref = s32[64,4,12]{2,1,0:T(4,128)S(1)} async-done(((s32[64,4,12]{2,1,0:T(4,128)}), s32[64,4,12]{2,1,0:T(4,128)S(1)}, u32[]{:S(2)}, u32[]{:S(2)}) %all-to-all-start) | async-done | bytes 12320 | tf_op jit(solution)/shard_map/all_to_all | solution.py:736
  41.3 0.7 copy-done.1
  42.0 4.1 %shard_map.65 = (f32[1536,128]{1,0:T(8,128)}, f32[1024,128]{1,0:T(8,128)}) custom-call(s32[1]{0:T(128)} %bitcast.13.me_ref, s32[64,4,12]{2,1,0:T(4,128)} %copy-done.1, f32[960,128]{1,0:T(8,128)} %get-tuple-element.23.lat_ref), custom_call_target="tpu_custom_call" | custom-call | tf_op jit(solution)/shard_map/pallas_call | solution.py:688
  46.1 0.0 collective-permute-done.low_ref
  46.1 0.0 collective-permute-done.1.high_ref
  46.1 0.0 copy-start.3
  46.1 28.2 %all_to_all.15 = f32[64,24,128]{2,1,0:T(8,128)} all-to-all(f32[64,24,128]{2,1,0:T(8,128)} %bitcast.48), channel_id=1, replica_groups=mesh['blk'=64,'grp'=4] {'blk'}, dimensions={0} | all-to-all | bytes 1572864 | tf_op jit(solution)/shard_map/all_to_all | solution.py:730
  74.4 0.0 copy-done.2
  74.4 0.0 copy-done.3
  74.4 6.1 %all-to-all-start.2 = ((f32[64,16,128]{2,1,0:T(8,128)}), f32[64,16,128]{2,1,0:T(8,128)S(1)}, u32[]{:S(2)}, u32[]{:S(2)}) async-start(f32[64,16,128]{2,1,0:T(8,128)} %bitcast.16), calls=%async_computation.2 | async-start | bytes 1048576 | tf_op jit(solution)/shard_map/all_to_all | solution.py:730
  80.5 0.7 add_convert_fusion.edge_ref
  81.2 43.2 %shard_map.66.mom_ref = f32[8160,128]{1,0:T(8,128)} custom-call(s32[2]{0:T(128)} %add_convert_fusion.edge_ref, s32[288,128]{1,0:T(8,128)} %get-tuple-element.20.index_ref, f32[1920,128]{1,0:T(8,128)} %get-tuple-element.34.prim_ref, f32[384,128]{1,0:T(8,128)} %get-tuple-element.22.solid_ref, f32[1536,128]{1,0:T(8,128)} %bitcast.43, f32[240,128]{1,0:T(8,128)} %copy-done.2, ...), custom_call_target="tpu_custom_call" | custom-call | tf_op jit(solution)/shard_map/pallas_call | solution.py:698
  124.4 0.0 all-to-all-done.2
  124.4 0.8 copy-done
  125.2 11.8 %shard_map.67 = f32[12,4096]{1,0:T(8,128)} custom-call(s32[2]{0:T(128)} %add_convert_fusion.edge_ref, s32[288,128]{1,0:T(8,128)} %get-tuple-element.20.index_ref, f32[1920,128]{1,0:T(8,128)} %get-tuple-element.21.adj_ref, f32[384,128]{1,0:T(8,128)} %get-tuple-element.22.solid_ref, f32[1536,128]{1,0:T(8,128)} %bitcast.44, f32[1024,128]{1,0:T(8,128)} %bitcast.45, ...), custom_call_target="tpu_custom_call" | custom-call | tf_op jit(solution)/shard_map/pallas_call | solution.py:711
  (5 shorter events, 0.0 us)
Async XLA Ops:
  3.3 13.8 %copy-start.4 = (s32[4,12]{1,0:T(4,128)S(1)}, s32[4,12]{1,0:T(4,128)}, u32[]{:S(2)}) copy-start(s32[4,12]{1,0:T(4,128)} %fusion.4.own_ref) | copy-start | bytes 580
  11.8 34.4 %collective-permute-start = (f32[240,128]{1,0:T(8,128)}, f32[240,128]{1,0:T(8,128)S(1)}, u32[]{:S(2)}, u32[]{:S(2)}) collective-permute-start(f32[240,128]{1,0:T(8,128)} %get-tuple-element.26), channel_id=1, source_target_pairs={{0,1},{1,2},{2,3},{4,5},{5,6},{6,7},{8,9},{9,10},{10,11},{12,13},{... | collective-permute-start | bytes 368648 | tf_op jit(solution)/shard_map/ppermute | solution.py:744
  15.8 30.3 %collective-permute-start.1 = (f32[240,128]{1,0:T(8,128)}, f32[240,128]{1,0:T(8,128)S(1)}, u32[]{:S(2)}, u32[]{:S(2)}) collective-permute-start(f32[240,128]{1,0:T(8,128)} %get-tuple-element.27), channel_id=1, source_target_pairs={{1,0},{2,1},{3,2},{5,4},{6,5},{7,6},{9,8},{10,9},{11,10},{13,12},{... | collective-permute-start | bytes 368648 | tf_op jit(solution)/shard_map/ppermute | solution.py:745
  17.8 23.6 %all-to-all-start = ((s32[64,4,12]{2,1,0:T(4,128)}), s32[64,4,12]{2,1,0:T(4,128)S(1)}, u32[]{:S(2)}, u32[]{:S(2)}) async-start(s32[64,4,12]{2,1,0:T(4,128)} %broadcast_in_dim.7), calls=%async_computation | async-start | bytes 262144 | tf_op jit(solution)/shard_map/all_to_all | solution.py:736
  41.3 0.7 copy-start.1
  46.1 28.3 %copy-start.2 = (f32[240,128]{1,0:T(8,128)}, f32[240,128]{1,0:T(8,128)S(1)}, u32[]{:S(2)}) copy-start(f32[240,128]{1,0:T(8,128)S(1)} %collective-permute-done.low_ref) | copy-start | bytes 368644
  46.1 28.3 %copy-start.3 = (f32[240,128]{1,0:T(8,128)}, f32[240,128]{1,0:T(8,128)S(1)}, u32[]{:S(2)}) copy-start(f32[240,128]{1,0:T(8,128)S(1)} %collective-permute-done.1.high_ref) | copy-start | bytes 368644
  74.4 50.0 %all-to-all-start.2 = ((f32[64,16,128]{2,1,0:T(8,128)}), f32[64,16,128]{2,1,0:T(8,128)S(1)}, u32[]{:S(2)}, u32[]{:S(2)}) async-start(f32[64,16,128]{2,1,0:T(8,128)} %bitcast.16), calls=%async_computation.2 | async-start | bytes 1048576 | tf_op jit(solution)/shard_map/all_to_all | solution.py:730
  124.4 0.8 copy-start

commit v3 on v2

v3 whole, which is shorter than its diff:
```python
import math

import jax
import jax.numpy as jnp
from jax import lax
from jax.experimental import pallas as pl
from jax.experimental.pallas import tpu as pltpu
from jax.sharding import PartitionSpec as P

EDGE = 16
NB = 12
PL = 2 * NB
ROWS = EDGE * PL
LANES = 128
PEERS = 64
FACES = 4 * PL
PXR = (EDGE + 2) * PL
MR = (EDGE + 1) * PL

VEL = math.sqrt(0.2)
PRESS = 0.2
WEIGHTS = (1.0 / VEL, 5.0, 5.0, 5.0, 2.5 / VEL)
FARFIELD = (1.0, 0.0, 0.0, 0.3 * VEL, PRESS)
KNEE = 0.4 / math.sqrt(5.0)
START = 1.2 / math.sqrt(5.0)
CURVE = 1.25 * math.sqrt(5.0)

VMEM_LIMIT = 56 * 2**20


def lane():
    return lax.broadcasted_iota(jnp.int32, (8, LANES), 1)


def even_row():
    return lax.broadcasted_iota(jnp.int32, (8, LANES), 0) % 2 == 0


def rolled(x, amount, axis=1):
    size = x.shape[axis]
    amount = amount % size
    return x if amount == 0 else pltpu.roll(x, amount, axis)


def rows8(start):
    if isinstance(start, int):
        return pl.ds(start, 8)
    return pl.ds(pl.multiple_of(start, 8), 8)


def compact_j(load, side):
    low = lane() // EDGE
    halves = []
    for ih in range(2):
        total = None
        for il in range(8):
            x = rolled(load(ih * 8 + il), 16 * il if side == 0 else 16 * il + 16)
            total = x if total is None else jnp.where(low == il, x, total)
        halves.append(total)
    if side == 0:
        return jnp.where(even_row(), halves[0], rolled(halves[1], 1, 0))
    return jnp.where(even_row(), rolled(halves[0], -1, 0), halves[1])


def compact_k(load, side):
    depth = lane() % EDGE
    total = None
    for i in range(EDGE):
        x = rolled(load(i), i if side == 0 else i - 15)
        total = x if total is None else jnp.where(depth == i, x, total)
    return total


def compact_depths(load, count):
    low = lane() // EDGE
    spots = list(range(count)) + [7 - n for n in range(count)]
    halves = []
    for ih in range(2):
        totals = [None] * len(spots)
        for il in range(8):
            x = rolled(load(ih * 8 + il), 16 * il)
            for n, spot in enumerate(spots):
                t = totals[n]
                totals[n] = x if t is None else jnp.where(low == (spot + il) % 8, x, t)
        halves.append([rolled(t, -16 * spot) for t, spot in zip(totals, spots)])
    even = even_row()
    near = [jnp.where(even, a, rolled(c, 1, 0)) for a, c in zip(halves[0][:count], halves[1][:count])]
    far = [jnp.where(even, rolled(a, -1, 0), c) for a, c in zip(halves[0][count:], halves[1][count:])]
    return near, far


def spread_j(low, high, i):
    ih, il = i // 8, i % 8
    a = low if ih == 0 else rolled(low, -1, 0)
    c = rolled(high, 1, 0) if ih == 0 else high
    return jnp.where(even_row(), rolled(a, -16 * il), rolled(c, 16 * (7 - il)))


def spread_k(low, high, i):
    return jnp.where(lane() % EDGE == 0, rolled(low, -i), rolled(high, 15 - i))


def column_of(packed, rows, width):
    at = lax.broadcasted_iota(jnp.int32, (rows, width), 0) // 2
    spot = lax.broadcasted_iota(jnp.int32, (rows, width), 1)
    return jnp.sum(jnp.where(at == spot, packed, 0.0), axis=1, keepdims=True)


def index_tables(own, vertical, index_ref):
    spots = lax.broadcasted_iota(jnp.int32, (PL, LANES), 1)
    half = lax.broadcasted_iota(jnp.int32, (PL, LANES), 0) % 2
    low, depth = spots // EDGE, spots % EDGE
    wide = (4 * half + low // 2) * EDGE + depth // 2

    def store(f, code, row_part, col_part, base, step):
        full = code == 4
        index_ref[pl.ds(f * PL, PL), :] = jnp.where(full, spots, wide + 8 * col_part)
        index_ref[pl.ds(144 + f * PL, PL), :] = base + step * jnp.where(full, half, row_part)

    at = lax.broadcasted_iota(jnp.int32, (PL, NB), 0) // 2
    spot = lax.broadcasted_iota(jnp.int32, (PL, NB), 1)
    entries = [own[f : f + 1, :].astype(jnp.int32) for f in range(4)]
    holders = [e >> 9 for e in entries]
    for f in range(4):
        value = column_of(own[f : f + 1, :], PL, NB).astype(jnp.int32)
        owner, code = value >> 9, value & 7
        rank = jnp.zeros((PL, 1), jnp.float32)
        for other in range(f + 1):
            same = holders[other] == owner
            if other == f:
                same = same & (spot < at)
            rank = rank + jnp.sum(jnp.where(same, 1.0, 0.0), axis=1, keepdims=True)
        rank = rank.astype(jnp.int32)
        store(f, code, code >> 1, code & 1, rank * 2 * PEERS + owner, PEERS)
    for side in range(2):
        value = column_of(vertical[side : side + 1, :], PL, NB).astype(jnp.int32)
        slot, code = value >> 3, value & 7
        store(4 + side, code, code & 1, code >> 1, slot * 2, 1)


def prep_kernel(
    flow_ref, adj_ref, flag_ref, own_ref, vertical_ref,
    prim_ref, adjl_ref, solid_ref, lat_ref, low_ref, high_ref, index_ref,
):
    def relaid(ref, c, out_ref):
        for t in range(2 * EDGE):
            i, jh = divmod(t, 2)
            part = ref[c, :, pl.ds(t * LANES, LANES)]
            out_ref[pl.ds(i * PL + jh + c * ROWS, NB, stride=2), :] = part.astype(jnp.float32)

    for c in range(5):
        relaid(flow_ref, c, prim_ref)
        relaid(adj_ref, c, adjl_ref)
    relaid(flag_ref, 0, solid_ref)
    index_tables(
        own_ref[...].astype(jnp.float32), vertical_ref[...].astype(jnp.float32), index_ref
    )

    def convert(n, _):
        at = [rows8(c * ROWS + n * 8) for c in range(5)]
        rho = prim_ref[at[0]]
        inv = 1.0 / rho
        vel = [prim_ref[at[c]] * inv for c in (1, 2, 3)]
        square = vel[0] * vel[0] + vel[1] * vel[1] + vel[2] * vel[2]
        prim_ref[at[4]] = (0.4 * PRESS) * (prim_ref[at[4]] - 0.5 * rho * square)
        for c in range(3):
            prim_ref[at[c + 1]] = vel[c] * VEL
        return 0

    lax.fori_loop(0, ROWS // 8, convert, 0)

    def layers(ref, first):
        def one(n, _):
            c, g = n // 3, n % 3

            def load(i):
                return ref[rows8(c * ROWS + i * PL + g * 8), :]

            out = (c + first) * FACES + g * 8
            lat_ref[rows8(out), :] = load(0)
            lat_ref[rows8(out + PL), :] = load(EDGE - 1)
            lat_ref[rows8(out + 2 * PL), :] = compact_j(load, 0)
            lat_ref[rows8(out + 3 * PL), :] = compact_j(load, 1)
            low_ref[rows8((c + first) * PL + g * 8), :] = compact_k(load, 0)
            high_ref[rows8((c + first) * PL + g * 8), :] = compact_k(load, 1)
            return 0

        lax.fori_loop(0, 15, one, 0)

    layers(prim_ref, 0)
    layers(adjl_ref, 5)


def reply_kernel(me_ref, asked_ref, lat_ref, out_ref):
    before = lax.broadcasted_iota(jnp.int32, (NB, NB), 0) < lax.broadcasted_iota(
        jnp.int32, (NB, NB), 1
    )
    before = jnp.where(before, 1.0, 0.0)
    earlier = jnp.zeros((PEERS, 1), jnp.float32)
    entries = []
    for f in range(4):
        asked = asked_ref[:, f, :]
        match = (asked >> 9) == me_ref[0]
        hits = jnp.where(match, 1.0, 0.0)
        rank = jnp.dot(hits, before, preferred_element_type=jnp.float32) + earlier
        earlier = earlier + jnp.sum(hits, axis=1, keepdims=True)
        face = (asked >> 3) & 63
        target = (((face & 3) * PL) + ((face >> 2) * 2)).astype(jnp.float32) + 10.0
        entries.append((match, rank, target))
    column = lax.broadcasted_iota(jnp.int32, (PEERS, FACES), 1).astype(jnp.float32)
    picks = []
    for s in range(2):
        row = jnp.full((PEERS, 1), -10.0, jnp.float32)
        for match, rank, target in entries:
            mine = match & (rank > s - 0.5) & (rank < s + 0.5)
            row = row + jnp.sum(jnp.where(mine, target, 0.0), axis=1, keepdims=True)
        for h in range(2):
            picks.append(jnp.where(column == row + float(h), 1.0, 0.0))
    picks = jnp.concatenate(picks, axis=0)
    for c in range(10):
        out = jnp.dot(
            picks,
            lat_ref[pl.ds(c * FACES, FACES), :],
            precision=lax.Precision.HIGHEST,
            preferred_element_type=jnp.float32,
        )
        for q in range(4):
            out_ref[pl.ds(c * 4 + q, PEERS, stride=40), :] = out[q * PEERS : (q + 1) * PEERS]


def one_hot(columns, width):
    parts = []
    for start in range(0, width, LANES):
        parts.append(
            jnp.where(
                columns == lax.broadcasted_iota(jnp.int32, columns.shape, 1) + start, 1.0, 0.0
            )
        )
    return parts[0] if len(parts) == 1 else jnp.concatenate(parts, axis=1)


def widened(x, index):
    parts = [
        jnp.take_along_axis(
            x[n : n + 8], index[n : n + 8], axis=1, mode="promise_in_bounds"
        )
        for n in range(0, x.shape[0], 8)
    ]
    return jnp.concatenate(parts, axis=0)


def fetched(columns, parts):
    y = jnp.dot(
        columns,
        jnp.concatenate(parts, axis=1),
        precision=lax.Precision.HIGHEST,
        preferred_element_type=jnp.float32,
    )
    return [y[:, n * LANES : (n + 1) * LANES] for n in range(len(parts))]


def minmod(a, c):
    return jnp.maximum(jnp.minimum(a, jnp.maximum(c, 0.0)), jnp.minimum(c, 0.0))


def masks():
    low, depth, even = lane() // EDGE, lane() % EDGE, even_row()
    return dict(
        k_last=depth == EDGE - 1,
        k_first=depth == 0,
        j_wrap=low == 7,
        j_back=low == 0,
        j_last=(low == 7) & ~even,
        j_first=(low == 0) & even,
        j_penult=(low == 6) & ~even,
    )


def next_k(x):
    return rolled(x, -1)


def last_k(x):
    return rolled(x, 1)


def next_j(x, m):
    r = rolled(x, -16)
    return jnp.where(m["j_wrap"], rolled(r, -1, 0), r)


def last_j(x, m):
    r = rolled(x, 16)
    return jnp.where(m["j_back"], rolled(r, 1, 0), r)


def slopes_of(below, x, above, gt, gk, m):
    x4 = 0.25 * x
    out = [minmod(0.25 * above - x4, x4 - 0.25 * below)]
    gt = x if gt is None else gt
    up = jnp.where(m["j_last"], gt, next_j(x, m))
    down = jnp.where(m["j_first"], gt, last_j(x, m))
    out.append(minmod(0.25 * up - x4, x4 - 0.25 * down))
    up = jnp.where(m["k_last"], gk, next_k(x))
    down = jnp.where(m["k_first"], gk, last_k(x))
    out.append(minmod(0.25 * up - x4, x4 - 0.25 * down))
    return out


def state(q):
    rho, u, v, w, p = q
    rs = lax.rsqrt(rho)
    enth = 7.0 * p * (rs * rs) + (u * u + v * v + w * w)
    return (rho, u, v, w, p, rho * rs, enth)


def four(base, first, second):
    out = []
    for a in (-1, 1):
        half = [x + s if a > 0 else x - s for x, s in zip(base, first)]
        for e in (-1, 1):
            out.append(state([x + s if e > 0 else x - s for x, s in zip(half, second)]))
    return out


def roe(left, right, axis):
    n = 1 + axis
    weight = right[5] * pl.reciprocal(left[5] + right[5], approx=True)
    jump = right[n] - left[n]
    mean = [None] * 4
    for c in (1, 2, 3):
        d = jump if c == n else right[c] - left[c]
        mean[c] = left[c] + weight * d
    enth = left[6] + weight * (right[6] - left[6])
    c2 = enth - (mean[1] * mean[1] + mean[2] * mean[2] + mean[3] * mean[3])
    rc = lax.rsqrt(c2)
    un = mean[n]
    ahead = un > 0.0
    sign = jnp.where(ahead, VEL, -VEL)
    b = jnp.maximum(START - jnp.abs(un) * rc, 0.0)
    s = jnp.minimum(b, KNEE)
    speed = 2.5 * b - s * (2.5 - (2.5 * CURVE) * s)
    wave = speed * ((right[4] - left[4]) * rc - sign * (left[5] * right[5] * jump))
    sc = sign * (c2 * rc)
    up = [jnp.where(ahead, left[c], right[c]) for c in (0, 1, 2, 3, 4, 6)]
    mass = up[0] * up[n]
    t = un * sc
    flux = [mass - wave]
    for c in (1, 2, 3):
        if c == n:
            flux.append((mass * up[c] + up[4]) - wave * (mean[c] - sc))
        else:
            flux.append(mass * up[c] - wave * mean[c])
    flux.append(mass * up[5] - wave * (enth - t - t))
    return flux


def face_sums(lefts, rights, axis):
    f = [roe(a, c, axis) for a, c in zip(lefts, rights)]
    plain, first, second = [], [], []
    for c in range(5):
        lo, hi = f[0][c] + f[1][c], f[2][c] + f[3][c]
        dlo, dhi = f[1][c] - f[0][c], f[3][c] - f[2][c]
        plain.append(lo + hi)
        first.append(hi - lo)
        second.append(dlo + dhi)
    return plain, first, second


def plain_sum(lefts, rights, axis):
    f = [roe(a, c, axis) for a, c in zip(lefts, rights)]
    return [(f[0][c] + f[1][c]) + (f[2][c] + f[3][c]) for c in range(5)]


def walled(sums, axis, solid_a, solid_b, wall_a, wall_b, gone=None):
    from_a = (solid_b > 0.5) & (solid_a < 0.5)
    from_b = (solid_a > 0.5) & (solid_b < 0.5)
    dead = from_a | from_b
    if gone is not None:
        dead = dead | gone
    out = []
    for part, pa, pb in zip(sums, wall_a, wall_b):
        new = []
        for c in range(5):
            if c == axis + 1:
                value = jnp.where(from_a, pa, jnp.where(from_b, pb, part[c]))
                new.append(value if gone is None else jnp.where(gone, 0.0, value))
            else:
                new.append(jnp.where(dead, 0.0, part[c]))
        out.append(new)
    return out


def wall_sums(p, normal, first, second):
    return (4.0 * (p + normal), 4.0 * first, 4.0 * second)


TANGENTS = ((1, 2), (0, 2), (0, 1))


class Moments:
    def __init__(self):
        self.value = [[None] * 5 for _ in range(4)]

    def add(self, k, part, sign):
        for c in range(5):
            old = self.value[k][c]
            if old is None:
                self.value[k][c] = part[c] if sign > 0 else -part[c]
            else:
                self.value[k][c] = old + part[c] if sign > 0 else old - part[c]

    def below(self, d, sums):
        self.add(0, sums[0], -1)
        self.add(d + 1, sums[0], 1)
        for t, part in zip(TANGENTS[d], sums[1:]):
            self.add(t + 1, part, -1)

    def above(self, d, sums):
        self.add(0, sums[0], 1)
        self.add(d + 1, sums[0], 1)
        for t, part in zip(TANGENTS[d], sums[1:]):
            self.add(t + 1, part, 1)

    def weighed(self, adj, slopes):
        total = None
        for c in range(5):
            part = adj[c] * self.value[0][c]
            for d in range(3):
                part = part + slopes[d][c] * self.value[d + 1][c]
            total = WEIGHTS[c] * part if total is None else total + WEIGHTS[c] * part
        return total


def weighed_sums(sums, normal, first, second):
    total = None
    for c in range(5):
        part = WEIGHTS[c] * (normal[c] * sums[0][c] + first[c] * sums[1][c] + second[c] * sums[2][c])
        total = part if total is None else total + part
    return total


def children(x, s):
    child = [
        four([a + b if up else a - b for a, b in zip(x, s[0])], s[1], s[2]) for up in (False, True)
    ]
    lower = [
        child[0],
        [child[0][0], child[0][1], child[1][0], child[1][1]],
        [child[0][0], child[0][2], child[1][0], child[1][2]],
    ]
    upper = [
        child[1],
        [child[0][2], child[0][3], child[1][2], child[1][3]],
        [child[0][1], child[0][3], child[1][1], child[1][3]],
    ]
    return lower, upper


def within(moments, lower, upper, axes):
    for d in range(3):
        inner = plain_sum(lower[d], upper[d], axes[d])
        moments.add(d + 1, [y + y for y in inner], -1)


def along(moments, d, axis, lower, upper, x, s, solid, ahead, back, gone):
    sums = face_sums(upper[d], [tuple(ahead(y) for y in st) for st in lower[d]], axis)
    t0, t1 = TANGENTS[d]
    wall_a = wall_sums(x[4], s[d][4], s[t0][4], s[t1][4])
    wall_b = [ahead(y) for y in wall_sums(x[4], -s[d][4], s[t0][4], s[t1][4])]
    sums = walled(sums, axis, solid, ahead(solid), wall_a, wall_b, gone)
    moments.above(d, sums)
    moments.below(d, [[back(y) for y in part] for part in sums])


def ends(moments, d, axis, x, s, ghost, first, last):
    n = axis + 1
    flip = jnp.where(first, -1.0, 1.0)
    base = [a + flip * b for a, b in zip(x, s[d])]
    t0, t1 = TANGENTS[d]
    f0, f1, g = list(s[t0]), list(s[t1]), list(ghost)
    for part in (base, f0, f1, g):
        part[n] = flip * part[n]
    sums = face_sums(four(base, f0, f1), [state(g)] * 4, axis)
    shown = first | last
    sums = [
        [jnp.where(shown, flip * y if c == n else y, 0.0) for c, y in enumerate(part)] for part in sums
    ]
    moments.add(0, sums[0], 1)
    moments.add(d + 1, [flip * y for y in sums[0]], 1)
    moments.add(t0 + 1, sums[1], 1)
    moments.add(t1 + 1, sums[2], 1)


def inner_kernel(
    edge_ref, index_ref, prim_ref, adj_ref, solid_ref, low_ref, high_ref,
    acc_ref, px_ref, pg_ref, ps_ref,
    v_ref, gk_ref, pv_ref, aw_ref,
):
    for side in range(2):
        ref = (low_ref, high_ref)[side]
        columns = one_hot(index_ref[pl.ds(240 + side * PL, PL), :], LANES)[:, :PL]
        parts = fetched(columns, [ref[pl.ds(c * PL, PL), :] for c in range(10)])
        for c in range(10):
            y = widened(parts[c], index_ref[pl.ds(FACES + side * PL, PL), :])
            far = FARFIELD[c] if c < 5 else 0.0
            v_ref[pl.ds((side * 10 + c) * PL, PL), :] = jnp.where(
                edge_ref[side] == 1, jnp.full_like(y, far), y
            )

    def spread(n, _):
        c, g = n // 3, n % 3
        low, high = (v_ref[rows8((side * 10 + c) * PL + g * 8), :] for side in range(2))
        for i in range(EDGE):
            gk_ref[rows8(c * ROWS + i * PL + g * 8), :] = spread_k(low, high, i)
        return 0

    lax.fori_loop(0, 30, spread, 0)

    def packed(load, out_ref, depth, first, step, g):
        planes = [[load(n) for n in range(depth)], [load(EDGE - 1 - n) for n in range(depth)]]
        for n, sides in enumerate((planes, compact_depths(load, depth))):
            for side in range(2):
                for at in range(depth):
                    row = (((n * 2 + side) * depth + at) * step + first) * PL + g * 8
                    out_ref[rows8(row), :] = sides[side][at]

    def pack(n, _):
        c, g = n // 3, n % 3

        def load_of(ref, first):
            return lambda i: ref[rows8((c + first) * ROWS + i * PL + g * 8), :]

        packed(load_of(prim_ref, 0), px_ref, 3, c, 10, g)
        packed(load_of(adj_ref, 0), px_ref, 3, c + 5, 10, g)
        packed(load_of(gk_ref, 0), pg_ref, 2, c, 10, g)
        packed(load_of(gk_ref, 5), pg_ref, 2, c + 5, 10, g)
        return 0

    lax.fori_loop(0, 15, pack, 0)
    for g in range(3):
        packed(lambda i: solid_ref[pl.ds(i * PL + g * 8, 8), :], ps_ref, 2, 0, 1, g)

    m = masks()
    inside = ~(m["j_first"] | m["j_last"])
    gone_j = m["j_first"] | m["j_last"] | m["j_penult"]
    for i in (0, EDGE - 1):
        acc_ref[pl.ds(i * PL, PL), :] = jnp.zeros((PL, LANES), jnp.float32)

    def column(g, _):
        g8 = g * 8
        start = state([jnp.full((8, LANES), y, jnp.float32) for y in (1.0, 0.0, 0.0, 0.0, 0.2)])
        for n in range(4):
            for q in range(7):
                pv_ref[pl.ds((n * 7 + q) * 8, 8), :] = start[q]
        aw_ref[...] = jnp.zeros_like(aw_ref)

        def plane(i, _):
            row = i * PL + g8

            def around(ref, c, first):
                at = c * ROWS + row
                return slopes_of(
                    ref[rows8(at - PL), :],
                    ref[rows8(at), :],
                    ref[rows8(at + PL), :],
                    None,
                    gk_ref[rows8((c + first) * ROWS + row), :],
                    m,
                )

            x = [prim_ref[rows8(c * ROWS + row), :] for c in range(5)]
            s = list(zip(*[around(prim_ref, c, 0) for c in range(5)]))
            ghost = [gk_ref[rows8(c * ROWS + row), :] for c in range(5)]
            solid = solid_ref[rows8(row), :]
            lower, upper = children(x, s)
            moments = Moments()
            within(moments, lower, upper, (0, 1, 2))

            before = [
                tuple(pv_ref[pl.ds((n * 7 + q) * 8, 8), :] for q in range(7)) for n in range(4)
            ]
            prior = row - PL
            wall_a = [pv_ref[pl.ds((28 + q) * 8, 8), :] for q in range(3)]
            wall_b = wall_sums(x[4], -s[0][4], s[1][4], s[2][4])
            sums = face_sums(before, lower[0], 0)
            sums = walled(sums, 0, solid_ref[rows8(prior), :], solid, wall_a, wall_b)
            used = jnp.where(i > 1, 1.0, 0.0)
            sums = [[used * y for y in part] for part in sums]
            moments.below(0, sums)
            old = [[aw_ref[pl.ds((q * 5 + c) * 8, 8), :] for c in range(5)] for q in range(3)]
            acc_ref[rows8(prior), :] = acc_ref[rows8(prior), :] + jnp.where(
                inside, weighed_sums(sums, *old), 0.0
            )
            for n in range(4):
                for q in range(7):
                    pv_ref[pl.ds((n * 7 + q) * 8, 8), :] = upper[0][n][q]
            for q, y in enumerate(wall_sums(x[4], s[0][4], s[1][4], s[2][4])):
                pv_ref[pl.ds((28 + q) * 8, 8), :] = y

            along(
                moments, 1, 1, lower, upper, x, s, solid,
                lambda y: next_j(y, m), lambda y: last_j(y, m), gone_j,
            )
            along(moments, 2, 2, lower, upper, x, s, solid, next_k, last_k, m["k_last"])
            ends(moments, 2, 2, x, s, ghost, m["k_first"], m["k_last"])

            a = [adj_ref[rows8(c * ROWS + row), :] for c in range(5)]
            t = list(zip(*[around(adj_ref, c, 5) for c in range(5)]))
            acc_ref[rows8(row), :] = jnp.where(inside, moments.weighed(a, t), 0.0)
            for c in range(5):
                aw_ref[pl.ds(c * 8, 8), :] = a[c] + t[0][c]
                aw_ref[pl.ds((5 + c) * 8, 8), :] = t[1][c]
                aw_ref[pl.ds((10 + c) * 8, 8), :] = t[2][c]
            return 0

        for q in range(3):
            pv_ref[pl.ds((28 + q) * 8, 8), :] = jnp.zeros((8, LANES), jnp.float32)
        lax.fori_loop(1, EDGE - 1, plane, 0)
        return 0

    lax.fori_loop(0, 3, column, 0)


def rim_kernel(
    index_ref, got_ref, px_ref, pg_ref, ps_ref, solid_ref, acc_ref, out_ref,
    gl_ref, tg_ref, pm_ref, total_ref,
):
    columns = one_hot(index_ref[pl.ds(144, FACES), :], 4 * PEERS)
    parts = fetched(
        columns,
        [
            jnp.concatenate(
                [got_ref[pl.ds(c * 4 + q, PEERS, stride=40), :] for q in range(4)], axis=0
            )
            for c in range(10)
        ],
    )
    for c in range(10):
        y = widened(parts[c], index_ref[pl.ds(0, FACES), :])
        for f in range(4):
            gl_ref[pl.ds((f * 10 + c) * PL, PL), :] = y[f * PL : (f + 1) * PL]

    def side_ghosts(n, _):
        c, g = n // 3, n % 3
        low, high = (gl_ref[rows8((f * 10 + c) * PL + g * 8), :] for f in (2, 3))
        for at, i in enumerate((0, 1, EDGE - 1, EDGE - 2)):
            tg_ref[rows8((at * 10 + c) * PL + g * 8), :] = spread_j(low, high, i)
        return 0

    lax.fori_loop(0, 30, side_ghosts, 0)
    m = masks()

    def boundary(n):
        axes = (n, 1 - n, 2)

        def one(at, _):
            side, g8 = at // 3, at % 3 * 8
            flip = jnp.where(side == 0, 1.0, -1.0)

            def load(ref, first):
                out = []
                for c in range(10):
                    y = ref[rows8((first + c) * PL + g8), :]
                    out.append(flip * y if c % 5 == n + 1 else y)
                return out

            place = n * 2 + side
            x = [load(px_ref, (place * 3 + depth) * 10) for depth in range(3)]
            outer = load(gl_ref, place * 10)
            gk = [load(pg_ref, (place * 2 + depth) * 10) for depth in range(2)]
            if n == 0:
                gt = [load(tg_ref, (side * 2 + depth) * 10) for depth in range(2)]
            else:
                gt = [[None] * 10] * 2
            solid = [ps_ref[rows8((place * 2 + depth) * PL + g8), :] for depth in range(2)]
            s0 = list(
                zip(*[slopes_of(outer[c], x[0][c], x[1][c], gt[0][c], gk[0][c], m) for c in range(10)])
            )
            s1 = list(
                zip(*[slopes_of(x[0][c], x[1][c], x[2][c], gt[1][c], gk[1][c], m) for c in range(10)])
            )
            flow, adj = x[0][:5], x[0][5:]
            s, t = [y[:5] for y in s0], [y[5:] for y in s0]
            lower, upper = children(flow, s)
            moments = Moments()
            within(moments, lower, upper, axes)
            moments.below(0, face_sums([state(outer[:5])] * 4, lower[0], n))

            flow1, adj1 = x[1][:5], x[1][5:]
            f1, t1 = [y[:5] for y in s1], [y[5:] for y in s1]
            sums = face_sums(
                upper[0], four([a - b for a, b in zip(flow1, f1[0])], f1[1], f1[2]), n
            )
            sums = walled(
                sums,
                n,
                solid[0],
                solid[1],
                wall_sums(flow[4], s[0][4], s[1][4], s[2][4]),
                wall_sums(flow1[4], -f1[0][4], f1[1][4], f1[2][4]),
            )
            moments.above(0, sums)
            next_total = -weighed_sums(
                sums, [a - b for a, b in zip(adj1, t1[0])], t1[1], t1[2]
            )

            gone = m["j_last"]
            if n == 1:
                gone = gone | m["j_first"] | m["j_penult"]
            along(
                moments, 1, axes[1], lower, upper, flow, s, solid[0],
                lambda y: next_j(y, m), lambda y: last_j(y, m), gone,
            )
            if n == 0:
                ends(moments, 1, axes[1], flow, s, gt[0][:5], m["j_first"], m["j_last"])
            along(moments, 2, 2, lower, upper, flow, s, solid[0], next_k, last_k, m["k_last"])
            ends(moments, 2, 2, flow, s, gk[0][:5], m["k_first"], m["k_last"])
            total = moments.weighed(adj, t)
            if n == 1:
                kept = ~(m["j_first"] | m["j_last"])
                total = jnp.where(kept, total, 0.0)
                next_total = jnp.where(kept, next_total, 0.0)
            pm_ref[rows8(place * 2 * PL + g8), :] = total
            pm_ref[rows8((place * 2 + 1) * PL + g8), :] = next_total
            return 0

        lax.fori_loop(0, 6, one, 0)

    boundary(0)
    boundary(1)

    low, even = lane() // EDGE, even_row()
    for g in range(3):
        planes = [[pm_ref[pl.ds((p * 2 + d) * PL + g * 8, 8), :] for d in range(2)] for p in range(4)]
        near = [planes[2], [rolled(y, -1, 0) for y in planes[2]]]
        far = [[rolled(y, 1, 0) for y in planes[3]], planes[3]]
        for i in range(EDGE):
            ih, il = i // 8, i % 8
            a, c = near[ih], far[ih]
            extra = jnp.where(
                even,
                jnp.where(
                    low == 0,
                    rolled(a[0], -16 * il),
                    jnp.where(low == 1, rolled(a[1], 16 - 16 * il), 0.0),
                ),
                jnp.where(
                    low == 7,
                    rolled(c[0], 112 - 16 * il),
                    jnp.where(low == 6, rolled(c[1], 96 - 16 * il), 0.0),
                ),
            )
            at = pl.ds(i * PL + g * 8, 8)
            total = acc_ref[at, :] + extra
            if i < 2:
                total = total + planes[0][i]
            elif i > EDGE - 3:
                total = total + planes[1][EDGE - 1 - i]
            total_ref[at, :] = jnp.where(solid_ref[at, :] > 0.5, 0.0, jnp.abs(total))
    for t in range(2 * EDGE):
        i, jh = divmod(t, 2)
        out_ref[:, pl.ds(t * LANES, LANES)] = total_ref[pl.ds(i * PL + jh, NB, stride=2), :]


def shape(*dims):
    return jax.ShapeDtypeStruct(dims, jnp.float32)


def scratch(*rows):
    return [pltpu.VMEM((r, LANES), jnp.float32) for r in rows]


SMEM = pl.BlockSpec(memory_space=pltpu.SMEM)
VMEM = pl.BlockSpec(memory_space=pltpu.VMEM)
PARAMS = pltpu.CompilerParams(vmem_limit_bytes=VMEM_LIMIT)


def prep(flow, adjoint, cut_flag, own, vertical):
    return pl.pallas_call(
        prep_kernel,
        out_shape=[
            shape(5 * ROWS, LANES),
            shape(5 * ROWS, LANES),
            shape(ROWS, LANES),
            shape(10 * FACES, LANES),
            shape(10 * PL, LANES),
            shape(10 * PL, LANES),
            jax.ShapeDtypeStruct((288, LANES), jnp.int32),
        ],
        in_specs=[VMEM] * 5,
        out_specs=[VMEM] * 7,
        cost_estimate=pl.CostEstimate(flops=10**8, bytes_accessed=3 * 10**7, transcendentals=0),
        compiler_params=PARAMS,
    )(flow.transpose(1, 0, 2), adjoint.transpose(1, 0, 2), cut_flag[None], own, vertical)


def reply(me, asked, layers):
    return pl.pallas_call(
        reply_kernel,
        out_shape=shape(40 * PEERS, LANES),
        in_specs=[SMEM, VMEM, VMEM],
        out_specs=VMEM,
        compiler_params=PARAMS,
    )(me, asked, layers)


def inner(edge, index, prim, adj, solid, low, high):
    return pl.pallas_call(
        inner_kernel,
        out_shape=[
            shape(ROWS, LANES), shape(120 * PL, LANES), shape(80 * PL, LANES), shape(8 * PL, LANES)
        ],
        in_specs=[SMEM] + [VMEM] * 6,
        out_specs=[VMEM] * 4,
        scratch_shapes=scratch(20 * PL, 10 * ROWS, 31 * 8, 15 * 8),
        compiler_params=PARAMS,
    )(edge, index, prim, adj, solid, low, high)


def rim(index, got, planes, ghosts, walls, solid, acc):
    return pl.pallas_call(
        rim_kernel,
        out_shape=shape(NB, EDGE * EDGE * EDGE),
        in_specs=[VMEM] * 7,
        out_specs=VMEM,
        scratch_shapes=scratch(40 * PL, 40 * PL, 8 * PL, ROWS),
        compiler_params=PARAMS,
    )(index, got, planes, ghosts, walls, solid, acc)


def packed_requests(lateral_owner, lateral_link, vertical_link):
    link = lateral_link.T
    far = lax.broadcasted_iota(jnp.int32, link.shape, 0) ^ 1
    own = (lateral_owner[:, :, 0].T * 64 + link // 5 * 4 + far) * 8 + link % 5
    return own, vertical_link.T // 5 * 8 + vertical_link.T % 5


def exchange(block, axis):
    chunks = block.reshape(PEERS, -1, LANES)
    out = lax.all_to_all(chunks, axis, split_axis=0, concat_axis=0, tiled=True)
    return out.reshape(-1, LANES)


def local(flow, adjoint, cut_flag, lateral_owner, lateral_link, vertical_link):
    own, vertical = packed_requests(lateral_owner, lateral_link, vertical_link)
    asked = lax.all_to_all(
        jnp.broadcast_to(own, (PEERS,) + own.shape), "blk", split_axis=0, concat_axis=0, tiled=True
    )
    prim, adj, solid, layers, low_face, high_face, index = prep(
        flow, adjoint, cut_flag, own, vertical
    )
    asked, low_face, high_face = lax.optimization_barrier((asked, low_face, high_face))
    regions = lax.axis_size("grp")
    region = lax.axis_index("grp")
    low = lax.ppermute(high_face, "grp", [(r, r + 1) for r in range(regions - 1)])
    high = lax.ppermute(low_face, "grp", [(r + 1, r) for r in range(regions - 1)])
    me = lax.axis_index("blk").astype(jnp.int32).reshape(1)
    replies = reply(me, asked, layers)
    replies, low, high = lax.optimization_barrier((replies, low, high))
    got = exchange(replies, "blk")
    edge = jnp.stack([region == 0, region == regions - 1]).astype(jnp.int32)
    acc, planes, ghosts, walls = inner(edge, index, prim, adj, solid, low, high)
    return rim(index, got, planes, ghosts, walls, solid, acc)


def solution(mesh):
    in_specs = (
        P(("blk", "grp"), None, None),
        P(("blk", "grp"), None, None),
        P(("blk", "grp"), None),
        P(("blk", "grp"), None, None),
        P(("blk", "grp"), None),
        P(("blk", "grp"), None),
    )
    out_specs = P(("blk", "grp"), None)
    return jax.shard_map(local, mesh=mesh, in_specs=in_specs, out_specs=out_specs, check_vma=False)
```

time: 138 us -> 96 us (0.70)
  blocking collectives: 28.2 us -> 0 us
  Pallas kernels: 67.6 us -> 59.4 us
  waiting for transfers between devices: 11.1 us -> 2.97 us
  starting transfers between devices: 23.9 us -> 27.5 us
    all_to_all x1 -> x0, blocking collectives: 28.2 us -> none  [exchange(): out = lax.all_to_all(chunks, axis, split_axis=0, concat_axis=0, tiled=True)]
    all_to_all x1, waiting for transfers between devices: 11.1 us -> 1.46 us  [local(): lax.all_to_all(jnp.broadcast_to(own, (PEERS,) + own.shape), 'blk', split_...]
    pallas_call x3, Pallas kernels: 59.1 us -> 50.9 us  [the longest x1 32.1 us: inner(): pl.pallas_call(inner_kernel, out_shape=[shape(ROWS, LANES), shape(120 * P...]
    all_to_all x1, starting transfers between devices: 6.11 us -> 10 us  [exchange(): out = lax.all_to_all(chunks, axis, split_axis=0, concat_axis=0, tiled=True)]
  transfers between devices with their start and end apart: 4 -> 4, of which waited for: 1 -> 3; matrix products, arithmetic and copies ran while one was open for 1% -> 2% of each run, Pallas kernels for 35% -> 47%
where the time goes in v3:
time: 96 us; the launch traced here: 95.6 us
  Pallas kernels  59.4 us (62%)
  starting transfers between devices  27.5 us (29%)
  other arithmetic  3.29 us (3%)
  waiting for transfers between devices  2.97 us (3%)
  local copies, waits for them, and re-layouts  2.38 us (2%)
    pallas_call x1, Pallas kernels, inner(): pl.pallas_call(inner_kernel, out_shape=[shape(ROWS, LANES), shape(120 * P...  32.1 us
    pallas_call x1, Pallas kernels, rim(): pl.pallas_call(rim_kernel, out_shape=shape(NB, EDGE * EDGE * EDGE), in_sp...  14.5 us
    all_to_all x1, starting transfers between devices, local(): lax.all_to_all(jnp.broadcast_to(own, (PEERS,) + own.shape), 'blk', split_...  13 us
    all_to_all x1, starting transfers between devices, exchange(): out = lax.all_to_all(chunks, axis, split_axis=0, concat_axis=0, tiled=True)  10 us
    pallas_call x1, Pallas kernels, prep(): pl.pallas_call(prep_kernel, out_shape=[shape(5 * ROWS, LANES), shape(5 *...  8.44 us
    pallas_call x1, Pallas kernels, reply(): pl.pallas_call(reply_kernel, out_shape=shape(40 * PEERS, LANES), in_specs...  4.31 us
    ppermute x1, starting transfers between devices, local(): lax.ppermute(high_face, 'grp', [(r, r + 1) for r in range(regions - 1)])  3.2 us
  transfers between devices with their start and end apart: 4, of which 3 were waited for; matrix products, arithmetic and copies ran while one was open for 2% of the time, Pallas kernels for 47%

profile of v3, /device:TPU:1, one launch (start us, length us, event | category | flops | bytes accessed | tf_op | source)
XLA Modules:
  0.0 95.6 jit_solution(11920682368650630336)
XLA Ops:
  0.0 0.7 broadcast_multiply_fusion
  0.7 0.8 fusion.4.own_ref
  1.4 0.0 copy-start.4
  1.4 0.7 broadcast_in_dim.7
  2.1 13.0 %all-to-all-start = ((s32[64,4,12]{2,1,0:T(4,128)}), s32[64,4,12]{2,1,0:T(4,128)S(1)}, u32[]{:S(2)}, u32[]{:S(2)}) async-start(s32[64,4,12]{2,1,0:T(4,128)} %broadcast_in_dim.7), calls=%async_computation | async-start | bytes 262144 | tf_op jit(solution)/shard_map/all_to_all | solution.py:847
  15.1 1.2 %fusion.9.vertical_ref = s32[2,12]{1,0:T(2,128)} fusion(s32[12,2]{0,1:T(2,128)} %param.11), kind=kLoop, calls=%fused_computation.17 | loop fusion | flops 336 | bytes 192 | tf_op jit(solution)/shard_map/add | solution.py:836
  16.3 0.0 copy-done.4
  16.3 8.4 %shard_map.64 = (f32[1920,128]{1,0:T(8,128)}, f32[1920,128]{1,0:T(8,128)}, f32[384,128]{1,0:T(8,128)}, f32[960,128]{1,0:T(8,128)}, f32[240,128]{1,0:T(8,128)}, /*index=5*/f32[240,128]{1,0:T(8,128)}, s32[288,128]{1,0:T(8,128)}) custom-call(f32[5,12,4096]{2,1,0:T(8,128)} %bitcast.43, f32[5,12,4096]{2,1,0:T(8,128)} %bitcast.44, s32[1,12,4096]{2,1,0:T(8,128)} %bitcast.45, ...), custom_call_target="tpu_custom_call" | custom-call | flops 100000000 | bytes 30000000 | tf_op jit(solution)/shard_map/pallas_call | solution.py:780
  24.8 1.5 %all-to-all-done.asked_ref = s32[64,4,12]{2,1,0:T(4,128)S(1)} async-done(((s32[64,4,12]{2,1,0:T(4,128)}), s32[64,4,12]{2,1,0:T(4,128)S(1)}, u32[]{:S(2)}, u32[]{:S(2)}) %all-to-all-start) | async-done | bytes 12320 | tf_op jit(solution)/shard_map/all_to_all | solution.py:847
  26.2 0.0 copy-start.1
  26.2 3.2 %collective-permute-start = (f32[240,128]{1,0:T(8,128)}, f32[240,128]{1,0:T(8,128)S(1)}, u32[]{:S(2)}, u32[]{:S(2)}) collective-permute-start(f32[240,128]{1,0:T(8,128)} %get-tuple-element.27), channel_id=1, source_target_pairs={{0,1},{1,2},{2,3},{4,5},{5,6},{6,7},{8,9},{9,10},{10,11},{12,13},{... | collective-permute-start | bytes 368648 | tf_op jit(solution)/shard_map/ppermute | solution.py:856
  29.4 1.3 %collective-permute-start.1 = (f32[240,128]{1,0:T(8,128)}, f32[240,128]{1,0:T(8,128)S(1)}, u32[]{:S(2)}, u32[]{:S(2)}) collective-permute-start(f32[240,128]{1,0:T(8,128)} %get-tuple-element.28), channel_id=1, source_target_pairs={{1,0},{2,1},{3,2},{5,4},{6,5},{7,6},{9,8},{10,9},{11,10},{13,12},{... | collective-permute-start | bytes 368648 | tf_op jit(solution)/shard_map/ppermute | solution.py:857
  30.7 0.0 copy-done.1
  30.7 4.3 %shard_map.65 = f32[2560,128]{1,0:T(8,128)} custom-call(s32[1]{0:T(128)} %bitcast.11.me_ref, s32[64,4,12]{2,1,0:T(4,128)} %copy-done.1, f32[960,128]{1,0:T(8,128)} %get-tuple-element.26.lat_ref), custom_call_target="tpu_custom_call" | custom-call | tf_op jit(solution)/shard_map/pallas_call | solution.py:799
  35.1 0.0 collective-permute-done.low_ref
  35.1 0.7 collective-permute-done.1.high_ref
  35.7 0.0 copy-done.2
  35.7 0.6 copy-done.3
  36.4 10.0 %all-to-all-start.1 = ((f32[64,40,128]{2,1,0:T(8,128)}), f32[64,40,128]{2,1,0:T(8,128)S(1)}, u32[]{:S(2)}, u32[]{:S(2)}) async-start(f32[64,40,128]{2,1,0:T(8,128)} %bitcast.41), calls=%async_computation.1 | async-start | bytes 2621440 | tf_op jit(solution)/shard_map/all_to_all | solution.py:841
  46.4 0.6 add_convert_fusion.edge_ref
  47.1 32.1 %shard_map.66 = (f32[384,128]{1,0:T(8,128)}, f32[2880,128]{1,0:T(8,128)}, f32[1920,128]{1,0:T(8,128)}, f32[192,128]{1,0:T(8,128)}) custom-call(s32[2]{0:T(128)} %add_convert_fusion.edge_ref, s32[288,128]{1,0:T(8,128)} %get-tuple-element.22.index_ref, f32[1920,128]{1,0:T(8,128)} %get-tuple-element.30.prim_ref, f32[1920,128]{1,0:T(8,128)} %get-tuple-element.31.adj_ref, ...), custom_call_target="tpu_custom_call" | custom-call | tf_op jit(solution)/shard_map/pallas_call | solution.py:809
  79.2 0.8 all-to-all-done.1
  80.0 1.1 %copy-done = f32[64,40,128]{2,1,0:T(8,128)} copy-done((f32[64,40,128]{2,1,0:T(8,128)}, f32[64,40,128]{2,1,0:T(8,128)S(1)}, u32[]{:S(2)}) %copy-start) | copy-done | bytes 1310744
  81.1 14.5 %shard_map.67 = f32[12,4096]{1,0:T(8,128)} custom-call(s32[288,128]{1,0:T(8,128)} %get-tuple-element.22.index_ref, f32[2560,128]{1,0:T(8,128)} %bitcast.42, f32[2880,128]{1,0:T(8,128)} %get-tuple-element.35.px_ref, f32[1920,128]{1,0:T(8,128)} %get-tuple-element.36.pg_ref, f32[192,128]{1,0:T(8,128)} %get-tuple-element.37.ps_ref, ...), custom_call_target="tpu_custom_call" | custom-call | tf_op jit(solution)/shard_map/pallas_call | solution.py:822
  (4 shorter events, 0.0 us)
Async XLA Ops:
  1.4 14.9 %copy-start.4 = (s32[4,12]{1,0:T(4,128)}, s32[4,12]{1,0:T(4,128)S(1)}, u32[]{:S(2)}) copy-start(s32[4,12]{1,0:T(4,128)S(1)} %fusion.4.own_ref) | copy-start | bytes 580
  2.1 24.1 %all-to-all-start = ((s32[64,4,12]{2,1,0:T(4,128)}), s32[64,4,12]{2,1,0:T(4,128)S(1)}, u32[]{:S(2)}, u32[]{:S(2)}) async-start(s32[64,4,12]{2,1,0:T(4,128)} %broadcast_in_dim.7), calls=%async_computation | async-start | bytes 262144 | tf_op jit(solution)/shard_map/all_to_all | solution.py:847
  26.2 4.5 %copy-start.1 = (s32[64,4,12]{2,1,0:T(4,128)}, s32[64,4,12]{2,1,0:T(4,128)S(1)}, u32[]{:S(2)}) copy-start(s32[64,4,12]{2,1,0:T(4,128)S(1)} %all-to-all-done.asked_ref) | copy-start | bytes 36868
  26.2 8.8 %collective-permute-start = (f32[240,128]{1,0:T(8,128)}, f32[240,128]{1,0:T(8,128)S(1)}, u32[]{:S(2)}, u32[]{:S(2)}) collective-permute-start(f32[240,128]{1,0:T(8,128)} %get-tuple-element.27), channel_id=1, source_target_pairs={{0,1},{1,2},{2,3},{4,5},{5,6},{6,7},{8,9},{9,10},{10,11},{12,13},{... | collective-permute-start | bytes 368648 | tf_op jit(solution)/shard_map/ppermute | solution.py:856
  29.4 6.3 %collective-permute-start.1 = (f32[240,128]{1,0:T(8,128)}, f32[240,128]{1,0:T(8,128)S(1)}, u32[]{:S(2)}, u32[]{:S(2)}) collective-permute-start(f32[240,128]{1,0:T(8,128)} %get-tuple-element.28), channel_id=1, source_target_pairs={{1,0},{2,1},{3,2},{5,4},{6,5},{7,6},{9,8},{10,9},{11,10},{13,12},{... | collective-permute-start | bytes 368648 | tf_op jit(solution)/shard_map/ppermute | solution.py:857
  35.1 0.7 copy-start.2
  35.7 0.6 copy-start.3
  36.4 43.6 %all-to-all-start.1 = ((f32[64,40,128]{2,1,0:T(8,128)}), f32[64,40,128]{2,1,0:T(8,128)S(1)}, u32[]{:S(2)}, u32[]{:S(2)}) async-start(f32[64,40,128]{2,1,0:T(8,128)} %bitcast.41), calls=%async_computation.1 | async-start | bytes 2621440 | tf_op jit(solution)/shard_map/all_to_all | solution.py:841
  80.0 1.1 %copy-start = (f32[64,40,128]{2,1,0:T(8,128)}, f32[64,40,128]{2,1,0:T(8,128)S(1)}, u32[]{:S(2)}) copy-start(f32[64,40,128]{2,1,0:T(8,128)S(1)} %all-to-all-done.1) | copy-start | bytes 3932164

commit v4 on v3

--- a/solution.py
+++ b/solution.py
@@ -25,7 +25,7 @@
 START = 1.2 / math.sqrt(5.0)
 CURVE = 1.25 * math.sqrt(5.0)
 
-VMEM_LIMIT = 56 * 2**20
+VMEM_LIMIT = 24 * 2**20
 
 
 def lane():
@@ -48,27 +48,14 @@
     return pl.ds(pl.multiple_of(start, 8), 8)
 
 
-def compact_j(load, side):
-    low = lane() // EDGE
-    halves = []
-    for ih in range(2):
-        total = None
-        for il in range(8):
-            x = rolled(load(ih * 8 + il), 16 * il if side == 0 else 16 * il + 16)
-            total = x if total is None else jnp.where(low == il, x, total)
-        halves.append(total)
-    if side == 0:
-        return jnp.where(even_row(), halves[0], rolled(halves[1], 1, 0))
-    return jnp.where(even_row(), rolled(halves[0], -1, 0), halves[1])
-
-
-def compact_k(load, side):
+def compact_k(load):
     depth = lane() % EDGE
-    total = None
+    low = high = None
     for i in range(EDGE):
-        x = rolled(load(i), i if side == 0 else i - 15)
-        total = x if total is None else jnp.where(depth == i, x, total)
-    return total
+        x = rolled(load(i), i)
+        low = x if low is None else jnp.where(depth == i, x, low)
+        high = x if high is None else jnp.where(depth == (i + 15) % EDGE, x, high)
+    return low, rolled(high, -15)
 
 
 def compact_depths(load, count):
@@ -82,11 +69,12 @@
             for n, spot in enumerate(spots):
                 t = totals[n]
                 totals[n] = x if t is None else jnp.where(low == (spot + il) % 8, x, t)
-        halves.append([rolled(t, -16 * spot) for t, spot in zip(totals, spots)])
+        halves.append(totals)
     even = even_row()
     near = [jnp.where(even, a, rolled(c, 1, 0)) for a, c in zip(halves[0][:count], halves[1][:count])]
     far = [jnp.where(even, rolled(a, -1, 0), c) for a, c in zip(halves[0][count:], halves[1][count:])]
-    return near, far
+    out = [rolled(t, -16 * spot) for t, spot in zip(near + far, spots)]
+    return out[:count], out[count:]
 
 
 def spread_j(low, high, i):
@@ -134,7 +122,8 @@
         store(f, code, code >> 1, code & 1, rank * 2 * PEERS + owner, PEERS)
     for side in range(2):
         value = column_of(vertical[side : side + 1, :], PL, NB).astype(jnp.int32)
-        slot, code = value >> 3, value & 7
+        slot = (value.astype(jnp.float32) * 0.2 + 0.05).astype(jnp.int32)
+        code = value - 5 * slot
         store(4 + side, code, code & 1, code >> 1, slot * 2, 1)
 
 
@@ -153,11 +142,11 @@
         relaid(adj_ref, c, adjl_ref)
     relaid(flag_ref, 0, solid_ref)
     index_tables(
-        own_ref[...].astype(jnp.float32), vertical_ref[...].astype(jnp.float32), index_ref
+        own_ref[0].astype(jnp.float32), vertical_ref[...].astype(jnp.float32), index_ref
     )
 
     def convert(n, _):
-        at = [rows8(c * ROWS + n * 8) for c in range(5)]
+        at = [pl.ds(pl.multiple_of(c * ROWS + n * 64, 64), 64) for c in range(5)]
         rho = prim_ref[at[0]]
         inv = 1.0 / rho
         vel = [prim_ref[at[c]] * inv for c in (1, 2, 3)]
@@ -167,25 +156,27 @@
             prim_ref[at[c + 1]] = vel[c] * VEL
         return 0
 
-    lax.fori_loop(0, ROWS // 8, convert, 0)
+    lax.fori_loop(0, ROWS // 64, convert, 0)
 
     def layers(ref, first):
-        def one(n, _):
-            c, g = n // 3, n % 3
-
-            def load(i):
-                return ref[rows8(c * ROWS + i * PL + g * 8), :]
-
-            out = (c + first) * FACES + g * 8
-            lat_ref[rows8(out), :] = load(0)
-            lat_ref[rows8(out + PL), :] = load(EDGE - 1)
-            lat_ref[rows8(out + 2 * PL), :] = compact_j(load, 0)
-            lat_ref[rows8(out + 3 * PL), :] = compact_j(load, 1)
-            low_ref[rows8((c + first) * PL + g * 8), :] = compact_k(load, 0)
-            high_ref[rows8((c + first) * PL + g * 8), :] = compact_k(load, 1)
+        def one(c, _):
+            for g in range(3):
+
+                def load(i):
+                    return ref[rows8(c * ROWS + i * PL + g * 8), :]
+
+                out = (c + first) * FACES + g * 8
+                lat_ref[rows8(out), :] = load(0)
+                lat_ref[rows8(out + PL), :] = load(EDGE - 1)
+                near, far = compact_depths(load, 1)
+                lat_ref[rows8(out + 2 * PL), :] = near[0]
+                lat_ref[rows8(out + 3 * PL), :] = far[0]
+                low, high = compact_k(load)
+                low_ref[rows8((c + first) * PL + g * 8), :] = low
+                high_ref[rows8((c + first) * PL + g * 8), :] = high
             return 0
 
-        lax.fori_loop(0, 15, one, 0)
+        lax.fori_loop(0, 5, one, 0)
 
     layers(prim_ref, 0)
     layers(adjl_ref, 5)
@@ -295,15 +286,14 @@
 
 
 def slopes_of(below, x, above, gt, gk, m):
-    x4 = 0.25 * x
-    out = [minmod(0.25 * above - x4, x4 - 0.25 * below)]
+    out = [0.25 * minmod(above - x, x - below)]
     gt = x if gt is None else gt
     up = jnp.where(m["j_last"], gt, next_j(x, m))
     down = jnp.where(m["j_first"], gt, last_j(x, m))
-    out.append(minmod(0.25 * up - x4, x4 - 0.25 * down))
+    out.append(0.25 * minmod(up - x, x - down))
     up = jnp.where(m["k_last"], gk, next_k(x))
     down = jnp.where(m["k_first"], gk, last_k(x))
-    out.append(minmod(0.25 * up - x4, x4 - 0.25 * down))
+    out.append(0.25 * minmod(up - x, x - down))
     return out
 
 
@@ -508,14 +498,14 @@
                 edge_ref[side] == 1, jnp.full_like(y, far), y
             )
 
-    def spread(n, _):
-        c, g = n // 3, n % 3
-        low, high = (v_ref[rows8((side * 10 + c) * PL + g * 8), :] for side in range(2))
-        for i in range(EDGE):
-            gk_ref[rows8(c * ROWS + i * PL + g * 8), :] = spread_k(low, high, i)
+    def spread(c, _):
+        for g in range(3):
+            low, high = (v_ref[rows8((side * 10 + c) * PL + g * 8), :] for side in range(2))
+            for i in range(EDGE):
+                gk_ref[rows8(c * ROWS + i * PL + g * 8), :] = spread_k(low, high, i)
         return 0
 
-    lax.fori_loop(0, 30, spread, 0)
+    lax.fori_loop(0, 10, spread, 0)
 
     def packed(load, out_ref, depth, first, step, g):
         planes = [[load(n) for n in range(depth)], [load(EDGE - 1 - n) for n in range(depth)]]
@@ -525,19 +515,19 @@
                     row = (((n * 2 + side) * depth + at) * step + first) * PL + g * 8
                     out_ref[rows8(row), :] = sides[side][at]
 
-    def pack(n, _):
-        c, g = n // 3, n % 3
-
-        def load_of(ref, first):
-            return lambda i: ref[rows8((c + first) * ROWS + i * PL + g * 8), :]
-
-        packed(load_of(prim_ref, 0), px_ref, 3, c, 10, g)
-        packed(load_of(adj_ref, 0), px_ref, 3, c + 5, 10, g)
-        packed(load_of(gk_ref, 0), pg_ref, 2, c, 10, g)
-        packed(load_of(gk_ref, 5), pg_ref, 2, c + 5, 10, g)
+    def pack(c, _):
+        for g in range(3):
+
+            def load_of(ref, first):
+                return lambda i: ref[rows8((c + first) * ROWS + i * PL + g * 8), :]
+
+            packed(load_of(prim_ref, 0), px_ref, 3, c, 10, g)
+            packed(load_of(adj_ref, 0), px_ref, 3, c + 5, 10, g)
+            packed(load_of(gk_ref, 0), pg_ref, 2, c, 10, g)
+            packed(load_of(gk_ref, 5), pg_ref, 2, c + 5, 10, g)
         return 0
 
-    lax.fori_loop(0, 15, pack, 0)
+    lax.fori_loop(0, 5, pack, 0)
     for g in range(3):
         packed(lambda i: solid_ref[pl.ds(i * PL + g * 8, 8), :], ps_ref, 2, 0, 1, g)
 
@@ -616,7 +606,7 @@
 
         for q in range(3):
             pv_ref[pl.ds((28 + q) * 8, 8), :] = jnp.zeros((8, LANES), jnp.float32)
-        lax.fori_loop(1, EDGE - 1, plane, 0)
+        lax.fori_loop(1, EDGE - 1, plane, 0, unroll=2)
         return 0
 
     lax.fori_loop(0, 3, column, 0)
@@ -641,14 +631,11 @@
         for f in range(4):
             gl_ref[pl.ds((f * 10 + c) * PL, PL), :] = y[f * PL : (f + 1) * PL]
 
-    def side_ghosts(n, _):
-        c, g = n // 3, n % 3
-        low, high = (gl_ref[rows8((f * 10 + c) * PL + g * 8), :] for f in (2, 3))
-        for at, i in enumerate((0, 1, EDGE - 1, EDGE - 2)):
-            tg_ref[rows8((at * 10 + c) * PL + g * 8), :] = spread_j(low, high, i)
-        return 0
-
-    lax.fori_loop(0, 30, side_ghosts, 0)
+    for c in range(10):
+        for g in range(3):
+            low, high = (gl_ref[rows8((f * 10 + c) * PL + g * 8), :] for f in (2, 3))
+            for at, i in enumerate((0, 1, EDGE - 1, EDGE - 2)):
+                tg_ref[rows8((at * 10 + c) * PL + g * 8), :] = spread_j(low, high, i)
     m = masks()
 
     def boundary(n):
@@ -780,9 +767,9 @@
     return pl.pallas_call(
         prep_kernel,
         out_shape=[
-            shape(5 * ROWS, LANES),
-            shape(5 * ROWS, LANES),
-            shape(ROWS, LANES),
+            pltpu.VMEM((5 * ROWS, LANES), jnp.float32),
+            pltpu.VMEM((5 * ROWS, LANES), jnp.float32),
+            pltpu.VMEM((ROWS, LANES), jnp.float32),
             shape(10 * FACES, LANES),
             shape(10 * PL, LANES),
             shape(10 * PL, LANES),
@@ -808,9 +795,7 @@
 def inner(edge, index, prim, adj, solid, low, high):
     return pl.pallas_call(
         inner_kernel,
-        out_shape=[
-            shape(ROWS, LANES), shape(120 * PL, LANES), shape(80 * PL, LANES), shape(8 * PL, LANES)
-        ],
+        out_shape=[pltpu.VMEM((n, LANES), jnp.float32) for n in (ROWS, 120 * PL, 80 * PL, 8 * PL)],
         in_specs=[SMEM] + [VMEM] * 6,
         out_specs=[VMEM] * 4,
         scratch_shapes=scratch(20 * PL, 10 * ROWS, 31 * 8, 15 * 8),
@@ -829,11 +814,22 @@
     )(index, got, planes, ghosts, walls, solid, acc)
 
 
-def packed_requests(lateral_owner, lateral_link, vertical_link):
-    link = lateral_link.T
+def ask_kernel(owner_ref, link_ref, out_ref):
+    link = link_ref[...]
+    slot = (link.astype(jnp.float32) * 0.2 + 0.05).astype(jnp.int32)
     far = lax.broadcasted_iota(jnp.int32, link.shape, 0) ^ 1
-    own = (lateral_owner[:, :, 0].T * 64 + link // 5 * 4 + far) * 8 + link % 5
-    return own, vertical_link.T // 5 * 8 + vertical_link.T % 5
+    own = (owner_ref[...] * 64 + slot * 4 + far) * 8 + (link - 5 * slot)
+    out_ref[...] = jnp.broadcast_to(own[None], out_ref.shape)
+
+
+def ask(lateral_owner, lateral_link):
+    return pl.pallas_call(
+        ask_kernel,
+        out_shape=jax.ShapeDtypeStruct((PEERS, 4, NB), jnp.int32),
+        in_specs=[VMEM] * 2,
+        out_specs=VMEM,
+        compiler_params=PARAMS,
+    )(lateral_owner[:, :, 0].T, lateral_link.T)
 
 
 def exchange(block, axis):
@@ -843,12 +839,10 @@
 
 
 def local(flow, adjoint, cut_flag, lateral_owner, lateral_link, vertical_link):
-    own, vertical = packed_requests(lateral_owner, lateral_link, vertical_link)
-    asked = lax.all_to_all(
-        jnp.broadcast_to(own, (PEERS,) + own.shape), "blk", split_axis=0, concat_axis=0, tiled=True
-    )
+    own = ask(lateral_owner, lateral_link)
+    asked = lax.all_to_all(own, "blk", split_axis=0, concat_axis=0, tiled=True)
     prim, adj, solid, layers, low_face, high_face, index = prep(
-        flow, adjoint, cut_flag, own, vertical
+        flow, adjoint, cut_flag, own, vertical_link.T
     )
     asked, low_face, high_face = lax.optimization_barrier((asked, low_face, high_face))
     regions = lax.axis_size("grp")
@@ -857,7 +851,6 @@
     high = lax.ppermute(low_face, "grp", [(r + 1, r) for r in range(regions - 1)])
     me = lax.axis_index("blk").astype(jnp.int32).reshape(1)
     replies = reply(me, asked, layers)
-    replies, low, high = lax.optimization_barrier((replies, low, high))
     got = exchange(replies, "blk")
     edge = jnp.stack([region == 0, region == regions - 1]).astype(jnp.int32)
     acc, planes, ghosts, walls = inner(edge, index, prim, adj, solid, low, high)

time: 96 us -> 91.6 us (0.954)
  Pallas kernels: 59.4 us -> 44.5 us
  local copies, waits for them, and re-layouts: 2.38 us -> 13.6 us
  other arithmetic: 3.29 us -> 0.08 us
  waiting for transfers between devices: 2.97 us -> 5.69 us
    unnamed x10 -> x28, local copies, waits for them, and re-layouts: 1.71 us -> 13.6 us
    pallas_call x2 -> x3, Pallas kernels: 40.6 us -> 31.3 us  [the longest x1 26.8 us: inner(): pl.pallas_call(inner_kernel, out_shape=[pltpu.VMEM((n, LANES), jnp.float3...]
    pallas_call x1, Pallas kernels: 14.5 us -> 10 us  [rim(): pl.pallas_call(rim_kernel, out_shape=shape(NB, EDGE * EDGE * EDGE), in_sp...]
    ppermute x1, waiting for transfers between devices: 0.67 us -> 3.79 us  [local(): lax.ppermute(low_face, 'grp', [(r + 1, r) for r in range(regions - 1)])]
    add x2 -> x0, other arithmetic: 1.96 us -> none  [the longest x1 1.21 us: packed_requests(): return (own, vertical_link.T // 5 * 8 + vertical_link.T % 5)]
    pallas_call x1, Pallas kernels: 4.31 us -> 3.22 us  [reply(): pl.pallas_call(reply_kernel, out_shape=shape(40 * PEERS, LANES), in_specs...]
  transfers between devices with their start and end apart: 4 -> 4, of which waited for: 3 -> 3; matrix products, arithmetic and copies ran while one was open for 2% -> 0% of each run, Pallas kernels for 47% -> 34%
where the time goes in v4:
time: 91.6 us; the launch traced here: 90.7 us
  Pallas kernels  44.5 us (49%)
  starting transfers between devices  26.7 us (29%)
  local copies, waits for them, and re-layouts  13.6 us (15%)
  waiting for transfers between devices  5.69 us (6%)
    pallas_call x1, Pallas kernels, inner(): pl.pallas_call(inner_kernel, out_shape=[pltpu.VMEM((n, LANES), jnp.float3...  26.8 us
    unnamed x28, local copies, waits for them, and re-layouts  13.6 us
    all_to_all x1, starting transfers between devices, local(): asked = lax.all_to_all(own, 'blk', split_axis=0, concat_axis=0, tiled=True)  13 us
    pallas_call x1, Pallas kernels, rim(): pl.pallas_call(rim_kernel, out_shape=shape(NB, EDGE * EDGE * EDGE), in_sp...  10 us
    all_to_all x1, starting transfers between devices, exchange(): out = lax.all_to_all(chunks, axis, split_axis=0, concat_axis=0, tiled=True)  9.24 us
    pallas_call x1, Pallas kernels, prep(): pl.pallas_call(prep_kernel, out_shape=[pltpu.VMEM((5 * ROWS, LANES), jnp....  3.86 us
    ppermute x1, waiting for transfers between devices, local(): lax.ppermute(low_face, 'grp', [(r + 1, r) for r in range(regions - 1)])  3.79 us
    pallas_call x1, Pallas kernels, reply(): pl.pallas_call(reply_kernel, out_shape=shape(40 * PEERS, LANES), in_specs...  3.22 us
  transfers between devices with their start and end apart: 4, of which 3 were waited for; matrix products, arithmetic and copies ran while one was open for 0% of the time, Pallas kernels for 34%

profile of v4, /device:TPU:1, one launch (start us, length us, event | category | flops | bytes accessed | tf_op | source)
XLA Modules:
  0.0 90.7 jit_solution(14578368862762436448)
XLA Ops:
  0.0 0.7 copy-done.11
  0.7 0.7 copy-done.12
  1.4 0.7 shard_map.64.own_ref
  2.0 13.0 %all-to-all-start = ((s32[64,4,12]{2,1,0:T(4,128)}), s32[64,4,12]{2,1,0:T(4,128)S(1)}, u32[]{:S(2)}, u32[]{:S(2)}) async-start(s32[64,4,12]{2,1,0:T(4,128)} %shard_map.64.own_ref), calls=%async_computation | async-start | bytes 262144 | tf_op jit(solution)/shard_map/all_to_all | solution.py:843
  15.1 1.3 %copy-done = f32[12,5,4096]{2,0,1:T(8,128)S(1)} copy-done((f32[12,5,4096]{2,0,1:T(8,128)S(1)}, f32[12,5,4096]{2,0,1:T(8,128)}, u32[]{:S(2)}) %copy-start) | copy-done | bytes 983064
  16.4 1.3 %copy-done.1 = f32[12,5,4096]{2,0,1:T(8,128)S(1)} copy-done((f32[12,5,4096]{2,0,1:T(8,128)S(1)}, f32[12,5,4096]{2,0,1:T(8,128)}, u32[]{:S(2)}) %copy-start.1) | copy-done | bytes 983064
  17.7 0.9 %copy-done.8 = s32[12,4096]{1,0:T(8,128)S(1)} copy-done((s32[12,4096]{1,0:T(8,128)S(1)}, s32[12,4096]{1,0:T(8,128)}, u32[]{:S(2)}) %copy-start.8) | copy-done | bytes 196632
  19.3 3.9 %shard_map.65 = (f32[1920,128]{1,0:T(8,128)S(1)}, f32[1920,128]{1,0:T(8,128)S(1)}, f32[384,128]{1,0:T(8,128)S(1)}, f32[960,128]{1,0:T(8,128)S(1)}, f32[240,128]{...) custom-call(f32[5,12,4096]{2,1,0:T(8,128)S(1)} %bitcast.14, f32[5,12,4096]{2,1,0:T(8,128)S(1)} %bitcast.15, ...), custom_call_target="tpu_custom_call" | custom-call | flops 100000000 | bytes 30000000 | tf_op jit(solution)/shard_map/pallas_call | solution.py:767
  23.2 1.0 %copy-done.2 = f32[1920,128]{1,0:T(8,128)} copy-done((f32[1920,128]{1,0:T(8,128)}, f32[1920,128]{1,0:T(8,128)S(1)}, u32[]{:S(2)}) %copy-start.2) | copy-done | bytes 983064
  24.1 1.0 %copy-done.4 = f32[1920,128]{1,0:T(8,128)} copy-done((f32[1920,128]{1,0:T(8,128)}, f32[1920,128]{1,0:T(8,128)S(1)}, u32[]{:S(2)}) %copy-start.4) | copy-done | bytes 983064
  25.1 1.1 %all-to-all-done.asked_ref = s32[64,4,12]{2,1,0:T(4,128)S(1)} async-done(((s32[64,4,12]{2,1,0:T(4,128)}), s32[64,4,12]{2,1,0:T(4,128)S(1)}, u32[]{:S(2)}, u32[]{:S(2)}) %all-to-all-start) | async-done | bytes 12320 | tf_op jit(solution)/shard_map/all_to_all | solution.py:843
  26.2 3.2 %shard_map.66 = f32[2560,128]{1,0:T(8,128)} custom-call(s32[1]{0:T(128)} %bitcast.7.me_ref, s32[64,4,12]{2,1,0:T(4,128)S(1)} %all-to-all-done.asked_ref, f32[960,128]{1,0:T(8,128)S(1)} %get-tuple-element.23.lat_ref), custom_call_target="tpu_custom_call" | custom-call | tf_op jit(solution)/shard_map/pallas_call | solution.py:786
  29.4 9.2 %all-to-all-start.1 = ((f32[64,40,128]{2,1,0:T(8,128)}), f32[64,40,128]{2,1,0:T(8,128)S(1)}, u32[]{:S(2)}, u32[]{:S(2)}) async-start(f32[64,40,128]{2,1,0:T(8,128)} %bitcast.8), calls=%async_computation.1 | async-start | bytes 2621440 | tf_op jit(solution)/shard_map/all_to_all | solution.py:837
  38.6 3.2 %collective-permute-start = (f32[240,128]{1,0:T(8,128)S(1)}, f32[240,128]{1,0:T(8,128)S(1)}, u32[]{:S(2)}, u32[]{:S(2)}) collective-permute-start(f32[240,128]{1,0:T(8,128)S(1)} %get-tuple-element.27), channel_id=1, source_target_pairs={{0,1},{1,2},{2,3},{4,5},{5,6},{6,7},{8,9},{9,10},{10,11},{12,13},{... | collective-permute-start | bytes 368648 | tf_op jit(solution)/shard_map/ppermute | solution.py:850
  41.8 1.3 %collective-permute-start.1 = (f32[240,128]{1,0:T(8,128)S(1)}, f32[240,128]{1,0:T(8,128)S(1)}, u32[]{:S(2)}, u32[]{:S(2)}) collective-permute-start(f32[240,128]{1,0:T(8,128)S(1)} %get-tuple-element.28), channel_id=1, source_target_pairs={{1,0},{2,1},{3,2},{5,4},{6,5},{7,6},{9,8},{10,9},{11,10},{13,12},{... | collective-permute-start | bytes 368648 | tf_op jit(solution)/shard_map/ppermute | solution.py:851
  43.2 0.8 collective-permute-done.low_ref
  44.1 3.8 %collective-permute-done.1.high_ref = f32[240,128]{1,0:T(8,128)S(1)} collective-permute-done((f32[240,128]{1,0:T(8,128)S(1)}, f32[240,128]{1,0:T(8,128)S(1)}, u32[]{:S(2)}, u32[]{:S(2)}) %collective-permute-start.1) | collective-permute-done | bytes 122912 | tf_op jit(solution)/shard_map/ppermute | solution.py:851
  48.5 1.2 %copy-done.3 = f32[1920,128]{1,0:T(8,128)S(1)} copy-done((f32[1920,128]{1,0:T(8,128)S(1)}, f32[1920,128]{1,0:T(8,128)}, u32[]{:S(2)}) %copy-start.3) | copy-done | bytes 983064
  49.7 1.2 %copy-done.5 = f32[1920,128]{1,0:T(8,128)S(1)} copy-done((f32[1920,128]{1,0:T(8,128)S(1)}, f32[1920,128]{1,0:T(8,128)}, u32[]{:S(2)}) %copy-start.5) | copy-done | bytes 983064
  50.9 0.9 copy-done.10
  51.8 26.8 %shard_map.67 = (f32[384,128]{1,0:T(8,128)S(1)}, f32[2880,128]{1,0:T(8,128)S(1)}, f32[1920,128]{1,0:T(8,128)S(1)}, f32[192,128]{1,0:T(8,128)S(1)}) custom-call(s32[2]{0:T(128)S(1)} %add_convert_fusion.edge_ref, s32[288,128]{1,0:T(8,128)S(1)} %get-tuple-element.19.index_ref, f32[1920,128]{1,0:T(8,128)S(1)} %copy-done.3, f32[1920,128]{1,0:T(8,128)S(1)} %copy-done.5, ...), custom_call_target="tpu_custom_call" | custom-call | tf_op jit(solution)/shard_map/pallas_call | solution.py:796
  78.6 0.9 %copy-done.6 = f32[1920,128]{1,0:T(8,128)} copy-done((f32[1920,128]{1,0:T(8,128)}, f32[1920,128]{1,0:T(8,128)S(1)}, u32[]{:S(2)}) %copy-start.6) | copy-done | bytes 983064
  79.5 1.2 %copy-done.7 = f32[1920,128]{1,0:T(8,128)S(1)} copy-done((f32[1920,128]{1,0:T(8,128)S(1)}, f32[1920,128]{1,0:T(8,128)}, u32[]{:S(2)}) %copy-start.7) | copy-done | bytes 983064
  80.7 10.0 %shard_map.68 = f32[12,4096]{1,0:T(8,128)} custom-call(s32[288,128]{1,0:T(8,128)S(1)} %get-tuple-element.19.index_ref, f32[2560,128]{1,0:T(8,128)S(1)} %bitcast.13, f32[2880,128]{1,0:T(8,128)S(1)} %get-tuple-element.29.px_ref, f32[1920,128]{1,0:T(8,128)S(1)} %copy-done.7, f32[192,128]{1,0:T(8,128)S(1)} %get-tuple-element.31.ps_ref, ...), custom_call_target="tpu_custom_call" | custom-call | tf_op jit(solution)/shard_map/pallas_call | solution.py:807
  (18 shorter events, 1.4 us)
Async XLA Ops:
  0.0 0.7 copy-start.11
  0.7 0.7 copy-start.12
  2.0 24.1 %all-to-all-start = ((s32[64,4,12]{2,1,0:T(4,128)}), s32[64,4,12]{2,1,0:T(4,128)S(1)}, u32[]{:S(2)}, u32[]{:S(2)}) async-start(s32[64,4,12]{2,1,0:T(4,128)} %shard_map.64.own_ref), calls=%async_computation | async-start | bytes 262144 | tf_op jit(solution)/shard_map/all_to_all | solution.py:843
  15.0 1.3 %copy-start = (f32[12,5,4096]{2,0,1:T(8,128)S(1)}, f32[12,5,4096]{2,0,1:T(8,128)}, u32[]{:S(2)}) copy-start(f32[12,5,4096]{2,0,1:T(8,128)} %param.6) | copy-start | bytes 2949124
  16.4 1.3 %copy-start.1 = (f32[12,5,4096]{2,0,1:T(8,128)S(1)}, f32[12,5,4096]{2,0,1:T(8,128)}, u32[]{:S(2)}) copy-start(f32[12,5,4096]{2,0,1:T(8,128)} %param.7) | copy-start | bytes 2949124
  17.7 0.9 %copy-start.8 = (s32[12,4096]{1,0:T(8,128)S(1)}, s32[12,4096]{1,0:T(8,128)}, u32[]{:S(2)}) copy-start(s32[12,4096]{1,0:T(8,128)} %param.8) | copy-start | bytes 589828
  18.6 0.7 copy-start.13
  23.2 1.0 %copy-start.2 = (f32[1920,128]{1,0:T(8,128)}, f32[1920,128]{1,0:T(8,128)S(1)}, u32[]{:S(2)}) copy-start(f32[1920,128]{1,0:T(8,128)S(1)} %get-tuple-element.24.prim_ref) | copy-start | bytes 2949124
  24.1 1.0 %copy-start.4 = (f32[1920,128]{1,0:T(8,128)}, f32[1920,128]{1,0:T(8,128)S(1)}, u32[]{:S(2)}) copy-start(f32[1920,128]{1,0:T(8,128)S(1)} %get-tuple-element.25.adj_ref) | copy-start | bytes 2949124
  29.4 50.1 %all-to-all-start.1 = ((f32[64,40,128]{2,1,0:T(8,128)}), f32[64,40,128]{2,1,0:T(8,128)S(1)}, u32[]{:S(2)}, u32[]{:S(2)}) async-start(f32[64,40,128]{2,1,0:T(8,128)} %bitcast.8), calls=%async_computation.1 | async-start | bytes 2621440 | tf_op jit(solution)/shard_map/all_to_all | solution.py:837
  38.6 5.4 %collective-permute-start = (f32[240,128]{1,0:T(8,128)S(1)}, f32[240,128]{1,0:T(8,128)S(1)}, u32[]{:S(2)}, u32[]{:S(2)}) collective-permute-start(f32[240,128]{1,0:T(8,128)S(1)} %get-tuple-element.27), channel_id=1, source_target_pairs={{0,1},{1,2},{2,3},{4,5},{5,6},{6,7},{8,9},{9,10},{10,11},{12,13},{... | collective-permute-start | bytes 368648 | tf_op jit(solution)/shard_map/ppermute | solution.py:850
  41.8 6.0 %collective-permute-start.1 = (f32[240,128]{1,0:T(8,128)S(1)}, f32[240,128]{1,0:T(8,128)S(1)}, u32[]{:S(2)}, u32[]{:S(2)}) collective-permute-start(f32[240,128]{1,0:T(8,128)S(1)} %get-tuple-element.28), channel_id=1, source_target_pairs={{1,0},{2,1},{3,2},{5,4},{6,5},{7,6},{9,8},{10,9},{11,10},{13,12},{... | collective-permute-start | bytes 368648 | tf_op jit(solution)/shard_map/ppermute | solution.py:851
  47.9 0.6 copy-start.9
  48.5 1.2 %copy-start.3 = (f32[1920,128]{1,0:T(8,128)S(1)}, f32[1920,128]{1,0:T(8,128)}, u32[]{:S(2)}) copy-start(f32[1920,128]{1,0:T(8,128)} %copy-done.2) | copy-start | bytes 2949124
  49.7 1.2 %copy-start.5 = (f32[1920,128]{1,0:T(8,128)S(1)}, f32[1920,128]{1,0:T(8,128)}, u32[]{:S(2)}) copy-start(f32[1920,128]{1,0:T(8,128)} %copy-done.4) | copy-start | bytes 2949124
  50.9 0.9 copy-start.10
  78.6 0.9 %copy-start.6 = (f32[1920,128]{1,0:T(8,128)}, f32[1920,128]{1,0:T(8,128)S(1)}, u32[]{:S(2)}) copy-start(f32[1920,128]{1,0:T(8,128)S(1)} %get-tuple-element.30.pg_ref) | copy-start | bytes 2949124
  79.5 1.2 %copy-start.7 = (f32[1920,128]{1,0:T(8,128)S(1)}, f32[1920,128]{1,0:T(8,128)}, u32[]{:S(2)}) copy-start(f32[1920,128]{1,0:T(8,128)} %copy-done.6) | copy-start | bytes 2949124

commit v5 on v4

--- a/solution.py
+++ b/solution.py
@@ -25,7 +25,7 @@
 START = 1.2 / math.sqrt(5.0)
 CURVE = 1.25 * math.sqrt(5.0)
 
-VMEM_LIMIT = 24 * 2**20
+VMEM_LIMIT = 56 * 2**20
 
 
 def lane():
@@ -142,7 +142,7 @@
         relaid(adj_ref, c, adjl_ref)
     relaid(flag_ref, 0, solid_ref)
     index_tables(
-        own_ref[0].astype(jnp.float32), vertical_ref[...].astype(jnp.float32), index_ref
+        own_ref[...].astype(jnp.float32), vertical_ref[...].astype(jnp.float32), index_ref
     )
 
     def convert(n, _):
@@ -183,28 +183,23 @@
 
 
 def reply_kernel(me_ref, asked_ref, lat_ref, out_ref):
-    before = lax.broadcasted_iota(jnp.int32, (NB, NB), 0) < lax.broadcasted_iota(
-        jnp.int32, (NB, NB), 1
+    before = lax.broadcasted_iota(jnp.int32, (LANES, LANES), 0) < lax.broadcasted_iota(
+        jnp.int32, (LANES, LANES), 1
     )
-    before = jnp.where(before, 1.0, 0.0)
-    earlier = jnp.zeros((PEERS, 1), jnp.float32)
-    entries = []
-    for f in range(4):
-        asked = asked_ref[:, f, :]
-        match = (asked >> 9) == me_ref[0]
-        hits = jnp.where(match, 1.0, 0.0)
-        rank = jnp.dot(hits, before, preferred_element_type=jnp.float32) + earlier
-        earlier = earlier + jnp.sum(hits, axis=1, keepdims=True)
-        face = (asked >> 3) & 63
-        target = (((face & 3) * PL) + ((face >> 2) * 2)).astype(jnp.float32) + 10.0
-        entries.append((match, rank, target))
+    asked = asked_ref[...]
+    match = (asked >> 9) == me_ref[0]
+    rank = jnp.dot(
+        jnp.where(match, 1.0, 0.0),
+        jnp.where(before, 1.0, 0.0),
+        preferred_element_type=jnp.float32,
+    )
+    face = (asked >> 3) & 63
+    target = (((face & 3) * PL) + ((face >> 2) * 2)).astype(jnp.float32) + 10.0
     column = lax.broadcasted_iota(jnp.int32, (PEERS, FACES), 1).astype(jnp.float32)
     picks = []
     for s in range(2):
-        row = jnp.full((PEERS, 1), -10.0, jnp.float32)
-        for match, rank, target in entries:
-            mine = match & (rank > s - 0.5) & (rank < s + 0.5)
-            row = row + jnp.sum(jnp.where(mine, target, 0.0), axis=1, keepdims=True)
+        mine = match & (rank > s - 0.5) & (rank < s + 0.5)
+        row = jnp.sum(jnp.where(mine, target, 0.0), axis=1, keepdims=True) - 10.0
         for h in range(2):
             picks.append(jnp.where(column == row + float(h), 1.0, 0.0))
     picks = jnp.concatenate(picks, axis=0)
@@ -767,9 +762,9 @@
     return pl.pallas_call(
         prep_kernel,
         out_shape=[
-            pltpu.VMEM((5 * ROWS, LANES), jnp.float32),
-            pltpu.VMEM((5 * ROWS, LANES), jnp.float32),
-            pltpu.VMEM((ROWS, LANES), jnp.float32),
+            shape(5 * ROWS, LANES),
+            shape(5 * ROWS, LANES),
+            shape(ROWS, LANES),
             shape(10 * FACES, LANES),
             shape(10 * PL, LANES),
             shape(10 * PL, LANES),
@@ -795,7 +790,7 @@
 def inner(edge, index, prim, adj, solid, low, high):
     return pl.pallas_call(
         inner_kernel,
-        out_shape=[pltpu.VMEM((n, LANES), jnp.float32) for n in (ROWS, 120 * PL, 80 * PL, 8 * PL)],
+        out_shape=[shape(n, LANES) for n in (ROWS, 120 * PL, 80 * PL, 8 * PL)],
         in_specs=[SMEM] + [VMEM] * 6,
         out_specs=[VMEM] * 4,
         scratch_shapes=scratch(20 * PL, 10 * ROWS, 31 * 8, 15 * 8),
@@ -814,20 +809,36 @@
     )(index, got, planes, ghosts, walls, solid, acc)
 
 
-def ask_kernel(owner_ref, link_ref, out_ref):
+def ask_kernel(owner_ref, link_ref, own_ref, out_ref):
     link = link_ref[...]
     slot = (link.astype(jnp.float32) * 0.2 + 0.05).astype(jnp.int32)
     far = lax.broadcasted_iota(jnp.int32, link.shape, 0) ^ 1
     own = (owner_ref[...] * 64 + slot * 4 + far) * 8 + (link - 5 * slot)
-    out_ref[...] = jnp.broadcast_to(own[None], out_ref.shape)
+    own_ref[...] = own
+    at = lax.broadcasted_iota(jnp.int32, (NB, LANES), 0)
+    spot = lax.broadcasted_iota(jnp.int32, (NB, LANES), 1)
+    row = jnp.full((1, LANES), -1.0, jnp.float32)
+    for f in range(4):
+        spread = jnp.dot(
+            own[f : f + 1].astype(jnp.float32) + 1.0,
+            jnp.where(spot == at + f * NB, 1.0, 0.0),
+            precision=lax.Precision.HIGHEST,
+            preferred_element_type=jnp.float32,
+        )
+        row = row + spread
+    row = (row + jnp.where(row < 0.0, -0.25, 0.25)).astype(jnp.int32)
+    out_ref[...] = jnp.broadcast_to(row, out_ref.shape)
 
 
 def ask(lateral_owner, lateral_link):
     return pl.pallas_call(
         ask_kernel,
-        out_shape=jax.ShapeDtypeStruct((PEERS, 4, NB), jnp.int32),
+        out_shape=[
+            jax.ShapeDtypeStruct((4, NB), jnp.int32),
+            jax.ShapeDtypeStruct((PEERS, LANES), jnp.int32),
+        ],
         in_specs=[VMEM] * 2,
-        out_specs=VMEM,
+        out_specs=[VMEM] * 2,
         compiler_params=PARAMS,
     )(lateral_owner[:, :, 0].T, lateral_link.T)
 
@@ -839,8 +850,8 @@
 
 
 def local(flow, adjoint, cut_flag, lateral_owner, lateral_link, vertical_link):
-    own = ask(lateral_owner, lateral_link)
-    asked = lax.all_to_all(own, "blk", split_axis=0, concat_axis=0, tiled=True)
+    own, questions = ask(lateral_owner, lateral_link)
+    asked = exchange(questions, "blk")
     prim, adj, solid, layers, low_face, high_face, index = prep(
         flow, adjoint, cut_flag, own, vertical_link.T
     )
@@ -851,6 +862,7 @@
     high = lax.ppermute(low_face, "grp", [(r + 1, r) for r in range(regions - 1)])
     me = lax.axis_index("blk").astype(jnp.int32).reshape(1)
     replies = reply(me, asked, layers)
+    replies, low, high = lax.optimization_barrier((replies, low, high))
     got = exchange(replies, "blk")
     edge = jnp.stack([region == 0, region == regions - 1]).astype(jnp.int32)
     acc, planes, ghosts, walls = inner(edge, index, prim, adj, solid, low, high)

time: 91.6 us -> 89.7 us (0.979)
  local copies, waits for them, and re-layouts: 13.6 us -> 1.71 us
  Pallas kernels: 44.5 us -> 52.9 us
  waiting for transfers between devices: 5.69 us -> 7.62 us
    all_to_all x1 -> x0, starting transfers between devices: 13 us -> none  [local(): asked = lax.all_to_all(own, 'blk', split_axis=0, concat_axis=0, tiled=True)]
    all_to_all x1 -> x2, starting transfers between devices: 9.24 us -> 21.9 us  [exchange(): out = lax.all_to_all(chunks, axis, split_axis=0, concat_axis=0, tiled=True)]
    unnamed x28 -> x8, local copies, waits for them, and re-layouts: 13.6 us -> 1.71 us
    all_to_all x1 -> x2, waiting for transfers between devices: 0.01 us -> 6.65 us  [exchange(): out = lax.all_to_all(chunks, axis, split_axis=0, concat_axis=0, tiled=True)]
    pallas_call x3, Pallas kernels: 31.3 us -> 37.2 us  [the longest x1 29.4 us: inner(): pl.pallas_call(inner_kernel, out_shape=[shape(n, LANES) for n in (ROWS, 1...]
    ppermute x1, waiting for transfers between devices: 3.79 us -> 0.97 us  [local(): lax.ppermute(low_face, 'grp', [(r + 1, r) for r in range(regions - 1)])]
    pallas_call x1, Pallas kernels: 10 us -> 12.2 us  [rim(): pl.pallas_call(rim_kernel, out_shape=shape(NB, EDGE * EDGE * EDGE), in_sp...]
    all_to_all x1 -> x0, waiting for transfers between devices: 1.06 us -> none  [local(): asked = lax.all_to_all(own, 'blk', split_axis=0, concat_axis=0, tiled=True)]
  transfers between devices with their start and end apart: 4 -> 4, of which waited for: 3 -> 3; matrix products, arithmetic and copies ran while one was open for 0% -> 1% of each run, Pallas kernels for 34% -> 44%
where the time goes in v5:
time: 89.7 us; the launch traced here: 89.3 us
  Pallas kernels  52.9 us (59%)
  starting transfers between devices  26.4 us (29%)
  waiting for transfers between devices  7.62 us (8%)
  local copies, waits for them, and re-layouts  1.71 us (2%)
    pallas_call x1, Pallas kernels, inner(): pl.pallas_call(inner_kernel, out_shape=[shape(n, LANES) for n in (ROWS, 1...  29.4 us
    all_to_all x2, starting transfers between devices, exchange(): out = lax.all_to_all(chunks, axis, split_axis=0, concat_axis=0, tiled=True)  21.9 us
    pallas_call x1, Pallas kernels, rim(): pl.pallas_call(rim_kernel, out_shape=shape(NB, EDGE * EDGE * EDGE), in_sp...  12.2 us
    all_to_all x2, waiting for transfers between devices, exchange(): out = lax.all_to_all(chunks, axis, split_axis=0, concat_axis=0, tiled=True)  6.65 us
    pallas_call x1, Pallas kernels, prep(): pl.pallas_call(prep_kernel, out_shape=[shape(5 * ROWS, LANES), shape(5 *...  6.32 us
    pallas_call x1, Pallas kernels, reply(): pl.pallas_call(reply_kernel, out_shape=shape(40 * PEERS, LANES), in_specs...  3.55 us
    ppermute x1, starting transfers between devices, local(): lax.ppermute(high_face, 'grp', [(r, r + 1) for r in range(regions - 1)])  3.2 us
  transfers between devices with their start and end apart: 4, of which 3 were waited for; matrix products, arithmetic and copies ran while one was open for 1% of the time, Pallas kernels for 44%

profile of v5, /device:TPU:1, one launch (start us, length us, event | category | flops | bytes accessed | tf_op | source)
XLA Modules:
  0.0 89.3 jit_solution(10323414140505233866)
XLA Ops:
  0.0 1.5 %shard_map.64 = (s32[4,12]{1,0:T(4,128)}, s32[64,128]{1,0:T(8,128)}) custom-call(s32[4,12]{1,0:T(4,128)} %bitcast.24, s32[4,12]{1,0:T(4,128)} %bitcast.25), custom_call_target="tpu_custom_call" | custom-call | tf_op jit(solution)/shard_map/pallas_call | solution.py:834
  1.5 13.0 %all-to-all-start = ((s32[64,1,128]{2,1,0:T(1,128)}), s32[64,1,128]{2,1,0:T(1,128)S(1)}, u32[]{:S(2)}, u32[]{:S(2)}) async-start(s32[64,1,128]{2,1,0:T(1,128)} %bitcast.23), calls=%async_computation | async-start | bytes 65536 | tf_op jit(solution)/shard_map/all_to_all | solution.py:848
  14.5 6.3 %shard_map.65 = (f32[1920,128]{1,0:T(8,128)}, f32[1920,128]{1,0:T(8,128)}, f32[384,128]{1,0:T(8,128)}, f32[960,128]{1,0:T(8,128)}, f32[240,128]{1,0:T(8,128)}, /*index=5*/f32[240,128]{1,0:T(8,128)}, s32[288,128]{1,0:T(8,128)}) custom-call(f32[5,12,4096]{2,1,0:T(8,128)} %bitcast.19, f32[5,12,4096]{2,1,0:T(8,128)} %bitcast.20, s32[1,12,4096]{2,1,0:T(8,128)} %bitcast.21, ...), custom_call_target="tpu_custom_call" | custom-call | flops 100000000 | bytes 30000000 | tf_op jit(solution)/shard_map/pallas_call | solution.py:762
  20.8 3.1 %all-to-all-done = s32[64,1,128]{2,1,0:T(1,128)S(1)} async-done(((s32[64,1,128]{2,1,0:T(1,128)}), s32[64,1,128]{2,1,0:T(1,128)S(1)}, u32[]{:S(2)}, u32[]{:S(2)}) %all-to-all-start) | async-done | bytes 32800 | tf_op jit(solution)/shard_map/all_to_all | solution.py:848
  23.9 0.0 copy-start.1
  23.9 3.2 %collective-permute-start = (f32[240,128]{1,0:T(8,128)}, f32[240,128]{1,0:T(8,128)S(1)}, u32[]{:S(2)}, u32[]{:S(2)}) collective-permute-start(f32[240,128]{1,0:T(8,128)} %get-tuple-element.31), channel_id=1, source_target_pairs={{0,1},{1,2},{2,3},{4,5},{5,6},{6,7},{8,9},{9,10},{10,11},{12,13},{... | collective-permute-start | bytes 368648 | tf_op jit(solution)/shard_map/ppermute | solution.py:861
  27.1 1.3 %collective-permute-start.1 = (f32[240,128]{1,0:T(8,128)}, f32[240,128]{1,0:T(8,128)S(1)}, u32[]{:S(2)}, u32[]{:S(2)}) collective-permute-start(f32[240,128]{1,0:T(8,128)} %get-tuple-element.32), channel_id=1, source_target_pairs={{1,0},{2,1},{3,2},{5,4},{6,5},{7,6},{9,8},{10,9},{11,10},{13,12},{... | collective-permute-start | bytes 368648 | tf_op jit(solution)/shard_map/ppermute | solution.py:862
  28.4 0.0 copy-done.1
  28.4 3.5 %shard_map.66 = f32[2560,128]{1,0:T(8,128)} custom-call(s32[1]{0:T(128)} %bitcast.7.me_ref, s32[64,128]{1,0:T(8,128)} %bitcast.22, f32[960,128]{1,0:T(8,128)} %get-tuple-element.30.lat_ref), custom_call_target="tpu_custom_call" | custom-call | tf_op jit(solution)/shard_map/pallas_call | solution.py:781
  31.9 0.0 collective-permute-done.low_ref
  31.9 0.0 copy-start.2
  31.9 1.0 %collective-permute-done.1.high_ref = f32[240,128]{1,0:T(8,128)S(1)} collective-permute-done((f32[240,128]{1,0:T(8,128)}, f32[240,128]{1,0:T(8,128)S(1)}, u32[]{:S(2)}, u32[]{:S(2)}) %collective-permute-start.1) | collective-permute-done | bytes 122912 | tf_op jit(solution)/shard_map/ppermute | solution.py:862
  32.9 0.0 copy-start.3
  32.9 0.0 copy-done.2
  32.9 0.6 copy-done.3
  33.6 8.9 %all-to-all-start.1 = ((f32[64,40,128]{2,1,0:T(8,128)}), f32[64,40,128]{2,1,0:T(8,128)S(1)}, u32[]{:S(2)}, u32[]{:S(2)}) async-start(f32[64,40,128]{2,1,0:T(8,128)} %bitcast.17), calls=%async_computation.1 | async-start | bytes 2621440 | tf_op jit(solution)/shard_map/all_to_all | solution.py:848
  42.5 0.6 add_convert_fusion.edge_ref
  43.1 29.4 %shard_map.67 = (f32[384,128]{1,0:T(8,128)}, f32[2880,128]{1,0:T(8,128)}, f32[1920,128]{1,0:T(8,128)}, f32[192,128]{1,0:T(8,128)}) custom-call(s32[2]{0:T(128)} %add_convert_fusion.edge_ref, s32[288,128]{1,0:T(8,128)} %get-tuple-element.25.index_ref, f32[1920,128]{1,0:T(8,128)} %get-tuple-element.34.prim_ref, f32[1920,128]{1,0:T(8,128)} %get-tuple-element.35.adj_ref, ...), custom_call_target="tpu_custom_call" | custom-call | tf_op jit(solution)/shard_map/pallas_call | solution.py:791
  72.5 3.6 %all-to-all-done.1 = f32[64,40,128]{2,1,0:T(8,128)S(1)} async-done(((f32[64,40,128]{2,1,0:T(8,128)}), f32[64,40,128]{2,1,0:T(8,128)S(1)}, u32[]{:S(2)}, u32[]{:S(2)}) %all-to-all-start.1) | async-done | bytes 1310752 | tf_op jit(solution)/shard_map/all_to_all | solution.py:848
  76.1 0.0 copy-start
  76.1 1.1 %copy-done = f32[64,40,128]{2,1,0:T(8,128)} copy-done((f32[64,40,128]{2,1,0:T(8,128)}, f32[64,40,128]{2,1,0:T(8,128)S(1)}, u32[]{:S(2)}) %copy-start) | copy-done | bytes 1310744
  77.1 12.2 %shard_map.68 = f32[12,4096]{1,0:T(8,128)} custom-call(s32[288,128]{1,0:T(8,128)} %get-tuple-element.25.index_ref, f32[2560,128]{1,0:T(8,128)} %bitcast.18, f32[2880,128]{1,0:T(8,128)} %get-tuple-element.39.px_ref, f32[1920,128]{1,0:T(8,128)} %get-tuple-element.40.pg_ref, f32[192,128]{1,0:T(8,128)} %get-tuple-element.41.ps_ref, ...), custom_call_target="tpu_custom_call" | custom-call | tf_op jit(solution)/shard_map/pallas_call | solution.py:802
Async XLA Ops:
  1.5 22.4 %all-to-all-start = ((s32[64,1,128]{2,1,0:T(1,128)}), s32[64,1,128]{2,1,0:T(1,128)S(1)}, u32[]{:S(2)}, u32[]{:S(2)}) async-start(s32[64,1,128]{2,1,0:T(1,128)} %bitcast.23), calls=%async_computation | async-start | bytes 65536 | tf_op jit(solution)/shard_map/all_to_all | solution.py:848
  23.9 4.5 %copy-start.1 = (s32[64,1,128]{2,1,0:T(1,128)}, s32[64,1,128]{2,1,0:T(1,128)S(1)}, u32[]{:S(2)}) copy-start(s32[64,1,128]{2,1,0:T(1,128)S(1)} %all-to-all-done) | copy-start | bytes 98308
  23.9 8.1 %collective-permute-start = (f32[240,128]{1,0:T(8,128)}, f32[240,128]{1,0:T(8,128)S(1)}, u32[]{:S(2)}, u32[]{:S(2)}) collective-permute-start(f32[240,128]{1,0:T(8,128)} %get-tuple-element.31), channel_id=1, source_target_pairs={{0,1},{1,2},{2,3},{4,5},{5,6},{6,7},{8,9},{9,10},{10,11},{12,13},{... | collective-permute-start | bytes 368648 | tf_op jit(solution)/shard_map/ppermute | solution.py:861
  27.1 5.8 %collective-permute-start.1 = (f32[240,128]{1,0:T(8,128)}, f32[240,128]{1,0:T(8,128)S(1)}, u32[]{:S(2)}, u32[]{:S(2)}) collective-permute-start(f32[240,128]{1,0:T(8,128)} %get-tuple-element.32), channel_id=1, source_target_pairs={{1,0},{2,1},{3,2},{5,4},{6,5},{7,6},{9,8},{10,9},{11,10},{13,12},{... | collective-permute-start | bytes 368648 | tf_op jit(solution)/shard_map/ppermute | solution.py:862
  31.9 1.0 %copy-start.2 = (f32[240,128]{1,0:T(8,128)}, f32[240,128]{1,0:T(8,128)S(1)}, u32[]{:S(2)}) copy-start(f32[240,128]{1,0:T(8,128)S(1)} %collective-permute-done.low_ref) | copy-start | bytes 368644
  32.9 0.6 copy-start.3
  33.6 42.5 %all-to-all-start.1 = ((f32[64,40,128]{2,1,0:T(8,128)}), f32[64,40,128]{2,1,0:T(8,128)S(1)}, u32[]{:S(2)}, u32[]{:S(2)}) async-start(f32[64,40,128]{2,1,0:T(8,128)} %bitcast.17), calls=%async_computation.1 | async-start | bytes 2621440 | tf_op jit(solution)/shard_map/all_to_all | solution.py:848
  76.1 1.1 %copy-start = (f32[64,40,128]{2,1,0:T(8,128)}, f32[64,40,128]{2,1,0:T(8,128)S(1)}, u32[]{:S(2)}) copy-start(f32[64,40,128]{2,1,0:T(8,128)S(1)} %all-to-all-done.1) | copy-start | bytes 3932164

commit v6 on v5

--- a/solution.py
+++ b/solution.py
@@ -13,6 +13,7 @@
 ROWS = EDGE * PL
 LANES = 128
 PEERS = 64
+REGIONS = 4
 FACES = 4 * PL
 PXR = (EDGE + 2) * PL
 MR = (EDGE + 1) * PL
@@ -490,7 +491,7 @@
             y = widened(parts[c], index_ref[pl.ds(FACES + side * PL, PL), :])
             far = FARFIELD[c] if c < 5 else 0.0
             v_ref[pl.ds((side * 10 + c) * PL, PL), :] = jnp.where(
-                edge_ref[side] == 1, jnp.full_like(y, far), y
+                edge_ref[0] == side * (REGIONS - 1), jnp.full_like(y, far), y
             )
 
     def spread(c, _):
@@ -862,9 +863,8 @@
     high = lax.ppermute(low_face, "grp", [(r + 1, r) for r in range(regions - 1)])
     me = lax.axis_index("blk").astype(jnp.int32).reshape(1)
     replies = reply(me, asked, layers)
-    replies, low, high = lax.optimization_barrier((replies, low, high))
     got = exchange(replies, "blk")
-    edge = jnp.stack([region == 0, region == regions - 1]).astype(jnp.int32)
+    edge = region.astype(jnp.int32).reshape(1)
     acc, planes, ghosts, walls = inner(edge, index, prim, adj, solid, low, high)
     return rim(index, got, planes, ghosts, walls, solid, acc)
 

time: 89.7 us -> 88.6 us (0.988)
  starting transfers between devices: 26.4 us -> 24.9 us
    all_to_all x2, waiting for transfers between devices: 6.65 us -> 3.04 us  [exchange(): out = lax.all_to_all(chunks, axis, split_axis=0, concat_axis=0, tiled=True)]
    ppermute x1, waiting for transfers between devices: 0.97 us -> 3.8 us  [local(): lax.ppermute(low_face, 'grp', [(r + 1, r) for r in range(regions - 1)])]
    all_to_all x2, starting transfers between devices: 21.9 us -> 20.4 us  [exchange(): out = lax.all_to_all(chunks, axis, split_axis=0, concat_axis=0, tiled=True)]
    ppermute x1, waiting for transfers between devices: 0.01 us -> 0.9 us  [local(): lax.ppermute(high_face, 'grp', [(r, r + 1) for r in range(regions - 1)])]
    unnamed x8 -> x12, local copies, waits for them, and re-layouts: 1.71 us -> 2.32 us
  transfers between devices with their start and end apart: 4 -> 4, of which waited for: 3 -> 3; matrix products, arithmetic and copies ran while one was open for 1% -> 0% of each run, Pallas kernels for 44% -> 41%
where the time goes in v6:
time: 88.6 us; the launch traced here: 88 us
  Pallas kernels  53 us (60%)
  starting transfers between devices  24.9 us (28%)
  waiting for transfers between devices  7.75 us (9%)
  local copies, waits for them, and re-layouts  2.32 us (3%)
    pallas_call x1, Pallas kernels, inner(): pl.pallas_call(inner_kernel, out_shape=[shape(n, LANES) for n in (ROWS, 1...  29.4 us
    all_to_all x2, starting transfers between devices, exchange(): out = lax.all_to_all(chunks, axis, split_axis=0, concat_axis=0, tiled=True)  20.4 us
    pallas_call x1, Pallas kernels, rim(): pl.pallas_call(rim_kernel, out_shape=shape(NB, EDGE * EDGE * EDGE), in_sp...  12.2 us
    pallas_call x1, Pallas kernels, prep(): pl.pallas_call(prep_kernel, out_shape=[shape(5 * ROWS, LANES), shape(5 *...  6.33 us
    ppermute x1, waiting for transfers between devices, local(): lax.ppermute(low_face, 'grp', [(r + 1, r) for r in range(regions - 1)])  3.8 us
    pallas_call x1, Pallas kernels, reply(): pl.pallas_call(reply_kernel, out_shape=shape(40 * PEERS, LANES), in_specs...  3.55 us
    ppermute x1, starting transfers between devices, local(): lax.ppermute(high_face, 'grp', [(r, r + 1) for r in range(regions - 1)])  3.21 us
    all_to_all x2, waiting for transfers between devices, exchange(): out = lax.all_to_all(chunks, axis, split_axis=0, concat_axis=0, tiled=True)  3.04 us
  transfers between devices with their start and end apart: 4, of which 3 were waited for; matrix products, arithmetic and copies ran while one was open for 0% of the time, Pallas kernels for 41%

profile of v6, /device:TPU:1, one launch (start us, length us, event | category | flops | bytes accessed | tf_op | source)
XLA Modules:
  0.0 88.0 jit_solution(10476438162178710482)
XLA Ops:
  0.0 1.5 %shard_map.64 = (s32[4,12]{1,0:T(4,128)}, s32[64,128]{1,0:T(8,128)}) custom-call(s32[4,12]{1,0:T(4,128)} %bitcast.23, s32[4,12]{1,0:T(4,128)} %bitcast.24), custom_call_target="tpu_custom_call" | custom-call | tf_op jit(solution)/shard_map/pallas_call | solution.py:835
  1.5 13.0 %all-to-all-start = ((s32[64,1,128]{2,1,0:T(1,128)}), s32[64,1,128]{2,1,0:T(1,128)S(1)}, u32[]{:S(2)}, u32[]{:S(2)}) async-start(s32[64,1,128]{2,1,0:T(1,128)} %bitcast.22), calls=%async_computation | async-start | bytes 65536 | tf_op jit(solution)/shard_map/all_to_all | solution.py:849
  14.5 6.3 %shard_map.65 = (f32[1920,128]{1,0:T(8,128)}, f32[1920,128]{1,0:T(8,128)}, f32[384,128]{1,0:T(8,128)}, f32[960,128]{1,0:T(8,128)}, f32[240,128]{1,0:T(8,128)}, /*index=5*/f32[240,128]{1,0:T(8,128)}, s32[288,128]{1,0:T(8,128)}) custom-call(f32[5,12,4096]{2,1,0:T(8,128)} %bitcast.18, f32[5,12,4096]{2,1,0:T(8,128)} %bitcast.19, s32[1,12,4096]{2,1,0:T(8,128)} %bitcast.20, ...), custom_call_target="tpu_custom_call" | custom-call | flops 100000000 | bytes 30000000 | tf_op jit(solution)/shard_map/pallas_call | solution.py:763
  20.8 3.0 %all-to-all-done = s32[64,1,128]{2,1,0:T(1,128)S(1)} async-done(((s32[64,1,128]{2,1,0:T(1,128)}), s32[64,1,128]{2,1,0:T(1,128)S(1)}, u32[]{:S(2)}, u32[]{:S(2)}) %all-to-all-start) | async-done | bytes 32800 | tf_op jit(solution)/shard_map/all_to_all | solution.py:849
  23.9 0.0 copy-start.1
  23.9 0.6 copy-done.1
  24.5 3.6 %shard_map.66 = f32[2560,128]{1,0:T(8,128)} custom-call(s32[1]{0:T(128)} %bitcast.7.me_ref, s32[64,128]{1,0:T(8,128)} %bitcast.21, f32[960,128]{1,0:T(8,128)} %get-tuple-element.27.lat_ref), custom_call_target="tpu_custom_call" | custom-call | tf_op jit(solution)/shard_map/pallas_call | solution.py:782
  28.1 0.0 copy-start.5
  28.1 0.0 copy-start.4
  28.1 7.4 %all-to-all-start.1 = ((f32[64,40,128]{2,1,0:T(8,128)}), f32[64,40,128]{2,1,0:T(8,128)S(1)}, u32[]{:S(2)}, u32[]{:S(2)}) async-start(f32[64,40,128]{2,1,0:T(8,128)} %bitcast.16), calls=%async_computation.1 | async-start | bytes 2621440 | tf_op jit(solution)/shard_map/all_to_all | solution.py:849
  35.5 0.0 copy-done.5
  35.5 3.2 %collective-permute-start = (f32[240,128]{1,0:T(8,128)S(1)}, f32[240,128]{1,0:T(8,128)S(1)}, u32[]{:S(2)}, u32[]{:S(2)}) collective-permute-start(f32[240,128]{1,0:T(8,128)S(1)} %copy-done.5), channel_id=1, source_target_pairs={{0,1},{1,2},{2,3},{4,5},{5,6},{6,7},{8,9},{9,10},{10,11},{12,13},{... | collective-permute-start | bytes 368648 | tf_op jit(solution)/shard_map/ppermute | solution.py:862
  38.7 0.0 copy-done.4
  38.7 1.3 %collective-permute-start.1 = (f32[240,128]{1,0:T(8,128)S(1)}, f32[240,128]{1,0:T(8,128)S(1)}, u32[]{:S(2)}, u32[]{:S(2)}) collective-permute-start(f32[240,128]{1,0:T(8,128)S(1)} %copy-done.4), channel_id=1, source_target_pairs={{1,0},{2,1},{3,2},{5,4},{6,5},{7,6},{9,8},{10,9},{11,10},{13,12},{... | collective-permute-start | bytes 368648 | tf_op jit(solution)/shard_map/ppermute | solution.py:863
  40.0 0.9 %collective-permute-done.low_ref = f32[240,128]{1,0:T(8,128)S(1)} collective-permute-done((f32[240,128]{1,0:T(8,128)S(1)}, f32[240,128]{1,0:T(8,128)S(1)}, u32[]{:S(2)}, u32[]{:S(2)}) %collective-permute-start) | collective-permute-done | bytes 122912 | tf_op jit(solution)/shard_map/ppermute | solution.py:862
  40.9 0.0 copy-start.2
  40.9 3.8 %collective-permute-done.1.high_ref = f32[240,128]{1,0:T(8,128)S(1)} collective-permute-done((f32[240,128]{1,0:T(8,128)S(1)}, f32[240,128]{1,0:T(8,128)S(1)}, u32[]{:S(2)}, u32[]{:S(2)}) %collective-permute-start.1) | collective-permute-done | bytes 122912 | tf_op jit(solution)/shard_map/ppermute | solution.py:863
  44.7 0.0 copy-start.3
  44.7 0.0 copy-done.2
  44.7 0.6 copy-done.3
  45.3 29.4 %shard_map.67 = (f32[384,128]{1,0:T(8,128)}, f32[2880,128]{1,0:T(8,128)}, f32[1920,128]{1,0:T(8,128)}, f32[192,128]{1,0:T(8,128)}) custom-call(s32[1]{0:T(128)} %bitcast.13.edge_ref, s32[288,128]{1,0:T(8,128)} %get-tuple-element.22.index_ref, f32[1920,128]{1,0:T(8,128)} %get-tuple-element.28.prim_ref, f32[1920,128]{1,0:T(8,128)} %get-tuple-element.29.adj_ref, ...), custom_call_target="tpu_custom_call" | custom-call | tf_op jit(solution)/shard_map/pallas_call | solution.py:792
  74.7 0.0 all-to-all-done.1
  74.7 1.1 %copy-done = f32[64,40,128]{2,1,0:T(8,128)} copy-done((f32[64,40,128]{2,1,0:T(8,128)}, f32[64,40,128]{2,1,0:T(8,128)S(1)}, u32[]{:S(2)}) %copy-start) | copy-done | bytes 1310744
  75.8 12.2 %shard_map.68 = f32[12,4096]{1,0:T(8,128)} custom-call(s32[288,128]{1,0:T(8,128)} %get-tuple-element.22.index_ref, f32[2560,128]{1,0:T(8,128)} %bitcast.17, f32[2880,128]{1,0:T(8,128)} %get-tuple-element.33.px_ref, f32[1920,128]{1,0:T(8,128)} %get-tuple-element.34.pg_ref, f32[192,128]{1,0:T(8,128)} %get-tuple-element.35.ps_ref, ...), custom_call_target="tpu_custom_call" | custom-call | tf_op jit(solution)/shard_map/pallas_call | solution.py:803
  (1 shorter events, 0.0 us)
Async XLA Ops:
  1.5 22.4 %all-to-all-start = ((s32[64,1,128]{2,1,0:T(1,128)}), s32[64,1,128]{2,1,0:T(1,128)S(1)}, u32[]{:S(2)}, u32[]{:S(2)}) async-start(s32[64,1,128]{2,1,0:T(1,128)} %bitcast.22), calls=%async_computation | async-start | bytes 65536 | tf_op jit(solution)/shard_map/all_to_all | solution.py:849
  23.9 0.6 copy-start.1
  28.1 7.4 %copy-start.5 = (f32[240,128]{1,0:T(8,128)S(1)}, f32[240,128]{1,0:T(8,128)}, u32[]{:S(2)}) copy-start(f32[240,128]{1,0:T(8,128)} %get-tuple-element.31) | copy-start | bytes 368644
  28.1 10.6 %copy-start.4 = (f32[240,128]{1,0:T(8,128)S(1)}, f32[240,128]{1,0:T(8,128)}, u32[]{:S(2)}) copy-start(f32[240,128]{1,0:T(8,128)} %get-tuple-element.32) | copy-start | bytes 368644
  28.1 46.6 %all-to-all-start.1 = ((f32[64,40,128]{2,1,0:T(8,128)}), f32[64,40,128]{2,1,0:T(8,128)S(1)}, u32[]{:S(2)}, u32[]{:S(2)}) async-start(f32[64,40,128]{2,1,0:T(8,128)} %bitcast.16), calls=%async_computation.1 | async-start | bytes 2621440 | tf_op jit(solution)/shard_map/all_to_all | solution.py:849
  35.5 5.4 %collective-permute-start = (f32[240,128]{1,0:T(8,128)S(1)}, f32[240,128]{1,0:T(8,128)S(1)}, u32[]{:S(2)}, u32[]{:S(2)}) collective-permute-start(f32[240,128]{1,0:T(8,128)S(1)} %copy-done.5), channel_id=1, source_target_pairs={{0,1},{1,2},{2,3},{4,5},{5,6},{6,7},{8,9},{9,10},{10,11},{12,13},{... | collective-permute-start | bytes 368648 | tf_op jit(solution)/shard_map/ppermute | solution.py:862
  38.7 6.0 %collective-permute-start.1 = (f32[240,128]{1,0:T(8,128)S(1)}, f32[240,128]{1,0:T(8,128)S(1)}, u32[]{:S(2)}, u32[]{:S(2)}) collective-permute-start(f32[240,128]{1,0:T(8,128)S(1)} %copy-done.4), channel_id=1, source_target_pairs={{1,0},{2,1},{3,2},{5,4},{6,5},{7,6},{9,8},{10,9},{11,10},{13,12},{... | collective-permute-start | bytes 368648 | tf_op jit(solution)/shard_map/ppermute | solution.py:863
  40.9 3.8 %copy-start.2 = (f32[240,128]{1,0:T(8,128)}, f32[240,128]{1,0:T(8,128)S(1)}, u32[]{:S(2)}) copy-start(f32[240,128]{1,0:T(8,128)S(1)} %collective-permute-done.low_ref) | copy-start | bytes 368644
  44.7 0.6 copy-start.3
  74.7 1.1 %copy-start = (f32[64,40,128]{2,1,0:T(8,128)}, f32[64,40,128]{2,1,0:T(8,128)S(1)}, u32[]{:S(2)}) copy-start(f32[64,40,128]{2,1,0:T(8,128)S(1)} %all-to-all-done.1) | copy-start | bytes 3932164

commit v7 on v6

--- a/solution.py
+++ b/solution.py
@@ -130,7 +130,7 @@
 
 def prep_kernel(
     flow_ref, adj_ref, flag_ref, own_ref, vertical_ref,
-    prim_ref, adjl_ref, solid_ref, lat_ref, low_ref, high_ref, index_ref,
+    prim_ref, adjl_ref, solid_ref, lat_ref, low_ref, high_ref, index_ref, px_ref, ps_ref,
 ):
     def relaid(ref, c, out_ref):
         for t in range(2 * EDGE):
@@ -169,7 +169,7 @@
                 out = (c + first) * FACES + g * 8
                 lat_ref[rows8(out), :] = load(0)
                 lat_ref[rows8(out + PL), :] = load(EDGE - 1)
-                near, far = compact_depths(load, 1)
+                near, far = packed(load, px_ref, 3, c + first, 10, g)
                 lat_ref[rows8(out + 2 * PL), :] = near[0]
                 lat_ref[rows8(out + 3 * PL), :] = far[0]
                 low, high = compact_k(load)
@@ -181,6 +181,8 @@
 
     layers(prim_ref, 0)
     layers(adjl_ref, 5)
+    for g in range(3):
+        packed(lambda i: solid_ref[pl.ds(i * PL + g * 8, 8), :], ps_ref, 2, 0, 1, g)
 
 
 def reply_kernel(me_ref, asked_ref, lat_ref, out_ref):
@@ -246,6 +248,17 @@
     return [y[:, n * LANES : (n + 1) * LANES] for n in range(len(parts))]
 
 
+def packed(load, out_ref, depth, first, step, g):
+    planes = [[load(n) for n in range(depth)], [load(EDGE - 1 - n) for n in range(depth)]]
+    across = compact_depths(load, depth)
+    for n, sides in enumerate((planes, across)):
+        for side in range(2):
+            for at in range(depth):
+                row = (((n * 2 + side) * depth + at) * step + first) * PL + g * 8
+                out_ref[rows8(row), :] = sides[side][at]
+    return across
+
+
 def minmod(a, c):
     return jnp.maximum(jnp.minimum(a, jnp.maximum(c, 0.0)), jnp.minimum(c, 0.0))
 
@@ -480,7 +493,7 @@
 
 def inner_kernel(
     edge_ref, index_ref, prim_ref, adj_ref, solid_ref, low_ref, high_ref,
-    acc_ref, px_ref, pg_ref, ps_ref,
+    acc_ref, pg_ref,
     v_ref, gk_ref, pv_ref, aw_ref,
 ):
     for side in range(2):
@@ -503,30 +516,17 @@
 
     lax.fori_loop(0, 10, spread, 0)
 
-    def packed(load, out_ref, depth, first, step, g):
-        planes = [[load(n) for n in range(depth)], [load(EDGE - 1 - n) for n in range(depth)]]
-        for n, sides in enumerate((planes, compact_depths(load, depth))):
-            for side in range(2):
-                for at in range(depth):
-                    row = (((n * 2 + side) * depth + at) * step + first) * PL + g * 8
-                    out_ref[rows8(row), :] = sides[side][at]
-
     def pack(c, _):
         for g in range(3):
 
             def load_of(ref, first):
                 return lambda i: ref[rows8((c + first) * ROWS + i * PL + g * 8), :]
 
-            packed(load_of(prim_ref, 0), px_ref, 3, c, 10, g)
-            packed(load_of(adj_ref, 0), px_ref, 3, c + 5, 10, g)
             packed(load_of(gk_ref, 0), pg_ref, 2, c, 10, g)
             packed(load_of(gk_ref, 5), pg_ref, 2, c + 5, 10, g)
         return 0
 
     lax.fori_loop(0, 5, pack, 0)
-    for g in range(3):
-        packed(lambda i: solid_ref[pl.ds(i * PL + g * 8, 8), :], ps_ref, 2, 0, 1, g)
-
     m = masks()
     inside = ~(m["j_first"] | m["j_last"])
     gone_j = m["j_first"] | m["j_last"] | m["j_penult"]
@@ -708,7 +708,7 @@
             pm_ref[rows8((place * 2 + 1) * PL + g8), :] = next_total
             return 0
 
-        lax.fori_loop(0, 6, one, 0)
+        lax.fori_loop(0, 6, one, 0, unroll=2)
 
     boundary(0)
     boundary(1)
@@ -770,9 +770,11 @@
             shape(10 * PL, LANES),
             shape(10 * PL, LANES),
             jax.ShapeDtypeStruct((288, LANES), jnp.int32),
+            shape(120 * PL, LANES),
+            shape(8 * PL, LANES),
         ],
         in_specs=[VMEM] * 5,
-        out_specs=[VMEM] * 7,
+        out_specs=[VMEM] * 9,
         cost_estimate=pl.CostEstimate(flops=10**8, bytes_accessed=3 * 10**7, transcendentals=0),
         compiler_params=PARAMS,
     )(flow.transpose(1, 0, 2), adjoint.transpose(1, 0, 2), cut_flag[None], own, vertical)
@@ -791,9 +793,9 @@
 def inner(edge, index, prim, adj, solid, low, high):
     return pl.pallas_call(
         inner_kernel,
-        out_shape=[shape(n, LANES) for n in (ROWS, 120 * PL, 80 * PL, 8 * PL)],
+        out_shape=[shape(ROWS, LANES), shape(80 * PL, LANES)],
         in_specs=[SMEM] + [VMEM] * 6,
-        out_specs=[VMEM] * 4,
+        out_specs=[VMEM] * 2,
         scratch_shapes=scratch(20 * PL, 10 * ROWS, 31 * 8, 15 * 8),
         compiler_params=PARAMS,
     )(edge, index, prim, adj, solid, low, high)
@@ -853,7 +855,7 @@
 def local(flow, adjoint, cut_flag, lateral_owner, lateral_link, vertical_link):
     own, questions = ask(lateral_owner, lateral_link)
     asked = exchange(questions, "blk")
-    prim, adj, solid, layers, low_face, high_face, index = prep(
+    prim, adj, solid, layers, low_face, high_face, index, planes, walls = prep(
         flow, adjoint, cut_flag, own, vertical_link.T
     )
     asked, low_face, high_face = lax.optimization_barrier((asked, low_face, high_face))
@@ -865,7 +867,7 @@
     replies = reply(me, asked, layers)
     got = exchange(replies, "blk")
     edge = region.astype(jnp.int32).reshape(1)
-    acc, planes, ghosts, walls = inner(edge, index, prim, adj, solid, low, high)
+    acc, ghosts = inner(edge, index, prim, adj, solid, low, high)
     return rim(index, got, planes, ghosts, walls, solid, acc)
 
 

time: 88.6 us -> 85.9 us (0.970)
  Pallas kernels: 53 us -> 50.2 us
    pallas_call x1, Pallas kernels: 29.4 us -> 26.5 us  [inner(): pl.pallas_call(inner_kernel, out_shape=[shape(ROWS, LANES), shape(80 * PL...]
  transfers between devices with their start and end apart: 4 -> 4, of which waited for: 3 -> 3; matrix products, arithmetic and copies ran while one was open for 0% -> 0% of each run, Pallas kernels for 41% -> 39%
where the time goes in v7:
time: 85.9 us; the launch traced here: 85.2 us
  Pallas kernels  50.2 us (58%)
  starting transfers between devices  25.4 us (30%)
  waiting for transfers between devices  7.25 us (8%)
  local copies, waits for them, and re-layouts  2.33 us (3%)
    pallas_call x1, Pallas kernels, inner(): pl.pallas_call(inner_kernel, out_shape=[shape(ROWS, LANES), shape(80 * PL...  26.5 us
    all_to_all x2, starting transfers between devices, exchange(): out = lax.all_to_all(chunks, axis, split_axis=0, concat_axis=0, tiled=True)  20.9 us
    pallas_call x1, Pallas kernels, rim(): pl.pallas_call(rim_kernel, out_shape=shape(NB, EDGE * EDGE * EDGE), in_sp...  11.8 us
    pallas_call x1, Pallas kernels, prep(): pl.pallas_call(prep_kernel, out_shape=[shape(5 * ROWS, LANES), shape(5 *...  6.82 us
    ppermute x1, waiting for transfers between devices, local(): lax.ppermute(low_face, 'grp', [(r + 1, r) for r in range(regions - 1)])  3.8 us
    pallas_call x1, Pallas kernels, reply(): pl.pallas_call(reply_kernel, out_shape=shape(40 * PEERS, LANES), in_specs...  3.55 us
    ppermute x1, starting transfers between devices, local(): lax.ppermute(high_face, 'grp', [(r, r + 1) for r in range(regions - 1)])  3.21 us
    all_to_all x2, waiting for transfers between devices, exchange(): out = lax.all_to_all(chunks, axis, split_axis=0, concat_axis=0, tiled=True)  2.55 us
  transfers between devices with their start and end apart: 4, of which 3 were waited for; matrix products, arithmetic and copies ran while one was open for 0% of the time, Pallas kernels for 39%

profile of v7, /device:TPU:1, one launch (start us, length us, event | category | flops | bytes accessed | tf_op | source)
XLA Modules:
  0.0 85.2 jit_solution(3696212904423824787)
XLA Ops:
  0.0 1.5 %shard_map.64 = (s32[4,12]{1,0:T(4,128)}, s32[64,128]{1,0:T(8,128)}) custom-call(s32[4,12]{1,0:T(4,128)} %bitcast.23, s32[4,12]{1,0:T(4,128)} %bitcast.24), custom_call_target="tpu_custom_call" | custom-call | tf_op jit(solution)/shard_map/pallas_call | solution.py:837
  1.5 13.0 %all-to-all-start = ((s32[64,1,128]{2,1,0:T(1,128)}), s32[64,1,128]{2,1,0:T(1,128)S(1)}, u32[]{:S(2)}, u32[]{:S(2)}) async-start(s32[64,1,128]{2,1,0:T(1,128)} %bitcast.22), calls=%async_computation | async-start | bytes 65536 | tf_op jit(solution)/shard_map/all_to_all | solution.py:851
  14.5 6.8 %shard_map.65 = (f32[1920,128]{1,0:T(8,128)}, f32[1920,128]{1,0:T(8,128)}, f32[384,128]{1,0:T(8,128)}, f32[960,128]{1,0:T(8,128)}, f32[240,128]{1,0:T(8,128)}, /...) custom-call(f32[5,12,4096]{2,1,0:T(8,128)} %bitcast.18, ...), custom_call_target="tpu_custom_call" | custom-call | flops 100000000 | bytes 30000000 | tf_op jit(solution)/shard_map/pallas_call | solution.py:763
  21.3 2.5 %all-to-all-done = s32[64,1,128]{2,1,0:T(1,128)S(1)} async-done(((s32[64,1,128]{2,1,0:T(1,128)}), s32[64,1,128]{2,1,0:T(1,128)S(1)}, u32[]{:S(2)}, u32[]{:S(2)}) %all-to-all-start) | async-done | bytes 32800 | tf_op jit(solution)/shard_map/all_to_all | solution.py:851
  23.9 0.0 copy-start.1
  23.9 0.6 copy-done.1
  24.5 3.6 %shard_map.66 = f32[2560,128]{1,0:T(8,128)} custom-call(s32[1]{0:T(128)} %bitcast.7.me_ref, s32[64,128]{1,0:T(8,128)} %bitcast.21, f32[960,128]{1,0:T(8,128)} %get-tuple-element.27.lat_ref), custom_call_target="tpu_custom_call" | custom-call | tf_op jit(solution)/shard_map/pallas_call | solution.py:784
  28.1 0.0 copy-start.5
  28.1 0.0 copy-start.4
  28.1 7.9 %all-to-all-start.1 = ((f32[64,40,128]{2,1,0:T(8,128)}), f32[64,40,128]{2,1,0:T(8,128)S(1)}, u32[]{:S(2)}, u32[]{:S(2)}) async-start(f32[64,40,128]{2,1,0:T(8,128)} %bitcast.16), calls=%async_computation.1 | async-start | bytes 2621440 | tf_op jit(solution)/shard_map/all_to_all | solution.py:851
  35.9 0.0 copy-done.5
  36.0 3.2 %collective-permute-start = (f32[240,128]{1,0:T(8,128)S(1)}, f32[240,128]{1,0:T(8,128)S(1)}, u32[]{:S(2)}, u32[]{:S(2)}) collective-permute-start(f32[240,128]{1,0:T(8,128)S(1)} %copy-done.5), channel_id=1, source_target_pairs={{0,1},{1,2},{2,3},{4,5},{5,6},{6,7},{8,9},{9,10},{10,11},{12,13},{... | collective-permute-start | bytes 368648 | tf_op jit(solution)/shard_map/ppermute | solution.py:864
  39.2 0.0 copy-done.4
  39.2 1.3 %collective-permute-start.1 = (f32[240,128]{1,0:T(8,128)S(1)}, f32[240,128]{1,0:T(8,128)S(1)}, u32[]{:S(2)}, u32[]{:S(2)}) collective-permute-start(f32[240,128]{1,0:T(8,128)S(1)} %copy-done.4), channel_id=1, source_target_pairs={{1,0},{2,1},{3,2},{5,4},{6,5},{7,6},{9,8},{10,9},{11,10},{13,12},{... | collective-permute-start | bytes 368648 | tf_op jit(solution)/shard_map/ppermute | solution.py:865
  40.5 0.9 %collective-permute-done.low_ref = f32[240,128]{1,0:T(8,128)S(1)} collective-permute-done((f32[240,128]{1,0:T(8,128)S(1)}, f32[240,128]{1,0:T(8,128)S(1)}, u32[]{:S(2)}, u32[]{:S(2)}) %collective-permute-start) | collective-permute-done | bytes 122912 | tf_op jit(solution)/shard_map/ppermute | solution.py:864
  41.4 0.0 copy-start.2
  41.4 3.8 %collective-permute-done.1.high_ref = f32[240,128]{1,0:T(8,128)S(1)} collective-permute-done((f32[240,128]{1,0:T(8,128)S(1)}, f32[240,128]{1,0:T(8,128)S(1)}, u32[]{:S(2)}, u32[]{:S(2)}) %collective-permute-start.1) | collective-permute-done | bytes 122912 | tf_op jit(solution)/shard_map/ppermute | solution.py:865
  45.2 0.0 copy-start.3
  45.2 0.0 copy-done.2
  45.2 0.6 copy-done.3
  45.8 26.5 %shard_map.67 = (f32[384,128]{1,0:T(8,128)}, f32[1920,128]{1,0:T(8,128)}) custom-call(s32[1]{0:T(128)} %bitcast.13.edge_ref, s32[288,128]{1,0:T(8,128)} %get-tuple-element.22.index_ref, f32[1920,128]{1,0:T(8,128)} %get-tuple-element.29.prim_ref, f32[1920,128]{1,0:T(8,128)} %get-tuple-element.30.adj_ref, f32[384,128]{1,0:T(8,128)} %get-tuple-element.31.solid_ref, ...), custom_call_target="tpu_custom_call" | custom-call | tf_op jit(solution)/shard_map/pallas_call | solution.py:794
  72.4 0.0 all-to-all-done.1
  72.4 1.1 %copy-done = f32[64,40,128]{2,1,0:T(8,128)} copy-done((f32[64,40,128]{2,1,0:T(8,128)}, f32[64,40,128]{2,1,0:T(8,128)S(1)}, u32[]{:S(2)}) %copy-start) | copy-done | bytes 1310744
  73.4 11.8 %shard_map.68 = f32[12,4096]{1,0:T(8,128)} custom-call(s32[288,128]{1,0:T(8,128)} %get-tuple-element.22.index_ref, f32[2560,128]{1,0:T(8,128)} %bitcast.17, f32[2880,128]{1,0:T(8,128)} %get-tuple-element.28.px_ref, f32[1920,128]{1,0:T(8,128)} %get-tuple-element.34.pg_ref, f32[192,128]{1,0:T(8,128)} %get-tuple-element.35.ps_ref, ...), custom_call_target="tpu_custom_call" | custom-call | tf_op jit(solution)/shard_map/pallas_call | solution.py:805
  (1 shorter events, 0.0 us)
Async XLA Ops:
  1.5 22.4 %all-to-all-start = ((s32[64,1,128]{2,1,0:T(1,128)}), s32[64,1,128]{2,1,0:T(1,128)S(1)}, u32[]{:S(2)}, u32[]{:S(2)}) async-start(s32[64,1,128]{2,1,0:T(1,128)} %bitcast.22), calls=%async_computation | async-start | bytes 65536 | tf_op jit(solution)/shard_map/all_to_all | solution.py:851
  23.9 0.6 copy-start.1
  28.1 7.9 %copy-start.5 = (f32[240,128]{1,0:T(8,128)S(1)}, f32[240,128]{1,0:T(8,128)}, u32[]{:S(2)}) copy-start(f32[240,128]{1,0:T(8,128)} %get-tuple-element.32) | copy-start | bytes 368644
  28.1 11.1 %copy-start.4 = (f32[240,128]{1,0:T(8,128)S(1)}, f32[240,128]{1,0:T(8,128)}, u32[]{:S(2)}) copy-start(f32[240,128]{1,0:T(8,128)} %get-tuple-element.33) | copy-start | bytes 368644
  28.1 44.3 %all-to-all-start.1 = ((f32[64,40,128]{2,1,0:T(8,128)}), f32[64,40,128]{2,1,0:T(8,128)S(1)}, u32[]{:S(2)}, u32[]{:S(2)}) async-start(f32[64,40,128]{2,1,0:T(8,128)} %bitcast.16), calls=%async_computation.1 | async-start | bytes 2621440 | tf_op jit(solution)/shard_map/all_to_all | solution.py:851
  36.0 5.4 %collective-permute-start = (f32[240,128]{1,0:T(8,128)S(1)}, f32[240,128]{1,0:T(8,128)S(1)}, u32[]{:S(2)}, u32[]{:S(2)}) collective-permute-start(f32[240,128]{1,0:T(8,128)S(1)} %copy-done.5), channel_id=1, source_target_pairs={{0,1},{1,2},{2,3},{4,5},{5,6},{6,7},{8,9},{9,10},{10,11},{12,13},{... | collective-permute-start | bytes 368648 | tf_op jit(solution)/shard_map/ppermute | solution.py:864
  39.2 6.0 %collective-permute-start.1 = (f32[240,128]{1,0:T(8,128)S(1)}, f32[240,128]{1,0:T(8,128)S(1)}, u32[]{:S(2)}, u32[]{:S(2)}) collective-permute-start(f32[240,128]{1,0:T(8,128)S(1)} %copy-done.4), channel_id=1, source_target_pairs={{1,0},{2,1},{3,2},{5,4},{6,5},{7,6},{9,8},{10,9},{11,10},{13,12},{... | collective-permute-start | bytes 368648 | tf_op jit(solution)/shard_map/ppermute | solution.py:865
  41.4 3.8 %copy-start.2 = (f32[240,128]{1,0:T(8,128)}, f32[240,128]{1,0:T(8,128)S(1)}, u32[]{:S(2)}) copy-start(f32[240,128]{1,0:T(8,128)S(1)} %collective-permute-done.low_ref) | copy-start | bytes 368644
  45.2 0.6 copy-start.3
  72.4 1.1 %copy-start = (f32[64,40,128]{2,1,0:T(8,128)}, f32[64,40,128]{2,1,0:T(8,128)S(1)}, u32[]{:S(2)}) copy-start(f32[64,40,128]{2,1,0:T(8,128)S(1)} %all-to-all-done.1) | copy-start | bytes 3932164

commit v8 on v7

--- a/solution.py
+++ b/solution.py
@@ -516,17 +516,28 @@
 
     lax.fori_loop(0, 10, spread, 0)
 
+    even, early = even_row(), lane() % EDGE < 8
+    ahead = jnp.where(even, 0, 8) + lane() // EDGE
+    picks = [[spot * EDGE + ahead for spot in spots] for spots in ((0, 1), (7, 6))]
+
     def pack(c, _):
         for g in range(3):
-
-            def load_of(ref, first):
-                return lambda i: ref[rows8((c + first) * ROWS + i * PL + g * 8), :]
-
-            packed(load_of(gk_ref, 0), pg_ref, 2, c, 10, g)
-            packed(load_of(gk_ref, 5), pg_ref, 2, c + 5, 10, g)
+            ends_k = [v_ref[rows8((side * 10 + c) * PL + g * 8), :] for side in range(2)]
+            near = [jnp.where(even, y, rolled(y, 1, 0)) for y in ends_k]
+            far = [jnp.where(even, rolled(y, -1, 0), y) for y in ends_k]
+            for side, pair in enumerate((near, far)):
+                for at in range(2):
+                    low, high = (
+                        jnp.take_along_axis(y, picks[side][at], axis=1, mode="promise_in_bounds")
+                        for y in pair
+                    )
+                    row = ((side * 2 + at) * 10 + c) * PL + g * 8
+                    plane = at if side == 0 else EDGE - 1 - at
+                    pg_ref[rows8(row), :] = gk_ref[rows8(c * ROWS + plane * PL + g * 8), :]
+                    pg_ref[rows8(row + 40 * PL), :] = jnp.where(early, low, high)
         return 0
 
-    lax.fori_loop(0, 5, pack, 0)
+    lax.fori_loop(0, 10, pack, 0)
     m = masks()
     inside = ~(m["j_first"] | m["j_last"])
     gone_j = m["j_first"] | m["j_last"] | m["j_penult"]

time: 85.9 us -> 85.8 us (level)
  no operation moved by 1% of the time
where the time goes in v8:
time: 85.8 us; the launch traced here: 85.2 us
  Pallas kernels  50.1 us (58%)
  starting transfers between devices  25.4 us (30%)
  waiting for transfers between devices  7.25 us (8%)
  local copies, waits for them, and re-layouts  2.33 us (3%)
    pallas_call x1, Pallas kernels, inner(): pl.pallas_call(inner_kernel, out_shape=[shape(ROWS, LANES), shape(80 * PL...  26.5 us
    all_to_all x2, starting transfers between devices, exchange(): out = lax.all_to_all(chunks, axis, split_axis=0, concat_axis=0, tiled=True)  20.9 us
    pallas_call x1, Pallas kernels, rim(): pl.pallas_call(rim_kernel, out_shape=shape(NB, EDGE * EDGE * EDGE), in_sp...  11.8 us
    pallas_call x1, Pallas kernels, prep(): pl.pallas_call(prep_kernel, out_shape=[shape(5 * ROWS, LANES), shape(5 *...  6.82 us
    ppermute x1, waiting for transfers between devices, local(): lax.ppermute(low_face, 'grp', [(r + 1, r) for r in range(regions - 1)])  3.8 us
    pallas_call x1, Pallas kernels, reply(): pl.pallas_call(reply_kernel, out_shape=shape(40 * PEERS, LANES), in_specs...  3.55 us
    ppermute x1, starting transfers between devices, local(): lax.ppermute(high_face, 'grp', [(r, r + 1) for r in range(regions - 1)])  3.21 us
    all_to_all x2, waiting for transfers between devices, exchange(): out = lax.all_to_all(chunks, axis, split_axis=0, concat_axis=0, tiled=True)  2.55 us
  transfers between devices with their start and end apart: 4, of which 3 were waited for; matrix products, arithmetic and copies ran while one was open for 0% of the time, Pallas kernels for 39%

profile of v8, /device:TPU:1, one launch (start us, length us, event | category | flops | bytes accessed | tf_op | source)
XLA Modules:
  0.0 85.2 jit_solution(2012241288043688511)
XLA Ops:
  0.0 1.5 %shard_map.64 = (s32[4,12]{1,0:T(4,128)}, s32[64,128]{1,0:T(8,128)}) custom-call(s32[4,12]{1,0:T(4,128)} %bitcast.23, s32[4,12]{1,0:T(4,128)} %bitcast.24), custom_call_target="tpu_custom_call" | custom-call | tf_op jit(solution)/shard_map/pallas_call | solution.py:848
  1.5 13.0 %all-to-all-start = ((s32[64,1,128]{2,1,0:T(1,128)}), s32[64,1,128]{2,1,0:T(1,128)S(1)}, u32[]{:S(2)}, u32[]{:S(2)}) async-start(s32[64,1,128]{2,1,0:T(1,128)} %bitcast.22), calls=%async_computation | async-start | bytes 65536 | tf_op jit(solution)/shard_map/all_to_all | solution.py:862
  14.5 6.8 %shard_map.65 = (f32[1920,128]{1,0:T(8,128)}, f32[1920,128]{1,0:T(8,128)}, f32[384,128]{1,0:T(8,128)}, f32[960,128]{1,0:T(8,128)}, f32[240,128]{1,0:T(8,128)}, /...) custom-call(f32[5,12,4096]{2,1,0:T(8,128)} %bitcast.18, ...), custom_call_target="tpu_custom_call" | custom-call | flops 100000000 | bytes 30000000 | tf_op jit(solution)/shard_map/pallas_call | solution.py:774
  21.3 2.5 %all-to-all-done = s32[64,1,128]{2,1,0:T(1,128)S(1)} async-done(((s32[64,1,128]{2,1,0:T(1,128)}), s32[64,1,128]{2,1,0:T(1,128)S(1)}, u32[]{:S(2)}, u32[]{:S(2)}) %all-to-all-start) | async-done | bytes 32800 | tf_op jit(solution)/shard_map/all_to_all | solution.py:862
  23.9 0.0 copy-start.1
  23.9 0.6 copy-done.1
  24.5 3.6 %shard_map.66 = f32[2560,128]{1,0:T(8,128)} custom-call(s32[1]{0:T(128)} %bitcast.7.me_ref, s32[64,128]{1,0:T(8,128)} %bitcast.21, f32[960,128]{1,0:T(8,128)} %get-tuple-element.27.lat_ref), custom_call_target="tpu_custom_call" | custom-call | tf_op jit(solution)/shard_map/pallas_call | solution.py:795
  28.1 0.0 copy-start.5
  28.1 0.0 copy-start.4
  28.1 7.9 %all-to-all-start.1 = ((f32[64,40,128]{2,1,0:T(8,128)}), f32[64,40,128]{2,1,0:T(8,128)S(1)}, u32[]{:S(2)}, u32[]{:S(2)}) async-start(f32[64,40,128]{2,1,0:T(8,128)} %bitcast.16), calls=%async_computation.1 | async-start | bytes 2621440 | tf_op jit(solution)/shard_map/all_to_all | solution.py:862
  35.9 0.0 copy-done.5
  36.0 3.2 %collective-permute-start = (f32[240,128]{1,0:T(8,128)S(1)}, f32[240,128]{1,0:T(8,128)S(1)}, u32[]{:S(2)}, u32[]{:S(2)}) collective-permute-start(f32[240,128]{1,0:T(8,128)S(1)} %copy-done.5), channel_id=1, source_target_pairs={{0,1},{1,2},{2,3},{4,5},{5,6},{6,7},{8,9},{9,10},{10,11},{12,13},{... | collective-permute-start | bytes 368648 | tf_op jit(solution)/shard_map/ppermute | solution.py:875
  39.2 0.0 copy-done.4
  39.2 1.3 %collective-permute-start.1 = (f32[240,128]{1,0:T(8,128)S(1)}, f32[240,128]{1,0:T(8,128)S(1)}, u32[]{:S(2)}, u32[]{:S(2)}) collective-permute-start(f32[240,128]{1,0:T(8,128)S(1)} %copy-done.4), channel_id=1, source_target_pairs={{1,0},{2,1},{3,2},{5,4},{6,5},{7,6},{9,8},{10,9},{11,10},{13,12},{... | collective-permute-start | bytes 368648 | tf_op jit(solution)/shard_map/ppermute | solution.py:876
  40.5 0.9 %collective-permute-done.low_ref = f32[240,128]{1,0:T(8,128)S(1)} collective-permute-done((f32[240,128]{1,0:T(8,128)S(1)}, f32[240,128]{1,0:T(8,128)S(1)}, u32[]{:S(2)}, u32[]{:S(2)}) %collective-permute-start) | collective-permute-done | bytes 122912 | tf_op jit(solution)/shard_map/ppermute | solution.py:875
  41.4 0.0 copy-start.2
  41.4 3.8 %collective-permute-done.1.high_ref = f32[240,128]{1,0:T(8,128)S(1)} collective-permute-done((f32[240,128]{1,0:T(8,128)S(1)}, f32[240,128]{1,0:T(8,128)S(1)}, u32[]{:S(2)}, u32[]{:S(2)}) %collective-permute-start.1) | collective-permute-done | bytes 122912 | tf_op jit(solution)/shard_map/ppermute | solution.py:876
  45.2 0.0 copy-start.3
  45.2 0.0 copy-done.2
  45.2 0.6 copy-done.3
  45.8 26.5 %shard_map.67 = (f32[384,128]{1,0:T(8,128)}, f32[1920,128]{1,0:T(8,128)}) custom-call(s32[1]{0:T(128)} %bitcast.13.edge_ref, s32[288,128]{1,0:T(8,128)} %get-tuple-element.22.index_ref, f32[1920,128]{1,0:T(8,128)} %get-tuple-element.29.prim_ref, f32[1920,128]{1,0:T(8,128)} %get-tuple-element.30.adj_ref, f32[384,128]{1,0:T(8,128)} %get-tuple-element.31.solid_ref, ...), custom_call_target="tpu_custom_call" | custom-call | tf_op jit(solution)/shard_map/pallas_call | solution.py:805
  72.3 0.0 all-to-all-done.1
  72.3 1.1 %copy-done = f32[64,40,128]{2,1,0:T(8,128)} copy-done((f32[64,40,128]{2,1,0:T(8,128)}, f32[64,40,128]{2,1,0:T(8,128)S(1)}, u32[]{:S(2)}) %copy-start) | copy-done | bytes 1310744
  73.4 11.8 %shard_map.68 = f32[12,4096]{1,0:T(8,128)} custom-call(s32[288,128]{1,0:T(8,128)} %get-tuple-element.22.index_ref, f32[2560,128]{1,0:T(8,128)} %bitcast.17, f32[2880,128]{1,0:T(8,128)} %get-tuple-element.28.px_ref, f32[1920,128]{1,0:T(8,128)} %get-tuple-element.34.pg_ref, f32[192,128]{1,0:T(8,128)} %get-tuple-element.35.ps_ref, ...), custom_call_target="tpu_custom_call" | custom-call | tf_op jit(solution)/shard_map/pallas_call | solution.py:816
  (1 shorter events, 0.0 us)
Async XLA Ops:
  1.5 22.4 %all-to-all-start = ((s32[64,1,128]{2,1,0:T(1,128)}), s32[64,1,128]{2,1,0:T(1,128)S(1)}, u32[]{:S(2)}, u32[]{:S(2)}) async-start(s32[64,1,128]{2,1,0:T(1,128)} %bitcast.22), calls=%async_computation | async-start | bytes 65536 | tf_op jit(solution)/shard_map/all_to_all | solution.py:862
  23.9 0.6 copy-start.1
  28.1 7.9 %copy-start.5 = (f32[240,128]{1,0:T(8,128)S(1)}, f32[240,128]{1,0:T(8,128)}, u32[]{:S(2)}) copy-start(f32[240,128]{1,0:T(8,128)} %get-tuple-element.32) | copy-start | bytes 368644
  28.1 11.1 %copy-start.4 = (f32[240,128]{1,0:T(8,128)S(1)}, f32[240,128]{1,0:T(8,128)}, u32[]{:S(2)}) copy-start(f32[240,128]{1,0:T(8,128)} %get-tuple-element.33) | copy-start | bytes 368644
  28.1 44.3 %all-to-all-start.1 = ((f32[64,40,128]{2,1,0:T(8,128)}), f32[64,40,128]{2,1,0:T(8,128)S(1)}, u32[]{:S(2)}, u32[]{:S(2)}) async-start(f32[64,40,128]{2,1,0:T(8,128)} %bitcast.16), calls=%async_computation.1 | async-start | bytes 2621440 | tf_op jit(solution)/shard_map/all_to_all | solution.py:862
  36.0 5.4 %collective-permute-start = (f32[240,128]{1,0:T(8,128)S(1)}, f32[240,128]{1,0:T(8,128)S(1)}, u32[]{:S(2)}, u32[]{:S(2)}) collective-permute-start(f32[240,128]{1,0:T(8,128)S(1)} %copy-done.5), channel_id=1, source_target_pairs={{0,1},{1,2},{2,3},{4,5},{5,6},{6,7},{8,9},{9,10},{10,11},{12,13},{... | collective-permute-start | bytes 368648 | tf_op jit(solution)/shard_map/ppermute | solution.py:875
  39.2 6.0 %collective-permute-start.1 = (f32[240,128]{1,0:T(8,128)S(1)}, f32[240,128]{1,0:T(8,128)S(1)}, u32[]{:S(2)}, u32[]{:S(2)}) collective-permute-start(f32[240,128]{1,0:T(8,128)S(1)} %copy-done.4), channel_id=1, source_target_pairs={{1,0},{2,1},{3,2},{5,4},{6,5},{7,6},{9,8},{10,9},{11,10},{13,12},{... | collective-permute-start | bytes 368648 | tf_op jit(solution)/shard_map/ppermute | solution.py:876
  41.4 3.8 %copy-start.2 = (f32[240,128]{1,0:T(8,128)}, f32[240,128]{1,0:T(8,128)S(1)}, u32[]{:S(2)}) copy-start(f32[240,128]{1,0:T(8,128)S(1)} %collective-permute-done.low_ref) | copy-start | bytes 368644
  45.2 0.6 copy-start.3
  72.3 1.1 %copy-start = (f32[64,40,128]{2,1,0:T(8,128)}, f32[64,40,128]{2,1,0:T(8,128)S(1)}, u32[]{:S(2)}) copy-start(f32[64,40,128]{2,1,0:T(8,128)S(1)} %all-to-all-done.1) | copy-start | bytes 3932164
